TPU v7x, 128 devices: a whole 4x4x4 slice. The times are simulated.
128 devices in a mesh: tile: 16 (over x, z), dom: 8 (over y, core).
Axes of the slice: x: 4, y: 4, z: 4, core: 2. Of those that a mesh axis runs over, the one named last changes fastest.
Arguments:
- moisture: float32 [64, 128, 8192], P(None, 'dom', 'tile'), may hold values from -6 to 6
- ancestors: int32 [128], replicated, may hold values from 0 to 127, as said below
- adjacency: int32 [64, 3], replicated, may hold values from 0 to 63, as said below
- conductance: float32 [64, 3, 128, 128], P('tile'), may hold values from -0.15625 to 0.15625
- vertical: float32 [63, 8192], P(None, 'tile'), may hold values from 0.05 to 60
- rainfall: float32 [128, 8192], P('dom', 'tile'), may hold values from -6 to 6
Outputs:
- forecast: float32 [64, 128, 8192], P(None, 'dom', 'tile')
Inputs may be any that keep to these rules, and one draw needn't show every extreme that they name: `ancestors`: each group of 16 new particles p with the same p // 16 copies at most 2 distinct old particles of any one group of 16 old particles, and exactly 2 distinct ones of the old group with the same index. `adjacency`: row b is b, then b or b - 1, then b or b + 1; b - 1 is named at blocks 64 // 2 and 28, b + 1 at blocks 64 // 2 - 1 and 35.
All inputs are finite; a program needn't handle non-finite values.
Results may differ from a plain program's by a relative error of at most 0.0003.
Values sent between devices are 32-bit elements; how exact they have to be, the bound alone decides.
No kernel may reach another device: no remote copies, remote signals or barrier semaphores. Data moves between devices by JAX's collectives and lax.ppermute only.
A program may use at most 192 MiB of HBM per device.

v0:
```python
import jax
import jax.numpy as jnp
from jax import lax
from jax.sharding import PartitionSpec as P

SUBSTEPS = 8


def extended(cells, sides, width):
    for axis, dim in sides:
        count = lax.axis_size(axis)
        ends = count - 1
        head = lax.slice_in_dim(cells, 0, width, axis=dim)
        tail = lax.slice_in_dim(cells, cells.shape[dim] - width, cells.shape[dim], axis=dim)
        cells = jnp.concatenate(
            [
                lax.ppermute(tail, axis, [(i, (i + 1) % count) for i in range(ends)]),
                cells,
                lax.ppermute(head, axis, [((i + 1) % count, i) for i in range(ends)]),
            ],
            axis=dim,
        )
    return cells


def factorize(vertical):
    layers = vertical.shape[0] + 1
    zero = jnp.zeros_like(vertical[0])
    above_rows = [zero] + [vertical[l] for l in range(layers - 1)]
    below_rows = [vertical[l] for l in range(layers - 1)] + [zero]
    inverse_rows = []
    ecoef_rows = []
    e_prev = zero
    for l in range(layers):
        d_row = 1.0 + above_rows[l] + below_rows[l]
        inv = 1.0 / (d_row - above_rows[l] * e_prev)
        e_prev = below_rows[l] * inv
        inverse_rows.append(inv)
        ecoef_rows.append(e_prev)
    return (above_rows, inverse_rows, ecoef_rows)


def solve(rhs, above, inverse, ecoef):
    layers = rhs.shape[0]
    ys = []
    y_prev = jnp.zeros_like(rhs[0])
    for l in range(layers):
        y_prev = (rhs[l] + above[l][None] * y_prev) * inverse[l][None]
        ys.append(y_prev)
    xs = [None] * layers
    x_next = jnp.zeros_like(rhs[0])
    for l in range(layers - 1, -1, -1):
        x_next = ys[l] + ecoef[l][None] * x_next
        xs[l] = x_next
    return jnp.stack(xs, 0)


def lateral(state, coeff, links):
    layers, count, width = state.shape
    nblk, nlink, span, _ = coeff.shape
    blocks = state.reshape(layers, count, width // span, span)
    picked = jnp.take(blocks, links, axis=2)
    flux = jnp.einsum("lpbkc,bkdc->lpbd", picked, coeff, precision=lax.Precision.HIGHEST)
    return flux.reshape(layers, count, nblk * span)


def advance(state, flux, rain, above, inverse, ecoef):
    rhs = state + flux
    rhs = rhs.at[0].add(rain)
    return solve(rhs, above, inverse, ecoef)


def shards(moisture, ancestors, adjacency, conductance, vertical, rainfall):
    layers, count, width = moisture.shape
    nblk, nlink, span, _ = conductance.shape
    groups = lax.axis_size("dom")
    mine = lax.axis_index("dom")
    capacity = (count + groups - 1) // groups
    table = ancestors.reshape(groups, count)
    local = jnp.arange(count, dtype=jnp.int32)
    slots_range = jnp.arange(capacity, dtype=jnp.int32)
    wanted = jnp.any(table[:, :, None] == (mine * count + local)[None, None, :], axis=1)
    ranks = jnp.cumsum(wanted.astype(jnp.int32), axis=1) - 1
    chosen = wanted[:, :, None] & (ranks[:, :, None] == slots_range[None, None, :])
    picks = jnp.sum(jnp.where(chosen, local[None, :, None], 0), axis=1)
    outgoing = jnp.take(moisture, picks.reshape(-1), axis=1)
    incoming = lax.all_to_all(outgoing, "dom", split_axis=1, concat_axis=1, tiled=True)
    own = lax.dynamic_index_in_dim(table, mine, 0, keepdims=False)
    every = jnp.arange(groups * count, dtype=jnp.int32).reshape(groups, count)
    present = jnp.any(own[None, None, :] == every[:, :, None], axis=2)
    order_in = (jnp.cumsum(present.astype(jnp.int32), axis=1) - 1).reshape(-1)
    where_from = own // count * capacity + jnp.take(order_in, own)
    state = jnp.take(incoming, where_from, axis=1)
    tile = lax.axis_index("tile")
    first = tile * nblk
    mylinks = lax.dynamic_slice_in_dim(adjacency, first, nblk, 0)
    above, inverse, ecoef = factorize(vertical)
    for step in range(SUBSTEPS):
        wide = extended(state, (("tile", 2),), span)
        flux = lateral(wide, conductance, mylinks - first + 1)
        state = advance(state, flux, rainfall, above, inverse, ecoef)
    return state


def solution(mesh):
    in_specs = (
        P(None, "dom", "tile"),
        P(),
        P(),
        P("tile", None, None, None),
        P(None, "tile"),
        P("dom", "tile"),
    )
    out_specs = P(None, "dom", "tile")
    return jax.shard_map(shards, mesh=mesh, in_specs=in_specs, out_specs=out_specs, check_vma=False)
```

profile of v0, /device:TPU:0, one launch (start us, length us, event | category | flops | bytes accessed | tf_op | source)
XLA Modules:
  0.0 636.3 jit_solution(219625120239772801)
XLA Ops:
  18.3 24.7 %all-to-all-done = f32[64,16,512]{2,0,1:T(8,128)} async-done(((f32[64,16,512]{2,0,1:T(8,128)}), f32[64,16,512]{2,0,1:T(8,128)}, u32[]{:S(2)}, u32[]{:S(2)}) %all-to-all-start) | async-done | bytes 2097184 | tf_op jit(solution)/shard_map/all_to_all | solution.py:87
  52.8 8.7 %collective-permute-done = f32[64,16,128]{2,1,0:T(8,128)S(1)} collective-permute-done((f32[64,16,128]{2,1,0:T(8,128)S(1)}, f32[64,16,128]{2,1,0:T(8,128)S(1)}, u32[]{:S(2)}, u32[]{:S(2)}) %collective-permute-start) | collective-permute-done | bytes 524320 | tf_op jit(solution)/shard_map/ppermute | solution.py:17
  67.8 5.6 gather_fusion.3
  73.4 8.5 %fusion.41 = f32[4,64,2,8,128]{4,3,2,1,0:T(8,128)S(1)} fusion(f32[4,3,64,16,128]{4,3,2,1,0:T(8,128)} %bitcast.5115, pred[4,3]{1,0:T(4,128)(4,1)S(1)} %copy.3774, f32[4,3,128,128]{3,2,1,0:T(8,128)S(1)} %copy-done.2), kind=kOutput, calls=%fused_computation.78 | convolution fusion | flops 2417491968 | bytes 9175052 | tf_op jit(solution)/shard_map/lpbkc,bkdc->lpbd/dot_general | solution.py:63
  91.9 8.3 %collective-permute-done.2 = f32[64,16,128]{2,1,0:T(8,128)S(1)} collective-permute-done((f32[64,16,128]{2,1,0:T(8,128)S(1)}, f32[64,16,128]{2,1,0:T(8,128)S(1)}, u32[]{:S(2)}, u32[]{:S(2)}) %collective-permute-start.2) | collective-permute-done | bytes 524320 | tf_op jit(solution)/shard_map/ppermute | solution.py:17
  108.0 5.6 gather_fusion.4
  113.6 8.3 %fusion.44 = f32[4,64,2,8,128]{4,3,2,1,0:T(8,128)S(1)} fusion(f32[4,3,64,16,128]{4,3,2,1,0:T(8,128)} %bitcast.5116, pred[4,3]{1,0:T(4,128)(4,1)S(1)} %copy.3774, f32[4,3,128,128]{3,2,1,0:T(8,128)S(1)} %copy-done.2), kind=kOutput, calls=%fused_computation.79 | convolution fusion | flops 2417491968 | bytes 9175052 | tf_op jit(solution)/shard_map/lpbkc,bkdc->lpbd/dot_general | solution.py:63
  172.7 7.5 %collective-permute-done.4 = f32[64,16,128]{2,1,0:T(8,128)S(1)} collective-permute-done((f32[64,16,128]{2,1,0:T(8,128)S(1)}, f32[64,16,128]{2,1,0:T(8,128)S(1)}, u32[]{:S(2)}, u32[]{:S(2)}) %collective-permute-start.4) | collective-permute-done | bytes 524320 | tf_op jit(solution)/shard_map/ppermute | solution.py:17
  188.0 5.6 gather_fusion.5
  193.6 8.3 %fusion.47 = f32[4,64,2,8,128]{4,3,2,1,0:T(8,128)S(1)} fusion(f32[4,3,64,16,128]{4,3,2,1,0:T(8,128)} %bitcast.5117, pred[4,3]{1,0:T(4,128)(4,1)S(1)} %copy.3774, f32[4,3,128,128]{3,2,1,0:T(8,128)S(1)} %copy-done.2), kind=kOutput, calls=%fused_computation.80 | convolution fusion | flops 2417491968 | bytes 9175052 | tf_op jit(solution)/shard_map/lpbkc,bkdc->lpbd/dot_general | solution.py:63
  252.8 6.5 %collective-permute-done.6 = f32[64,16,128]{2,1,0:T(8,128)S(1)} collective-permute-done((f32[64,16,128]{2,1,0:T(8,128)S(1)}, f32[64,16,128]{2,1,0:T(8,128)S(1)}, u32[]{:S(2)}, u32[]{:S(2)}) %collective-permute-start.6) | collective-permute-done | bytes 524320 | tf_op jit(solution)/shard_map/ppermute | solution.py:17
  267.1 5.6 gather_fusion.6
  272.7 8.3 %fusion.50 = f32[4,64,2,8,128]{4,3,2,1,0:T(8,128)S(1)} fusion(f32[4,3,64,16,128]{4,3,2,1,0:T(8,128)} %bitcast.5118, pred[4,3]{1,0:T(4,128)(4,1)S(1)} %copy.3774, f32[4,3,128,128]{3,2,1,0:T(8,128)S(1)} %copy-done.2), kind=kOutput, calls=%fused_computation.81 | convolution fusion | flops 2417491968 | bytes 9175052 | tf_op jit(solution)/shard_map/lpbkc,bkdc->lpbd/dot_general | solution.py:63
  332.0 5.4 collective-permute-done.8
  345.2 5.6 gather_fusion.7
  350.8 8.3 %fusion.53 = f32[4,64,2,8,128]{4,3,2,1,0:T(8,128)S(1)} fusion(f32[4,3,64,16,128]{4,3,2,1,0:T(8,128)} %bitcast.5119, pred[4,3]{1,0:T(4,128)(4,1)S(1)} %copy.3774, f32[4,3,128,128]{3,2,1,0:T(8,128)S(1)} %copy-done.2), kind=kOutput, calls=%fused_computation.82 | convolution fusion | flops 2417491968 | bytes 9175052 | tf_op jit(solution)/shard_map/lpbkc,bkdc->lpbd/dot_general | solution.py:63
  409.9 5.2 collective-permute-done.10
  423.1 5.6 gather_fusion.8
  428.8 8.3 %fusion.56 = f32[4,64,2,8,128]{4,3,2,1,0:T(8,128)S(1)} fusion(f32[4,3,64,16,128]{4,3,2,1,0:T(8,128)} %bitcast.5120, pred[4,3]{1,0:T(4,128)(4,1)S(1)} %copy.3774, f32[4,3,128,128]{3,2,1,0:T(8,128)S(1)} %copy-done.2), kind=kOutput, calls=%fused_computation.83 | convolution fusion | flops 2417491968 | bytes 9175052 | tf_op jit(solution)/shard_map/lpbkc,bkdc->lpbd/dot_general | solution.py:63
  487.5 5.1 collective-permute-done.12
  500.8 5.6 gather_fusion.9
  506.4 8.3 %fusion.59 = f32[4,64,2,8,128]{4,3,2,1,0:T(8,128)S(1)} fusion(f32[4,3,64,16,128]{4,3,2,1,0:T(8,128)} %bitcast.5121, pred[4,3]{1,0:T(4,128)(4,1)S(1)} %copy.3774, f32[4,3,128,128]{3,2,1,0:T(8,128)S(1)} %copy-done.2), kind=kOutput, calls=%fused_computation.84 | convolution fusion | flops 2417491968 | bytes 9175052 | tf_op jit(solution)/shard_map/lpbkc,bkdc->lpbd/dot_general | solution.py:63
  578.4 5.6 gather_fusion.10
  584.0 8.3 %fusion.62 = f32[4,64,2,8,128]{4,3,2,1,0:T(8,128)S(1)} fusion(f32[4,3,64,16,128]{4,3,2,1,0:T(8,128)} %bitcast.5114, pred[4,3]{1,0:T(4,128)(4,1)S(1)} %copy.3774, f32[4,3,128,128]{3,2,1,0:T(8,128)S(1)} %copy-done.2), kind=kOutput, calls=%fused_computation.85 | convolution fusion | flops 2417491968 | bytes 9175052 | tf_op jit(solution)/shard_map/lpbkc,bkdc->lpbd/dot_general | solution.py:63
  (641 shorter events, 452.0 us)
Async XLA Ops:
  10.9 4.7 copy-start.7
  10.9 6.6 %copy-start.9 = (s32[64,3]{0,1:T(4,128)S(1)}, s32[64,3]{0,1:T(4,128)}, u32[]{:S(2)}) copy-start(s32[64,3]{0,1:T(4,128)} %param.28) | copy-start | bytes 2308
  10.9 32.0 %all-to-all-start = ((f32[64,16,512]{2,0,1:T(8,128)}), f32[64,16,512]{2,0,1:T(8,128)}, u32[]{:S(2)}, u32[]{:S(2)}) async-start(f32[64,16,512]{2,0,1:T(8,128)} %copy.3772), calls=%async_computation | async-start | bytes 4194304 | tf_op jit(solution)/shard_map/all_to_all | solution.py:87
  46.7 14.8 %collective-permute-start = (f32[64,16,128]{2,1,0:T(8,128)S(1)}, f32[64,16,128]{2,1,0:T(8,128)S(1)}, u32[]{:S(2)}, u32[]{:S(2)}) collective-permute-start(f32[64,16,128]{2,1,0:T(8,128)S(1)} %get-tuple-element.796), channel_id=1, source_target_pairs={{0,8},{8,16},{16,24},{24,32},{32,40},{40,48},{48,56},{56,64},{64,7... | collective-permute-start | bytes 1572872 | tf_op jit(solution)/shard_map/ppermute | solution.py:17
  50.6 15.2 %collective-permute-start.1 = (f32[64,16,128]{2,1,0:T(8,128)S(1)}, f32[64,16,128]{2,1,0:T(8,128)S(1)}, u32[]{:S(2)}, u32[]{:S(2)}) collective-permute-start(f32[64,16,128]{2,1,0:T(8,128)S(1)} %get-tuple-element.797), channel_id=1, source_target_pairs={{8,0},{16,8},{24,16},{32,24},{40,32},{48,40},{56,48},{64,56},{72,6... | collective-permute-start | bytes 1572872 | tf_op jit(solution)/shard_map/ppermute | solution.py:19
  52.4 15.4 %copy-start.8 = (s32[1024]{0:T(1024)}, s32[1024]{0:T(1024)S(1)}, u32[]{:S(2)}) copy-start(s32[1024]{0:T(1024)S(1)} %pad_clamp_fusion) | copy-start | bytes 12292
  67.8 5.6 copy-start.2
  73.4 8.5 %copy-start.5 = (f32[16,64,512]{2,1,0:T(8,128)S(1)}, f32[16,64,512]{2,1,0:T(8,128)}, u32[]{:S(2)}) copy-start(f32[16,64,512]{2,1,0:T(8,128)} %copy-done.4) | copy-start | bytes 6291460
  86.6 17.7 %copy-start.6 = (f32[64,16,512]{2,1,0:T(8,128)}, f32[64,16,512]{2,1,0:T(8,128)S(1)}, u32[]{:S(2)}) copy-start(f32[64,16,512]{2,1,0:T(8,128)S(1)} %constant_dynamic-update-slice_fusion) | copy-start | bytes 6291460
  86.7 13.4 %collective-permute-start.2 = (f32[64,16,128]{2,1,0:T(8,128)S(1)}, f32[64,16,128]{2,1,0:T(8,128)S(1)}, u32[]{:S(2)}, u32[]{:S(2)}) collective-permute-start(f32[64,16,128]{2,1,0:T(8,128)S(1)} %get-tuple-element.794), channel_id=1, source_target_pairs={{0,8},{8,16},{16,24},{24,32},{32,40},{40,48},{48,56},{56,64},{64,7... | collective-permute-start | bytes 1572872 | tf_op jit(solution)/shard_map/ppermute | solution.py:17
  90.4 13.9 %collective-permute-start.3 = (f32[64,16,128]{2,1,0:T(8,128)S(1)}, f32[64,16,128]{2,1,0:T(8,128)S(1)}, u32[]{:S(2)}, u32[]{:S(2)}) collective-permute-start(f32[64,16,128]{2,1,0:T(8,128)S(1)} %get-tuple-element.795), channel_id=1, source_target_pairs={{8,0},{16,8},{24,16},{32,24},{40,32},{48,40},{56,48},{64,56},{72,6... | collective-permute-start | bytes 1572872 | tf_op jit(solution)/shard_map/ppermute | solution.py:19
  166.8 13.4 %collective-permute-start.4 = (f32[64,16,128]{2,1,0:T(8,128)S(1)}, f32[64,16,128]{2,1,0:T(8,128)S(1)}, u32[]{:S(2)}, u32[]{:S(2)}) collective-permute-start(f32[64,16,128]{2,1,0:T(8,128)S(1)} %get-tuple-element.792), channel_id=1, source_target_pairs={{0,8},{8,16},{16,24},{24,32},{32,40},{40,48},{48,56},{56,64},{64,7... | collective-permute-start | bytes 1572872 | tf_op jit(solution)/shard_map/ppermute | solution.py:17
  171.2 13.1 %collective-permute-start.5 = (f32[64,16,128]{2,1,0:T(8,128)S(1)}, f32[64,16,128]{2,1,0:T(8,128)S(1)}, u32[]{:S(2)}, u32[]{:S(2)}) collective-permute-start(f32[64,16,128]{2,1,0:T(8,128)S(1)} %get-tuple-element.793), channel_id=1, source_target_pairs={{8,0},{16,8},{24,16},{32,24},{40,32},{48,40},{56,48},{64,56},{72,6... | collective-permute-start | bytes 1572872 | tf_op jit(solution)/shard_map/ppermute | solution.py:19
  246.9 12.4 %collective-permute-start.6 = (f32[64,16,128]{2,1,0:T(8,128)S(1)}, f32[64,16,128]{2,1,0:T(8,128)S(1)}, u32[]{:S(2)}, u32[]{:S(2)}) collective-permute-start(f32[64,16,128]{2,1,0:T(8,128)S(1)} %get-tuple-element.790), channel_id=1, source_target_pairs={{0,8},{8,16},{16,24},{24,32},{32,40},{40,48},{48,56},{56,64},{64,7... | collective-permute-start | bytes 1572872 | tf_op jit(solution)/shard_map/ppermute | solution.py:17
  251.2 12.2 %collective-permute-start.7 = (f32[64,16,128]{2,1,0:T(8,128)S(1)}, f32[64,16,128]{2,1,0:T(8,128)S(1)}, u32[]{:S(2)}, u32[]{:S(2)}) collective-permute-start(f32[64,16,128]{2,1,0:T(8,128)S(1)} %get-tuple-element.791), channel_id=1, source_target_pairs={{8,0},{16,8},{24,16},{32,24},{40,32},{48,40},{56,48},{64,56},{72,6... | collective-permute-start | bytes 1572872 | tf_op jit(solution)/shard_map/ppermute | solution.py:19
  325.9 11.5 %collective-permute-start.8 = (f32[64,16,128]{2,1,0:T(8,128)S(1)}, f32[64,16,128]{2,1,0:T(8,128)S(1)}, u32[]{:S(2)}, u32[]{:S(2)}) collective-permute-start(f32[64,16,128]{2,1,0:T(8,128)S(1)} %get-tuple-element.788), channel_id=1, source_target_pairs={{0,8},{8,16},{16,24},{24,32},{32,40},{40,48},{48,56},{56,64},{64,7... | collective-permute-start | bytes 1572872 | tf_op jit(solution)/shard_map/ppermute | solution.py:17
  330.3 11.3 %collective-permute-start.9 = (f32[64,16,128]{2,1,0:T(8,128)S(1)}, f32[64,16,128]{2,1,0:T(8,128)S(1)}, u32[]{:S(2)}, u32[]{:S(2)}) collective-permute-start(f32[64,16,128]{2,1,0:T(8,128)S(1)} %get-tuple-element.789), channel_id=1, source_target_pairs={{8,0},{16,8},{24,16},{32,24},{40,32},{48,40},{56,48},{64,56},{72,6... | collective-permute-start | bytes 1572872 | tf_op jit(solution)/shard_map/ppermute | solution.py:19
  404.1 11.0 %collective-permute-start.10 = (f32[64,16,128]{2,1,0:T(8,128)S(1)}, f32[64,16,128]{2,1,0:T(8,128)S(1)}, u32[]{:S(2)}, u32[]{:S(2)}) collective-permute-start(f32[64,16,128]{2,1,0:T(8,128)S(1)} %get-tuple-element.786), channel_id=1, source_target_pairs={{0,8},{8,16},{16,24},{24,32},{32,40},{40,48},{48,56},{56,64},{64,7... | collective-permute-start | bytes 1572872 | tf_op jit(solution)/shard_map/ppermute | solution.py:17
  408.4 11.1 %collective-permute-start.11 = (f32[64,16,128]{2,1,0:T(8,128)S(1)}, f32[64,16,128]{2,1,0:T(8,128)S(1)}, u32[]{:S(2)}, u32[]{:S(2)}) collective-permute-start(f32[64,16,128]{2,1,0:T(8,128)S(1)} %get-tuple-element.787), channel_id=1, source_target_pairs={{8,0},{16,8},{24,16},{32,24},{40,32},{48,40},{56,48},{64,56},{72,6... | collective-permute-start | bytes 1572872 | tf_op jit(solution)/shard_map/ppermute | solution.py:19
  482.0 10.7 %collective-permute-start.12 = (f32[64,16,128]{2,1,0:T(8,128)S(1)}, f32[64,16,128]{2,1,0:T(8,128)S(1)}, u32[]{:S(2)}, u32[]{:S(2)}) collective-permute-start(f32[64,16,128]{2,1,0:T(8,128)S(1)} %get-tuple-element.784), channel_id=1, source_target_pairs={{0,8},{8,16},{16,24},{24,32},{32,40},{40,48},{48,56},{56,64},{64,7... | collective-permute-start | bytes 1572872 | tf_op jit(solution)/shard_map/ppermute | solution.py:17
  486.0 11.1 %collective-permute-start.13 = (f32[64,16,128]{2,1,0:T(8,128)S(1)}, f32[64,16,128]{2,1,0:T(8,128)S(1)}, u32[]{:S(2)}, u32[]{:S(2)}) collective-permute-start(f32[64,16,128]{2,1,0:T(8,128)S(1)} %get-tuple-element.785), channel_id=1, source_target_pairs={{8,0},{16,8},{24,16},{32,24},{40,32},{48,40},{56,48},{64,56},{72,6... | collective-permute-start | bytes 1572872 | tf_op jit(solution)/shard_map/ppermute | solution.py:19
  559.6 10.7 %collective-permute-start.14 = (f32[64,16,128]{2,1,0:T(8,128)S(1)}, f32[64,16,128]{2,1,0:T(8,128)S(1)}, u32[]{:S(2)}, u32[]{:S(2)}) collective-permute-start(f32[64,16,128]{2,1,0:T(8,128)S(1)} %get-tuple-element.782), channel_id=1, source_target_pairs={{0,8},{8,16},{16,24},{24,32},{32,40},{40,48},{48,56},{56,64},{64,7... | collective-permute-start | bytes 1572872 | tf_op jit(solution)/shard_map/ppermute | solution.py:17
  563.7 11.1 %collective-permute-start.15 = (f32[64,16,128]{2,1,0:T(8,128)S(1)}, f32[64,16,128]{2,1,0:T(8,128)S(1)}, u32[]{:S(2)}, u32[]{:S(2)}) collective-permute-start(f32[64,16,128]{2,1,0:T(8,128)S(1)} %get-tuple-element.783), channel_id=1, source_target_pairs={{8,0},{16,8},{24,16},{32,24},{40,32},{48,40},{56,48},{64,56},{72,6... | collective-permute-start | bytes 1572872 | tf_op jit(solution)/shard_map/ppermute | solution.py:19
  605.6 30.4 %copy-start.1 = (f32[64,16,512]{2,1,0:T(8,128)S(1)}, f32[64,16,512]{2,1,0:T(8,128)}, u32[]{:S(2)}) copy-start(f32[64,16,512]{2,1,0:T(8,128)} %param.26) | copy-start | bytes 6291460
  (3 other events, 4.4 us)
where the time goes:
time: 645 us; the launch traced here: 636 us
  other arithmetic  209 us (32%)
  local copies, waits for them, and re-layouts  199 us (31%)
  waiting for transfers between devices  111 us (17%)
  matrix products  66.6 us (10%)
  starting transfers between devices  50.2 us (8%)
    unnamed x256, other arithmetic  154 us
    unnamed x268, local copies, waits for them, and re-layouts  134 us
    dot_general x8, matrix products, lateral(): jnp.einsum('lpbkc,bkdc->lpbd', picked, coeff, precision=lax.Precision.HIG...  66.6 us
    ppermute x8, waiting for transfers between devices, extended(): lax.ppermute(tail, axis, [(i, (i + 1) % count) for i in range(ends)])  51.7 us
    gather x8, local copies, waits for them, and re-layouts, lateral(): picked = jnp.take(blocks, links, axis=2)  44.8 us
    ppermute x8, waiting for transfers between devices, extended(): lax.ppermute(head, axis, [((i + 1) % count, i) for i in range(ends)])  34.2 us
    ppermute x8, starting transfers between devices, extended(): lax.ppermute(tail, axis, [(i, (i + 1) % count) for i in range(ends)])  32.9 us
    reshape x8, other arithmetic, lateral(): blocks = state.reshape(layers, count, width // span, span)  27.8 us
  transfers between devices with their start and end apart: 17, of which 17 were waited for; matrix products, arithmetic and copies ran while one was open for 0% of the time, Pallas kernels for 0%

commit v1 on v0

v1 whole, which is shorter than its diff:
```python
import jax
import jax.numpy as jnp
from jax import lax
from jax.experimental import pallas as pl
from jax.experimental.pallas import tpu as pltpu
from jax.sharding import PartitionSpec as P

SUBSTEPS = 8
RING = 4
OWN = 4
LAYERS = 64
HALF = 32
SPAN = 128
WIDTH = 512
GROUP = 16
GROUPS = 8
PAIRS = 16
ROWS = HALF * 8
MSG = 2 * (3 * SPAN + LAYERS)
F32 = jnp.float32
BF16 = jnp.bfloat16
VMEM_LIMIT = 60 * 1024 * 1024


def params():
    return pltpu.CompilerParams(vmem_limit_bytes=VMEM_LIMIT)


def shape(dims, dtype=F32):
    return jax.ShapeDtypeStruct(dims, dtype)


SMEM = pl.BlockSpec(memory_space=pltpu.SMEM)
VMEM = pl.BlockSpec(memory_space=pltpu.VMEM)
ANY = pl.BlockSpec(memory_space=pl.ANY)


def z_pairs(s):
    return [(4 * x + z, 4 * x + (z + s) % 4) for x in range(4) for z in range(4)]


def x_pairs(s):
    out = []
    for x in range(4):
        for z in range(4):
            step = -1 if (z - s) % 4 < 2 else 1
            out.append((4 * x + z, 4 * ((x + step) % 4) + z))
    return out


def dom_pairs(r):
    return [(g, (g + r) % GROUPS) for g in range(GROUPS)]


def core_pairs():
    return [(g, g ^ 1) for g in range(GROUPS)]


def send_kernel(ids, anc, moist, *refs):
    outs, held, sems = refs[:GROUPS], refs[GROUPS], refs[GROUPS + 1]
    copies = []
    for t in range(WIDTH // SPAN):
        copies.append(pltpu.make_async_copy(moist.at[:, pl.ds(t * SPAN, SPAN)], held.at[t], sems.at[t]))
        copies[-1].start()
    for c in copies:
        c.wait()
    mine = ids[1]
    flip = 7 - lax.broadcasted_iota(jnp.int32, (8, SPAN), 0)
    for r in range(GROUPS):
        target = lax.rem(mine + r, GROUPS)
        low = jnp.int32(GROUP)
        high = jnp.int32(-1)
        for i in range(GROUP):
            v = anc[target * GROUP + i] - mine * GROUP
            inside = (v >= 0) & (v < GROUP)
            low = jnp.where(inside, jnp.minimum(low, v), low)
            high = jnp.where(inside, jnp.maximum(high, v), high)
        low = jnp.minimum(low, GROUP - 1)
        high = jnp.maximum(high, 0)
        for j, p in enumerate((low, high)):
            for t in range(WIDTH // SPAN):
                lanes = slice(t * SPAN, (t + 1) * SPAN)
                rows = held[t, pl.ds(p, LAYERS, stride=GROUP), :]
                outs[r][j, :HALF, lanes] = rows[:HALF]
                for q in range(HALF // 8):
                    part = rows[LAYERS - 8 * (q + 1):LAYERS - 8 * q]
                    outs[r][j, HALF + 8 * q:HALF + 8 * (q + 1), lanes] = jnp.take_along_axis(part, flip, axis=0)


def pack_kernel(ids, anc, rain, *refs):
    ins, outs = refs[:GROUPS], refs[GROUPS:GROUPS + RING]
    slots, least, sems = refs[GROUPS + RING:]
    copies = [pltpu.make_async_copy(ins[r], slots.at[pl.ds(2 * r, 2)], sems.at[r]) for r in range(GROUPS)]
    for c in copies:
        c.start()
    z = lax.rem(ids[0], RING)
    mine = ids[1]
    for g in range(GROUPS):
        least[g] = jnp.int32(1 << 20)
    for i in range(GROUP):
        v = anc[mine * GROUP + i]
        g = v // GROUP
        least[g] = jnp.minimum(least[g], v)
    for c in copies:
        c.wait()
    upper = lax.broadcasted_iota(jnp.int32, (8, WIDTH), 0) < 4
    for s in range(RING):
        owner = lax.rem(z + s, RING)
        for p in range(OWN):
            n = owner * OWN + p
            v = anc[mine * GROUP + n]
            g = v // GROUP
            slot = 2 * lax.rem(mine - g + GROUPS, GROUPS) + jnp.where(v > least[g], 1, 0)
            for t in range(WIDTH // SPAN):
                lanes = slice(t * SPAN, (t + 1) * SPAN)
                for d in range(2):
                    outs[s][t, pl.ds(4 * d + p, HALF, stride=8), :] = slots[slot, d * HALF:(d + 1) * HALF, lanes]
        own_rain = rain[pl.ds(pl.multiple_of(owner // 2 * 8, 8), 8), :]
        own_rain = jnp.where(lax.rem(owner, 2) == 1, pltpu.roll(own_rain, 4, 0), own_rain)
        own_rain = jnp.where(upper, own_rain, 0.0)
        for t in range(WIDTH // SPAN):
            outs[s][t, ROWS:, :] = own_rain[:, t * SPAN:(t + 1) * SPAN]


def coeff_kernel(ids, adj, cond, vert, out):
    tile = ids[0]
    core = lax.rem(ids[1], 2)
    eye = (lax.broadcasted_iota(jnp.int32, (SPAN, SPAN), 0) == lax.broadcasted_iota(jnp.int32, (SPAN, SPAN), 1)).astype(F32)
    for i in range(2):
        local = 2 * core + i
        b = RING * tile + local
        prev = jnp.where(adj[b, 1] == b, 0.0, 1.0).astype(F32)
        after = jnp.where(adj[b, 2] == b, 0.0, 1.0).astype(F32)
        own, first, second = cond[local, 0], cond[local, 1], cond[local, 2]
        base = i * (3 * SPAN + LAYERS)
        out[base:base + SPAN, :] = (first * prev).T
        out[base + SPAN:base + 2 * SPAN, :] = (own + first * (1.0 - prev) + second * (1.0 - after)).T + eye
        out[base + 2 * SPAN:base + 3 * SPAN, :] = (second * after).T
        lanes = pl.ds(pl.multiple_of(local * SPAN, SPAN), SPAN)
        out[base + 3 * SPAN:base + 3 * SPAN + LAYERS - 1, :] = vert[:, lanes]
        out[base + 3 * SPAN + LAYERS - 1:base + 3 * SPAN + LAYERS, :] = jnp.zeros((1, SPAN), F32)


def window_base(z, s, halo):
    t = lax.rem(z - s + RING, RING)
    if halo:
        return jnp.where(t < 2, 24 + 4 * t, 4 * t - 8)
    return 8 + 4 * t


def expand_kernel(ids, *refs):
    msgs = refs[:16]
    w_hi, w_lo, inv_ref, ai_ref, e_ref, d_ref = refs[16:22]
    vs = refs[22]
    z = lax.rem(ids[0], RING)
    core = lax.rem(ids[1], 2)
    zero = jnp.zeros((SPAN, SPAN), BF16)
    at = 0
    for halo in (False, True):
        for s in range(RING):
            base = window_base(z, s, halo) // 2
            for other in (0, 1):
                msg = msgs[at]
                at += 1
                half = core if other == 0 else 1 - core
                k = base + half
                for i in range(2):
                    row = i * (3 * SPAN + LAYERS)
                    cols = slice(i * SPAN, (i + 1) * SPAN)
                    for j in range(3):
                        w = msg[row + j * SPAN:row + (j + 1) * SPAN, :]
                        hi = w.astype(BF16)
                        lo = (w - hi.astype(F32)).astype(BF16)
                        rows = slice((i + j) * SPAN, (i + j + 1) * SPAN)
                        w_hi[k, rows, cols] = hi
                        w_lo[k, rows, cols] = lo
                    empty = slice(3 * SPAN, 4 * SPAN) if i == 0 else slice(0, SPAN)
                    w_hi[k, empty, cols] = zero
                    w_lo[k, empty, cols] = zero
                    vs[k, :, cols] = msg[row + 3 * SPAN:row + 3 * SPAN + LAYERS, :]
    upper = lax.broadcasted_iota(jnp.int32, (8, 2 * SPAN), 0) < 4
    group = 4

    def chunk(c, _):
        e_prev = [jnp.zeros((8, 2 * SPAN), F32)] * group
        for l in range(HALF):
            for q in range(group):
                k = c * group + q
                a_low = vs[k, LAYERS - 1 - l:LAYERS - l, :]
                a_top = vs[k, l - 1:l, :] if l else jnp.zeros((1, 2 * SPAN), F32)
                a = jnp.where(upper, a_top, a_low)
                b = jnp.where(upper, vs[k, l:l + 1, :], vs[k, LAYERS - 2 - l:LAYERS - 1 - l, :])
                inv = 1.0 / (1.0 + a + b - a * e_prev[q])
                e = b * inv
                inv_ref[k, l] = inv
                ai_ref[k, l] = a * inv
                e_ref[k, l] = e
                e_prev[q] = e
        for q in range(group):
            e = e_prev[q]
            d_ref[c * group + q] = 1.0 / (1.0 - e * pltpu.roll(e, 4, 0))
        return 0

    lax.fori_loop(0, PAIRS // group, chunk, 0)


def step_kernel(ids, *refs):
    ins = refs[:8]
    w_hi, w_lo, inv_ref, ai_ref, e_ref, d_ref = refs[8:14]
    outs = refs[14:18]
    xh0, xl0, xh1, xl1, rain, r_a, r_b, final, sems = refs[18:]
    z = lax.rem(ids[0], RING)
    pad = jnp.zeros((ROWS, SPAN), BF16)
    for ref in (xh0, xl0):
        ref[:, :SPAN] = pad
        ref[:, (2 * PAIRS + 1) * SPAN:] = pad
    at = 0
    for halo in (False, True):
        for s in range(RING):
            src = ins[at]
            at += 1
            base = window_base(z, s, halo)
            for t in range(WIDTH // SPAN):
                lanes = pl.ds(pl.multiple_of((base + 1 + t) * SPAN, SPAN), SPAN)
                v = src[t, :ROWS, :]
                hi = v.astype(BF16)
                xh0[:, lanes] = hi
                xl0[:, lanes] = (v - hi.astype(F32)).astype(BF16)
                rain[:, pl.ds(pl.multiple_of((base + t) * SPAN, SPAN), SPAN)] = src[t, ROWS:, :]

    def product(k, xh, xl, r):
        lanes = pl.ds(pl.multiple_of(k * 2 * SPAN, 2 * SPAN), 4 * SPAN)
        h = xh[:, lanes]
        w = w_hi[k]
        acc = jnp.dot(h, w, preferred_element_type=F32)
        acc = acc + jnp.dot(xl[:, lanes], w, preferred_element_type=F32)
        acc = acc + jnp.dot(h, w_lo[k], preferred_element_type=F32)
        r[...] = acc
        r[:8, :] = acc[:8, :] + rain[:, pl.ds(pl.multiple_of(k * 2 * SPAN, 2 * SPAN), 2 * SPAN)]

    def solve(k, r, put):
        y = r[:8, :] * inv_ref[k, 0]
        r[:8, :] = y
        for l in range(1, HALF):
            y = r[8 * l:8 * l + 8, :] * inv_ref[k, l] + ai_ref[k, l] * y
            if l < HALF - 1:
                r[8 * l:8 * l + 8, :] = y
        x = (y + e_ref[k, HALF - 1] * pltpu.roll(y, 4, 0)) * d_ref[k]
        later = x
        for l in range(HALF - 2, -1, -1):
            x = r[8 * l:8 * l + 8, :] + e_ref[k, l] * x
            if l % 2:
                later = x
            else:
                put(k, l // 2, jnp.concatenate([x, later], axis=0))

    for step in range(1, SUBSTEPS + 1):
        src = (xh0, xl0) if step % 2 else (xh1, xl1)
        dst = (xh1, xl1) if step % 2 else (xh0, xl0)
        first, last = step // 2, PAIRS - step // 2

        def put(k, m, v, dst=dst):
            lanes = pl.ds(pl.multiple_of((2 * k + 1) * SPAN, SPAN), 2 * SPAN)
            hi = v.astype(BF16)
            dst[0][16 * m:16 * m + 16, lanes] = hi
            dst[1][16 * m:16 * m + 16, lanes] = (v - hi.astype(F32)).astype(BF16)

        def put_final(k, m, v):
            t = (k - 4) // 2
            s = lax.rem(t - z + RING, RING)
            lanes = pl.ds(pl.multiple_of(lax.rem(k, 2) * 2 * SPAN, 2 * SPAN), 2 * SPAN)
            final[s, 16 * m:16 * m + 16, lanes] = v

        write = put_final if step == SUBSTEPS else put

        product(first, *src, r_a)

        def body(i, _, first=first, src=src, write=write):
            k = first + 2 * i
            product(k + 1, *src, r_b)
            solve(k, r_a, write)
            product(k + 2, *src, r_a)
            solve(k + 1, r_b, write)
            return 0

        lax.fori_loop(0, (last - first) // 2 - 1, body, 0)
        product(last - 1, *src, r_b)
        solve(last - 2, r_a, write)
        solve(last - 1, r_b, write)

    copies = [pltpu.make_async_copy(final.at[s], outs[s], sems.at[s]) for s in range(RING)]
    for c in copies:
        c.start()
    for c in copies:
        c.wait()


def join_kernel(ids, *refs):
    ins, out, held, sems = refs[:RING], refs[RING], refs[RING + 1], refs[RING + 2]
    z = lax.rem(ids[0], RING)
    copies = []
    for s in range(RING):
        copies.append(pltpu.make_async_copy(ins[s], held.at[lax.rem(z - s + RING, RING)], sems.at[s]))
        copies[-1].start()
    for c in copies:
        c.wait()
    upper = lax.broadcasted_iota(jnp.int32, (8, WIDTH), 0) < 4

    def body(l, _):
        rows = pl.ds(pl.multiple_of(l * 8, 8), 8)
        for h in range(2):
            a = held[2 * h, rows, :]
            b = held[2 * h + 1, rows, :]
            out[l, 8 * h:8 * h + 8, :] = jnp.where(upper, a, pltpu.roll(b, 4, 0))
            out[LAYERS - 1 - l, 8 * h:8 * h + 8, :] = jnp.where(upper, pltpu.roll(a, 4, 0), b)
        return 0

    lax.fori_loop(0, HALF, body, 0, unroll=4)


def shards(moisture, ancestors, adjacency, conductance, vertical, rainfall):
    ids = jnp.stack([lax.axis_index("tile"), lax.axis_index("dom")]).astype(jnp.int32)

    flat = moisture.reshape(LAYERS * GROUP, WIDTH)
    sent = pl.pallas_call(
        send_kernel,
        out_shape=[shape((2, LAYERS, WIDTH))] * GROUPS,
        in_specs=[SMEM, SMEM, ANY],
        out_specs=[VMEM] * GROUPS,
        scratch_shapes=[
            pltpu.VMEM((WIDTH // SPAN, LAYERS * GROUP, SPAN), F32),
            pltpu.SemaphoreType.DMA((WIDTH // SPAN,)),
        ],
        compiler_params=params(),
    )(ids, ancestors, flat)
    coeff = pl.pallas_call(
        coeff_kernel,
        out_shape=shape((MSG, SPAN)),
        in_specs=[SMEM, SMEM, VMEM, VMEM],
        out_specs=VMEM,
        compiler_params=params(),
    )(ids, adjacency, conductance, vertical)

    got = [sent[0]] + [lax.ppermute(sent[r], "dom", dom_pairs(r)) for r in range(1, GROUPS)]
    c_ring = [coeff] + [lax.ppermute(coeff, "tile", z_pairs(s)) for s in range(1, RING)]
    c_side = [lax.ppermute(c_ring[s], "tile", x_pairs(s)) for s in range(RING)]
    c_all = []
    for c in c_ring + c_side:
        c_all += [c, lax.ppermute(c, "dom", core_pairs())]

    mine = pl.pallas_call(
        pack_kernel,
        out_shape=[shape((WIDTH // SPAN, ROWS + 8, SPAN))] * RING,
        in_specs=[SMEM, SMEM, VMEM] + [ANY] * GROUPS,
        out_specs=[VMEM] * RING,
        scratch_shapes=[
            pltpu.VMEM((2 * GROUPS, LAYERS, WIDTH), F32),
            pltpu.SMEM((GROUPS,), jnp.int32),
            pltpu.SemaphoreType.DMA((GROUPS,)),
        ],
        compiler_params=params(),
    )(ids, ancestors, rainfall, *got)
    ring = [mine[0]] + [lax.ppermute(mine[s], "tile", z_pairs(s)) for s in range(1, RING)]
    side = [lax.ppermute(ring[s], "tile", x_pairs(s)) for s in range(RING)]

    coefs = pl.pallas_call(
        expand_kernel,
        out_shape=[shape((PAIRS, 4 * SPAN, 2 * SPAN), BF16)] * 2
        + [shape((PAIRS, HALF, 8, 2 * SPAN))] * 3
        + [shape((PAIRS, 8, 2 * SPAN))],
        in_specs=[SMEM] + [VMEM] * 16,
        out_specs=[VMEM] * 6,
        scratch_shapes=[pltpu.VMEM((PAIRS, LAYERS, 2 * SPAN), F32)],
        compiler_params=params(),
    )(ids, *c_all)

    wide = (ROWS, (2 * PAIRS + 2) * SPAN)
    back = pl.pallas_call(
        step_kernel,
        out_shape=[shape((ROWS, WIDTH))] * RING,
        in_specs=[SMEM] + [VMEM] * 14,
        out_specs=[ANY] * RING,
        scratch_shapes=[pltpu.VMEM(wide, BF16)] * 4
        + [
            pltpu.VMEM((8, 2 * PAIRS * SPAN), F32),
            pltpu.VMEM((ROWS, 2 * SPAN), F32),
            pltpu.VMEM((ROWS, 2 * SPAN), F32),
            pltpu.VMEM((RING, ROWS, WIDTH), F32),
            pltpu.SemaphoreType.DMA((RING,)),
        ],
        compiler_params=params(),
    )(ids, *ring, *side, *coefs)

    home = [back[0]] + [lax.ppermute(back[s], "tile", z_pairs(s)) for s in range(1, RING)]
    return pl.pallas_call(
        join_kernel,
        out_shape=shape((LAYERS, GROUP, WIDTH)),
        in_specs=[SMEM] + [ANY] * RING,
        out_specs=VMEM,
        scratch_shapes=[pltpu.VMEM((RING, ROWS, WIDTH), F32), pltpu.SemaphoreType.DMA((RING,))],
        compiler_params=params(),
    )(ids, *home)


def solution(mesh):
    in_specs = (
        P(None, "dom", "tile"),
        P(),
        P(),
        P("tile", None, None, None),
        P(None, "tile"),
        P("dom", "tile"),
    )
    out_specs = P(None, "dom", "tile")
    return jax.shard_map(shards, mesh=mesh, in_specs=in_specs, out_specs=out_specs, check_vma=False)
```

time: 645 us -> 191 us (0.30); the launches traced: 636 us -> 189 us
  other arithmetic: 209 us -> 0.59 us
  local copies, waits for them, and re-layouts: 199 us -> 4.46 us
  Pallas kernels: 0 us -> 69.8 us
  matrix products: 66.6 us -> 0 us
  waiting for transfers between devices: 111 us -> 67.6 us
    unnamed x256 -> x0, other arithmetic: 154 us -> none
    unnamed x268 -> x63, local copies, waits for them, and re-layouts: 134 us -> 4.46 us
    pallas_call x0 -> x6, Pallas kernels: none -> 69.8 us  [the longest x1 42.7 us: shards(): pl.pallas_call(step_kernel, out_shape=[shape((ROWS, WIDTH))] * RING, in_s...]
    dot_general x8 -> x0, matrix products: 66.6 us -> none  [lateral(): jnp.einsum('lpbkc,bkdc->lpbd', picked, coeff, precision=lax.Precision.HIG...]
    gather x11 -> x0, local copies, waits for them, and re-layouts: 52.5 us -> none  [the longest x8 44.8 us: lateral(): picked = jnp.take(blocks, links, axis=2)]
    reshape x8 -> x0, other arithmetic: 27.8 us -> none  [lateral(): blocks = state.reshape(layers, count, width // span, span)]
    all_to_all x1 -> x0, waiting for transfers between devices: 24.7 us -> none  [shards(): lax.all_to_all(outgoing, 'dom', split_axis=1, concat_axis=1, tiled=True)]
    ppermute x16 -> x32, waiting for transfers between devices: 85.9 us -> 67.6 us  [the longest x3 22.9 us: shards(): lax.ppermute(back[s], 'tile', z_pairs(s))]
  transfers between devices with their start and end apart: 17 -> 32, of which waited for: 17 -> 11; matrix products, arithmetic and copies ran while one was open for 0% -> 1% of each run, Pallas kernels for 0% -> 10%
where the time goes in v1:
time: 191 us; the launch traced here: 189 us
  Pallas kernels  69.8 us (37%)
  waiting for transfers between devices  67.6 us (35%)
  starting transfers between devices  46.4 us (24%)
  local copies, waits for them, and re-layouts  4.46 us (2%)
    pallas_call x1, Pallas kernels, shards(): pl.pallas_call(step_kernel, out_shape=[shape((ROWS, WIDTH))] * RING, in_s...  42.7 us
    ppermute x3, waiting for transfers between devices, shards(): lax.ppermute(back[s], 'tile', z_pairs(s))  22.9 us
    ppermute x4, waiting for transfers between devices, shards(): c_side = [lax.ppermute(c_ring[s], 'tile', x_pairs(s)) for s in range(RING)]  20.7 us
    ppermute x7, starting transfers between devices, shards(): lax.ppermute(sent[r], 'dom', dom_pairs(r))  13.6 us
    pallas_call x1, Pallas kernels, shards(): pl.pallas_call(expand_kernel, out_shape=[shape((PAIRS, 4 * SPAN, 2 * SPAN...  12.3 us
    ppermute x3, starting transfers between devices, shards(): lax.ppermute(coeff, 'tile', z_pairs(s))  9.54 us
    ppermute x4, waiting for transfers between devices, shards(): side = [lax.ppermute(ring[s], 'tile', x_pairs(s)) for s in range(RING)]  8.95 us
    ppermute x3, waiting for transfers between devices, shards(): lax.ppermute(mine[s], 'tile', z_pairs(s))  7.13 us
  transfers between devices with their start and end apart: 32, of which 11 were waited for; matrix products, arithmetic and copies ran while one was open for 1% of the time, Pallas kernels for 10%

profile of v1, /device:TPU:0, one launch (start us, length us, event | category | flops | bytes accessed | tf_op | source)
XLA Modules:
  0.0 189.3 jit_solution(10158667581506981771)
XLA Ops:
  0.6 4.7 %shard_map.64 = (f32[2,64,512]{2,1,0:T(8,128)}, f32[2,64,512]{2,1,0:T(8,128)}, f32[2,64,512]{2,1,0:T(8,128)}, f32[2,64,512]{2,1,0:T(8,128)}, f32[2,64,512]{2,1,0...) custom-call(s32[2]{0:T(128)} %pad_add_fusion.ids, s32[128]{0:T(128)} %anc.3, ...), custom_call_target="tpu_custom_call" | custom-call | tf_op jit(solution)/shard_map/pallas_call | solution.py:325
  7.1 2.2 %collective-permute-start.2 = (f32[2,64,512]{2,1,0:T(8,128)}, f32[2,64,512]{2,1,0:T(8,128)S(1)}, u32[]{:S(2)}, u32[]{:S(2)}) collective-permute-start(f32[2,64,512]{2,1,0:T(8,128)} %get-tuple-element.30), channel_id=1, source_target_pairs={{0,3},{1,4},{2,5},{3,6},{4,7},{5,0},{6,1},{7,2},{8,11},{9,12},{10,... | collective-permute-start | bytes 786440 | tf_op jit(solution)/shard_map/ppermute | solution.py:344
  9.3 1.8 collective-permute-start.3
  12.5 2.2 %shard_map.66.refs_0_ = f32[896,128]{1,0:T(8,128)} custom-call(s32[2]{0:T(128)} %pad_add_fusion.ids, s32[64,3]{1,0:T(8,128)} %copy.7.adj, f32[4,3,128,128]{3,2,1,0:T(8,128)} %cond.1, f32[63,512]{1,0:T(8,128)} %vert.1), custom_call_target="tpu_custom_call" | custom-call | tf_op jit(solution)/shard_map/pallas_call | solution.py:336
  14.7 1.9 %collective-permute-start.15 = (f32[896,128]{1,0:T(8,128)}, f32[896,128]{1,0:T(8,128)S(1)}, u32[]{:S(2)}, u32[]{:S(2)}) collective-permute-start(f32[896,128]{1,0:T(8,128)} %shard_map.66.refs_0_), channel_id=1, source_target_pairs={{0,8},{8,16},{16,24},{24,0},{32,40},{40,48},{48,56},{56,32},{64,72... | collective-permute-start | bytes 1376264 | tf_op jit(solution)/shard_map/ppermute | solution.py:345
  16.6 3.6 %collective-permute-start.17 = (f32[896,128]{1,0:T(8,128)}, f32[896,128]{1,0:T(8,128)S(1)}, u32[]{:S(2)}, u32[]{:S(2)}) collective-permute-start(f32[896,128]{1,0:T(8,128)} %shard_map.66.refs_0_), channel_id=1, source_target_pairs={{0,16},{8,24},{16,0},{24,8},{32,48},{40,56},{48,32},{56,40},{64,80... | collective-permute-start | bytes 1376264 | tf_op jit(solution)/shard_map/ppermute | solution.py:345
  20.2 2.1 %collective-permute-start.4 = (f32[2,64,512]{2,1,0:T(8,128)}, f32[2,64,512]{2,1,0:T(8,128)S(1)}, u32[]{:S(2)}, u32[]{:S(2)}) collective-permute-start(f32[2,64,512]{2,1,0:T(8,128)} %get-tuple-element.32), channel_id=1, source_target_pairs={{0,5},{1,6},{2,7},{3,0},{4,1},{5,2},{6,3},{7,4},{8,13},{9,14},{10,... | collective-permute-start | bytes 786440 | tf_op jit(solution)/shard_map/ppermute | solution.py:344
  22.3 5.0 %collective-permute-done.2.refs_3_ = f32[2,64,512]{2,1,0:T(8,128)S(1)} collective-permute-done((f32[2,64,512]{2,1,0:T(8,128)}, f32[2,64,512]{2,1,0:T(8,128)S(1)}, u32[]{:S(2)}, u32[]{:S(2)}) %collective-permute-start.2) | collective-permute-done | bytes 262176 | tf_op jit(solution)/shard_map/ppermute | solution.py:344
  28.6 5.8 %collective-permute-start.6 = (f32[2,64,512]{2,1,0:T(8,128)}, f32[2,64,512]{2,1,0:T(8,128)S(1)}, u32[]{:S(2)}, u32[]{:S(2)}) collective-permute-start(f32[2,64,512]{2,1,0:T(8,128)} %get-tuple-element.34), channel_id=1, source_target_pairs={{0,7},{1,0},{2,1},{3,2},{4,3},{5,4},{6,5},{7,6},{8,15},{9,8},{10,9... | collective-permute-start | bytes 786440 | tf_op jit(solution)/shard_map/ppermute | solution.py:344
  34.3 4.0 %collective-permute-start.19 = (f32[896,128]{1,0:T(8,128)}, f32[896,128]{1,0:T(8,128)S(1)}, u32[]{:S(2)}, u32[]{:S(2)}) collective-permute-start(f32[896,128]{1,0:T(8,128)} %shard_map.66.refs_0_), channel_id=1, source_target_pairs={{0,24},{8,0},{16,8},{24,16},{32,56},{40,32},{48,40},{56,48},{64,88... | collective-permute-start | bytes 1376264 | tf_op jit(solution)/shard_map/ppermute | solution.py:345
  39.3 4.1 %shard_map.65 = (f32[4,264,128]{2,1,0:T(8,128)}, f32[4,264,128]{2,1,0:T(8,128)}, f32[4,264,128]{2,1,0:T(8,128)}, f32[4,264,128]{2,1,0:T(8,128)}) custom-call(s32[2]{0:T(128)} %pad_add_fusion.ids, s32[128]{0:T(128)} %anc.3, f32[16,512]{1,0:T(8,128)} %rain.1, f32[2,64,512]{2,1,0:T(8,128)} %get-tuple-element.27.refs_0_, f32[2,64,512]{2,1,0:T(8,128)} %copy-done.24, ...), custom_call_target="tpu_custom_call" | custom-call | tf_op jit(solution)/shard_map/pallas_call | solution.py:351
  43.4 2.0 %collective-permute-start.7 = (f32[4,264,128]{2,1,0:T(8,128)}, f32[4,264,128]{2,1,0:T(8,128)S(1)}, u32[]{:S(2)}, u32[]{:S(2)}) collective-permute-start(f32[4,264,128]{2,1,0:T(8,128)} %get-tuple-element.36), channel_id=1, source_target_pairs={{0,8},{8,16},{16,24},{24,0},{32,40},{40,48},{48,56},{56,32},{64,72... | collective-permute-start | bytes 1622024 | tf_op jit(solution)/shard_map/ppermute | solution.py:363
  45.4 3.6 %collective-permute-start.8 = (f32[4,264,128]{2,1,0:T(8,128)}, f32[4,264,128]{2,1,0:T(8,128)S(1)}, u32[]{:S(2)}, u32[]{:S(2)}) collective-permute-start(f32[4,264,128]{2,1,0:T(8,128)} %get-tuple-element.37), channel_id=1, source_target_pairs={{0,16},{8,24},{16,0},{24,8},{32,48},{40,56},{48,32},{56,40},{64,80... | collective-permute-start | bytes 1622024 | tf_op jit(solution)/shard_map/ppermute | solution.py:363
  49.0 2.8 %collective-permute-start.21 = (f32[896,128]{1,0:T(8,128)}, f32[896,128]{1,0:T(8,128)S(1)}, u32[]{:S(2)}, u32[]{:S(2)}) collective-permute-start(f32[896,128]{1,0:T(8,128)} %shard_map.66.refs_0_), channel_id=1, source_target_pairs={{0,96},{8,104},{16,48},{24,56},{32,0},{40,8},{48,80},{56,88},{64,3... | collective-permute-start | bytes 1376264 | tf_op jit(solution)/shard_map/ppermute | solution.py:346
  51.8 9.8 %collective-permute-done.21.refs_8_ = f32[896,128]{1,0:T(8,128)S(1)} collective-permute-done((f32[896,128]{1,0:T(8,128)}, f32[896,128]{1,0:T(8,128)S(1)}, u32[]{:S(2)}, u32[]{:S(2)}) %collective-permute-start.21) | collective-permute-done | bytes 458784 | tf_op jit(solution)/shard_map/ppermute | solution.py:346
  66.0 7.1 %collective-permute-done.8.refs_2_ = f32[4,264,128]{2,1,0:T(8,128)S(1)} collective-permute-done((f32[4,264,128]{2,1,0:T(8,128)}, f32[4,264,128]{2,1,0:T(8,128)S(1)}, u32[]{:S(2)}, u32[]{:S(2)}) %collective-permute-start.8) | collective-permute-done | bytes 540704 | tf_op jit(solution)/shard_map/ppermute | solution.py:363
  73.7 3.0 %collective-permute-done.23.refs_10_ = f32[896,128]{1,0:T(8,128)S(1)} collective-permute-done((f32[896,128]{1,0:T(8,128)S(1)}, f32[896,128]{1,0:T(8,128)S(1)}, u32[]{:S(2)}, u32[]{:S(2)}) %collective-permute-start.23) | collective-permute-done | bytes 458784 | tf_op jit(solution)/shard_map/ppermute | solution.py:346
  76.7 7.9 %collective-permute-done.25.refs_12_ = f32[896,128]{1,0:T(8,128)S(1)} collective-permute-done((f32[896,128]{1,0:T(8,128)S(1)}, f32[896,128]{1,0:T(8,128)S(1)}, u32[]{:S(2)}, u32[]{:S(2)}) %collective-permute-start.25) | collective-permute-done | bytes 458784 | tf_op jit(solution)/shard_map/ppermute | solution.py:346
  87.5 3.2 %collective-permute-start.13 = (f32[4,264,128]{2,1,0:T(8,128)S(1)}, f32[4,264,128]{2,1,0:T(8,128)S(1)}, u32[]{:S(2)}, u32[]{:S(2)}) collective-permute-start(f32[4,264,128]{2,1,0:T(8,128)S(1)} %collective-permute-done.9.refs_3_), channel_id=1, source_target_pairs={{0,96},{8,40},{16,48},{24,120},{32,0},{40,72},{48,80},{56,24},{64,... | collective-permute-start | bytes 1622024 | tf_op jit(solution)/shard_map/ppermute | solution.py:364
  93.0 12.3 %shard_map.67 = (bf16[16,512,256]{2,1,0:T(8,128)(2,1)}, bf16[16,512,256]{2,1,0:T(8,128)(2,1)}, f32[16,32,8,256]{3,2,1,0:T(8,128)}, f32[16,32,8,256]{3,2,1,0:T(8,...) custom-call(s32[2]{0:T(128)} %pad_add_fusion.ids, f32[896,128]{1,0:T(8,128)} %shard_map.66.refs_0_, ...), custom_call_target="tpu_custom_call" | custom-call | tf_op jit(solution)/shard_map/pallas_call | solution.py:366
  105.3 8.9 %collective-permute-done.12.refs_6_ = f32[4,264,128]{2,1,0:T(8,128)S(1)} collective-permute-done((f32[4,264,128]{2,1,0:T(8,128)S(1)}, f32[4,264,128]{2,1,0:T(8,128)S(1)}, u32[]{:S(2)}, u32[]{:S(2)}) %collective-permute-start.12) | collective-permute-done | bytes 540704 | tf_op jit(solution)/shard_map/ppermute | solution.py:364
  115.3 42.7 %shard_map.68 = (f32[256,512]{1,0:T(8,128)}, f32[256,512]{1,0:T(8,128)}, f32[256,512]{1,0:T(8,128)}, f32[256,512]{1,0:T(8,128)}) custom-call(s32[2]{0:T(128)} %pad_add_fusion.ids, f32[4,264,128]{2,1,0:T(8,128)} %get-tuple-element.35.refs_0_, f32[4,264,128]{2,1,0:T(8,128)} %copy-done, f32[4,264,128]{2,1,0:T(8,128)} %copy-done.1, f32[4,264,128]{2,1,0:T(8,128)} %copy-done.2, ...), custom_call_target="tpu_custom_call" | custom-call | tf_op jit(solution)/shard_map/pallas_call | solution.py:378
  161.6 22.3 %collective-permute-done.29.refs_1_ = f32[256,512]{1,0:T(8,128)S(1)} collective-permute-done((f32[256,512]{1,0:T(8,128)}, f32[256,512]{1,0:T(8,128)S(1)}, u32[]{:S(2)}, u32[]{:S(2)}) %collective-permute-start.29) | collective-permute-done | bytes 524320 | tf_op jit(solution)/shard_map/ppermute | solution.py:394
  185.3 3.7 %shard_map.69 = f32[64,16,512]{2,1,0:T(8,128)} custom-call(s32[2]{0:T(128)} %pad_add_fusion.ids, f32[256,512]{1,0:T(8,128)} %get-tuple-element.45.refs_0_, f32[256,512]{1,0:T(8,128)} %copy-done.7, f32[256,512]{1,0:T(8,128)} %copy-done.8, f32[256,512]{1,0:T(8,128)} %copy-done.9), custom_call_target="tpu_custom_call" | custom-call | tf_op jit(solution)/shard_map/pallas_call | solution.py:395
  (110 shorter events, 21.9 us)
Async XLA Ops:
  5.4 11.3 %collective-permute-start = (f32[2,64,512]{2,1,0:T(8,128)}, f32[2,64,512]{2,1,0:T(8,128)S(1)}, u32[]{:S(2)}, u32[]{:S(2)}) collective-permute-start(f32[2,64,512]{2,1,0:T(8,128)} %get-tuple-element.28), channel_id=1, source_target_pairs={{0,1},{1,2},{2,3},{3,4},{4,5},{5,6},{6,7},{7,0},{8,9},{9,10},{10,1... | collective-permute-start | bytes 786440 | tf_op jit(solution)/shard_map/ppermute | solution.py:344
  5.4 14.9 %collective-permute-start.1 = (f32[2,64,512]{2,1,0:T(8,128)}, f32[2,64,512]{2,1,0:T(8,128)S(1)}, u32[]{:S(2)}, u32[]{:S(2)}) collective-permute-start(f32[2,64,512]{2,1,0:T(8,128)} %get-tuple-element.29), channel_id=1, source_target_pairs={{0,2},{1,3},{2,4},{3,5},{4,6},{5,7},{6,0},{7,1},{8,10},{9,11},{10,... | collective-permute-start | bytes 786440 | tf_op jit(solution)/shard_map/ppermute | solution.py:344
  7.1 20.2 %collective-permute-start.2 = (f32[2,64,512]{2,1,0:T(8,128)}, f32[2,64,512]{2,1,0:T(8,128)S(1)}, u32[]{:S(2)}, u32[]{:S(2)}) collective-permute-start(f32[2,64,512]{2,1,0:T(8,128)} %get-tuple-element.30), channel_id=1, source_target_pairs={{0,3},{1,4},{2,5},{3,6},{4,7},{5,0},{6,1},{7,2},{8,11},{9,12},{10,... | collective-permute-start | bytes 786440 | tf_op jit(solution)/shard_map/ppermute | solution.py:344
  9.3 19.2 %collective-permute-start.3 = (f32[2,64,512]{2,1,0:T(8,128)}, f32[2,64,512]{2,1,0:T(8,128)S(1)}, u32[]{:S(2)}, u32[]{:S(2)}) collective-permute-start(f32[2,64,512]{2,1,0:T(8,128)} %get-tuple-element.31), channel_id=1, source_target_pairs={{0,4},{1,5},{2,6},{3,7},{4,0},{5,1},{6,2},{7,3},{8,12},{9,13},{10,... | collective-permute-start | bytes 786440 | tf_op jit(solution)/shard_map/ppermute | solution.py:344
  14.7 34.2 %collective-permute-start.15 = (f32[896,128]{1,0:T(8,128)}, f32[896,128]{1,0:T(8,128)S(1)}, u32[]{:S(2)}, u32[]{:S(2)}) collective-permute-start(f32[896,128]{1,0:T(8,128)} %shard_map.66.refs_0_), channel_id=1, source_target_pairs={{0,8},{8,16},{16,24},{24,0},{32,40},{40,48},{48,56},{56,32},{64,72... | collective-permute-start | bytes 1376264 | tf_op jit(solution)/shard_map/ppermute | solution.py:345
  16.6 35.1 %collective-permute-start.17 = (f32[896,128]{1,0:T(8,128)}, f32[896,128]{1,0:T(8,128)S(1)}, u32[]{:S(2)}, u32[]{:S(2)}) collective-permute-start(f32[896,128]{1,0:T(8,128)} %shard_map.66.refs_0_), channel_id=1, source_target_pairs={{0,16},{8,24},{16,0},{24,8},{32,48},{40,56},{48,32},{56,40},{64,80... | collective-permute-start | bytes 1376264 | tf_op jit(solution)/shard_map/ppermute | solution.py:345
  20.2 14.1 %collective-permute-start.4 = (f32[2,64,512]{2,1,0:T(8,128)}, f32[2,64,512]{2,1,0:T(8,128)S(1)}, u32[]{:S(2)}, u32[]{:S(2)}) collective-permute-start(f32[2,64,512]{2,1,0:T(8,128)} %get-tuple-element.32), channel_id=1, source_target_pairs={{0,5},{1,6},{2,7},{3,0},{4,1},{5,2},{6,3},{7,4},{8,13},{9,14},{10,... | collective-permute-start | bytes 786440 | tf_op jit(solution)/shard_map/ppermute | solution.py:344
  34.3 17.4 %collective-permute-start.19 = (f32[896,128]{1,0:T(8,128)}, f32[896,128]{1,0:T(8,128)S(1)}, u32[]{:S(2)}, u32[]{:S(2)}) collective-permute-start(f32[896,128]{1,0:T(8,128)} %shard_map.66.refs_0_), channel_id=1, source_target_pairs={{0,24},{8,0},{16,8},{24,16},{32,56},{40,32},{48,40},{56,48},{64,88... | collective-permute-start | bytes 1376264 | tf_op jit(solution)/shard_map/ppermute | solution.py:345
  43.4 20.9 %collective-permute-start.7 = (f32[4,264,128]{2,1,0:T(8,128)}, f32[4,264,128]{2,1,0:T(8,128)S(1)}, u32[]{:S(2)}, u32[]{:S(2)}) collective-permute-start(f32[4,264,128]{2,1,0:T(8,128)} %get-tuple-element.36), channel_id=1, source_target_pairs={{0,8},{8,16},{16,24},{24,0},{32,40},{40,48},{48,56},{56,32},{64,72... | collective-permute-start | bytes 1622024 | tf_op jit(solution)/shard_map/ppermute | solution.py:363
  45.4 27.8 %collective-permute-start.8 = (f32[4,264,128]{2,1,0:T(8,128)}, f32[4,264,128]{2,1,0:T(8,128)S(1)}, u32[]{:S(2)}, u32[]{:S(2)}) collective-permute-start(f32[4,264,128]{2,1,0:T(8,128)} %get-tuple-element.37), channel_id=1, source_target_pairs={{0,16},{8,24},{16,0},{24,8},{32,48},{40,56},{48,32},{56,40},{64,80... | collective-permute-start | bytes 1622024 | tf_op jit(solution)/shard_map/ppermute | solution.py:363
  49.0 12.7 %collective-permute-start.21 = (f32[896,128]{1,0:T(8,128)}, f32[896,128]{1,0:T(8,128)S(1)}, u32[]{:S(2)}, u32[]{:S(2)}) collective-permute-start(f32[896,128]{1,0:T(8,128)} %shard_map.66.refs_0_), channel_id=1, source_target_pairs={{0,96},{8,104},{16,48},{24,56},{32,0},{40,8},{48,80},{56,88},{64,3... | collective-permute-start | bytes 1376264 | tf_op jit(solution)/shard_map/ppermute | solution.py:346
  51.7 21.4 %collective-permute-start.9 = (f32[4,264,128]{2,1,0:T(8,128)}, f32[4,264,128]{2,1,0:T(8,128)S(1)}, u32[]{:S(2)}, u32[]{:S(2)}) collective-permute-start(f32[4,264,128]{2,1,0:T(8,128)} %get-tuple-element.38), channel_id=1, source_target_pairs={{0,24},{8,0},{16,8},{24,16},{32,56},{40,32},{48,40},{56,48},{64,88... | collective-permute-start | bytes 1622024 | tf_op jit(solution)/shard_map/ppermute | solution.py:363
  61.7 15.0 %collective-permute-start.23 = (f32[896,128]{1,0:T(8,128)S(1)}, f32[896,128]{1,0:T(8,128)S(1)}, u32[]{:S(2)}, u32[]{:S(2)}) collective-permute-start(f32[896,128]{1,0:T(8,128)S(1)} %collective-permute-done.15.refs_2_), channel_id=1, source_target_pairs={{0,32},{8,104},{16,112},{24,56},{32,64},{40,8},{48,16},{56,88},{64... | collective-permute-start | bytes 1376264 | tf_op jit(solution)/shard_map/ppermute | solution.py:346
  62.8 21.8 %collective-permute-start.25 = (f32[896,128]{1,0:T(8,128)S(1)}, f32[896,128]{1,0:T(8,128)S(1)}, u32[]{:S(2)}, u32[]{:S(2)}) collective-permute-start(f32[896,128]{1,0:T(8,128)S(1)} %collective-permute-done.17.refs_4_), channel_id=1, source_target_pairs={{0,32},{8,40},{16,112},{24,120},{32,64},{40,72},{48,16},{56,24},{6... | collective-permute-start | bytes 1376264 | tf_op jit(solution)/shard_map/ppermute | solution.py:346
  64.3 20.3 %collective-permute-start.27 = (f32[896,128]{1,0:T(8,128)S(1)}, f32[896,128]{1,0:T(8,128)S(1)}, u32[]{:S(2)}, u32[]{:S(2)}) collective-permute-start(f32[896,128]{1,0:T(8,128)S(1)} %collective-permute-done.19.refs_6_), channel_id=1, source_target_pairs={{0,96},{8,40},{16,48},{24,120},{32,0},{40,72},{48,80},{56,24},{64,... | collective-permute-start | bytes 1376264 | tf_op jit(solution)/shard_map/ppermute | solution.py:346
  73.2 11.9 %collective-permute-start.16 = (f32[896,128]{1,0:T(8,128)S(1)}, f32[896,128]{1,0:T(8,128)S(1)}, u32[]{:S(2)}, u32[]{:S(2)}) collective-permute-start(f32[896,128]{1,0:T(8,128)S(1)} %collective-permute-done.15.refs_2_), channel_id=1, source_target_pairs={{0,1},{1,0},{2,3},{3,2},{4,5},{5,4},{6,7},{7,6},{8,9},{9,8},{10,11... | collective-permute-start | bytes 1376264 | tf_op jit(solution)/shard_map/ppermute | solution.py:349
  73.2 12.0 %collective-permute-start.18 = (f32[896,128]{1,0:T(8,128)S(1)}, f32[896,128]{1,0:T(8,128)S(1)}, u32[]{:S(2)}, u32[]{:S(2)}) collective-permute-start(f32[896,128]{1,0:T(8,128)S(1)} %collective-permute-done.17.refs_4_), channel_id=1, source_target_pairs={{0,1},{1,0},{2,3},{3,2},{4,5},{5,4},{6,7},{7,6},{8,9},{9,8},{10,11... | collective-permute-start | bytes 1376264 | tf_op jit(solution)/shard_map/ppermute | solution.py:349
  85.2 20.0 %collective-permute-start.10 = (f32[4,264,128]{2,1,0:T(8,128)}, f32[4,264,128]{2,1,0:T(8,128)S(1)}, u32[]{:S(2)}, u32[]{:S(2)}) collective-permute-start(f32[4,264,128]{2,1,0:T(8,128)} %get-tuple-element.35.refs_0_), channel_id=1, source_target_pairs={{0,96},{8,104},{16,48},{24,56},{32,0},{40,8},{48,80},{56,88},{64,3... | collective-permute-start | bytes 1622024 | tf_op jit(solution)/shard_map/ppermute | solution.py:364
  87.0 18.2 %collective-permute-start.11 = (f32[4,264,128]{2,1,0:T(8,128)S(1)}, f32[4,264,128]{2,1,0:T(8,128)S(1)}, u32[]{:S(2)}, u32[]{:S(2)}) collective-permute-start(f32[4,264,128]{2,1,0:T(8,128)S(1)} %collective-permute-done.7.refs_1_), channel_id=1, source_target_pairs={{0,32},{8,104},{16,112},{24,56},{32,64},{40,8},{48,16},{56,88},{64... | collective-permute-start | bytes 1622024 | tf_op jit(solution)/shard_map/ppermute | solution.py:364
  87.4 26.8 %collective-permute-start.12 = (f32[4,264,128]{2,1,0:T(8,128)S(1)}, f32[4,264,128]{2,1,0:T(8,128)S(1)}, u32[]{:S(2)}, u32[]{:S(2)}) collective-permute-start(f32[4,264,128]{2,1,0:T(8,128)S(1)} %collective-permute-done.8.refs_2_), channel_id=1, source_target_pairs={{0,32},{8,40},{16,112},{24,120},{32,64},{40,72},{48,16},{56,24},{6... | collective-permute-start | bytes 1622024 | tf_op jit(solution)/shard_map/ppermute | solution.py:364
  87.5 26.7 %collective-permute-start.13 = (f32[4,264,128]{2,1,0:T(8,128)S(1)}, f32[4,264,128]{2,1,0:T(8,128)S(1)}, u32[]{:S(2)}, u32[]{:S(2)}) collective-permute-start(f32[4,264,128]{2,1,0:T(8,128)S(1)} %collective-permute-done.9.refs_3_), channel_id=1, source_target_pairs={{0,96},{8,40},{16,48},{24,120},{32,0},{40,72},{48,80},{56,24},{64,... | collective-permute-start | bytes 1622024 | tf_op jit(solution)/shard_map/ppermute | solution.py:364
  158.0 25.9 %collective-permute-start.29 = (f32[256,512]{1,0:T(8,128)}, f32[256,512]{1,0:T(8,128)S(1)}, u32[]{:S(2)}, u32[]{:S(2)}) collective-permute-start(f32[256,512]{1,0:T(8,128)} %get-tuple-element.46), channel_id=1, source_target_pairs={{0,8},{8,16},{16,24},{24,0},{32,40},{40,48},{48,56},{56,32},{64,72... | collective-permute-start | bytes 1572872 | tf_op jit(solution)/shard_map/ppermute | solution.py:394
  158.9 25.1 %collective-permute-start.30 = (f32[256,512]{1,0:T(8,128)}, f32[256,512]{1,0:T(8,128)S(1)}, u32[]{:S(2)}, u32[]{:S(2)}) collective-permute-start(f32[256,512]{1,0:T(8,128)} %get-tuple-element.47), channel_id=1, source_target_pairs={{0,16},{8,24},{16,0},{24,8},{32,48},{40,56},{48,32},{56,40},{64,80... | collective-permute-start | bytes 1572872 | tf_op jit(solution)/shard_map/ppermute | solution.py:394
  160.1 24.4 %collective-permute-start.31 = (f32[256,512]{1,0:T(8,128)}, f32[256,512]{1,0:T(8,128)S(1)}, u32[]{:S(2)}, u32[]{:S(2)}) collective-permute-start(f32[256,512]{1,0:T(8,128)} %get-tuple-element.48), channel_id=1, source_target_pairs={{0,24},{8,0},{16,8},{24,16},{32,56},{40,32},{48,40},{56,48},{64,88... | collective-permute-start | bytes 1572872 | tf_op jit(solution)/shard_map/ppermute | solution.py:394
  (39 other events, 483.8 us)

commit v2 on v1

v2 whole, which is shorter than its diff:
```python
import jax
import jax.numpy as jnp
from jax import lax
from jax.experimental import pallas as pl
from jax.experimental.pallas import tpu as pltpu
from jax.sharding import PartitionSpec as P

SUBSTEPS = 8
RING = 4
OWN = 4
LAYERS = 64
HALF = 32
SPAN = 128
WIDTH = 512
GROUP = 16
GROUPS = 8
PAIRS = 16
ROWS = HALF * 8
MSG = 2 * (3 * SPAN + LAYERS)
F32 = jnp.float32
BF16 = jnp.bfloat16


def params(mib):
    return pltpu.CompilerParams(vmem_limit_bytes=mib * 1024 * 1024)


def shape(dims, dtype=F32):
    return jax.ShapeDtypeStruct(dims, dtype)


SMEM = pl.BlockSpec(memory_space=pltpu.SMEM)
VMEM = pl.BlockSpec(memory_space=pltpu.VMEM)
ANY = pl.BlockSpec(memory_space=pl.ANY)


def z_pairs(s):
    return [(4 * x + z, 4 * x + (z + s) % 4) for x in range(4) for z in range(4)]


def x_pairs(s):
    out = []
    for x in range(4):
        for z in range(4):
            step = -1 if (z - s) % 4 < 2 else 1
            out.append((4 * x + z, 4 * ((x + step) % 4) + z))
    return out


def core_pairs():
    return [(g, g ^ 1) for g in range(GROUPS)]


def send_kernel(ids, anc, moist, out, held, ready, sems, out_sems):
    copies = []
    for t in range(WIDTH // SPAN):
        copies.append(pltpu.make_async_copy(moist.at[:, pl.ds(t * SPAN, SPAN)], held.at[t], sems.at[t]))
        copies[-1].start()
    mine = ids[1]
    flip = 7 - lax.broadcasted_iota(jnp.int32, (8, SPAN), 0)
    picks = []
    for target in range(GROUPS):
        low = jnp.int32(GROUP)
        high = jnp.int32(-1)
        for i in range(GROUP):
            v = anc[target * GROUP + i] - mine * GROUP
            inside = (v >= 0) & (v < GROUP)
            low = jnp.where(inside, jnp.minimum(low, v), low)
            high = jnp.where(inside, jnp.maximum(high, v), high)
        picks.append((jnp.minimum(low, GROUP - 1), jnp.maximum(high, 0)))
    for c in copies:
        c.wait()
    leave = []
    for r in range(GROUPS):
        for j in range(2):
            for t in range(WIDTH // SPAN):
                lanes = slice(t * SPAN, (t + 1) * SPAN)
                rows = held[t, pl.ds(picks[r][j], LAYERS, stride=GROUP), :]
                ready[2 * r + j, :HALF, lanes] = rows[:HALF]
                for q in range(HALF // 8):
                    part = rows[LAYERS - 8 * (q + 1):LAYERS - 8 * q]
                    ready[2 * r + j, HALF + 8 * q:HALF + 8 * (q + 1), lanes] = jnp.take_along_axis(part, flip, axis=0)
        span = pl.ds(2 * r, 2)
        leave.append(pltpu.make_async_copy(ready.at[span], out.at[span], out_sems.at[r]))
        leave[-1].start()
    for c in leave:
        c.wait()


def pack_kernel(ids, anc, rain, *refs):
    arrived, outs = refs[0], refs[1:1 + RING]
    slots, ready, least, sem, out_sems = refs[1 + RING:]
    fetch = pltpu.make_async_copy(arrived, slots, sem)
    fetch.start()
    z = lax.rem(ids[0], RING)
    mine = ids[1]
    for g in range(GROUPS):
        least[g] = jnp.int32(1 << 20)
    for i in range(GROUP):
        v = anc[mine * GROUP + i]
        g = v // GROUP
        least[g] = jnp.minimum(least[g], v)
    fetch.wait()
    upper = lax.broadcasted_iota(jnp.int32, (8, WIDTH), 0) < 4
    leave = []
    for s in list(range(1, RING)) + [0]:
        owner = lax.rem(z + s, RING)
        for p in range(OWN):
            v = anc[mine * GROUP + owner * OWN + p]
            g = v // GROUP
            slot = 2 * g + jnp.where(v > least[g], 1, 0)
            for t in range(WIDTH // SPAN):
                lanes = slice(t * SPAN, (t + 1) * SPAN)
                for d in range(2):
                    ready[s, t, pl.ds(4 * d + p, HALF, stride=8), :] = slots[slot, d * HALF:(d + 1) * HALF, lanes]
        own_rain = rain[pl.ds(pl.multiple_of(owner // 2 * 8, 8), 8), :]
        own_rain = jnp.where(lax.rem(owner, 2) == 1, pltpu.roll(own_rain, 4, 0), own_rain)
        own_rain = jnp.where(upper, own_rain, 0.0)
        for t in range(WIDTH // SPAN):
            ready[s, t, ROWS:, :] = own_rain[:, t * SPAN:(t + 1) * SPAN]
        leave.append(pltpu.make_async_copy(ready.at[s], outs[s], out_sems.at[s]))
        leave[-1].start()
    for c in leave:
        c.wait()


def coeff_kernel(ids, adj, cond, vert, after, out):
    tile = ids[0]
    core = lax.rem(ids[1], 2)
    eye = (lax.broadcasted_iota(jnp.int32, (SPAN, SPAN), 0) == lax.broadcasted_iota(jnp.int32, (SPAN, SPAN), 1)).astype(F32)
    links = adj[...]
    block = lax.broadcasted_iota(jnp.int32, links.shape, 1)
    place = lax.broadcasted_iota(jnp.int32, links.shape, 0)
    other = jnp.where(links == block, 0.0, 1.0).astype(F32)
    for i in range(2):
        local = 2 * core + i
        b = RING * tile + local
        prev = jnp.sum(jnp.where((block == b) & (place == 1), other, 0.0))
        after = jnp.sum(jnp.where((block == b) & (place == 2), other, 0.0))
        own, first, second = cond[local, 0], cond[local, 1], cond[local, 2]
        base = i * (3 * SPAN + LAYERS)
        out[base:base + SPAN, :] = (first * prev).T
        out[base + SPAN:base + 2 * SPAN, :] = (own + first * (1.0 - prev) + second * (1.0 - after)).T + eye
        out[base + 2 * SPAN:base + 3 * SPAN, :] = (second * after).T
        lanes = pl.ds(pl.multiple_of(local * SPAN, SPAN), SPAN)
        out[base + 3 * SPAN:base + 3 * SPAN + LAYERS - 1, :] = vert[:, lanes]
        out[base + 3 * SPAN + LAYERS - 1:base + 3 * SPAN + LAYERS, :] = jnp.zeros((1, SPAN), F32)


def window_base(z, s, halo):
    t = lax.rem(z - s + RING, RING)
    if halo:
        return jnp.where(t < 2, 24 + 4 * t, 4 * t - 8)
    return 8 + 4 * t


def expand_kernel(ids, mine, other, w_ref, c_ref, vs):
    z = lax.rem(ids[0], RING)
    core = lax.rem(ids[1], 2)
    for at in range(2 * RING):
        base = window_base(z, at % RING, at >= RING) // 2
        for msg, half in ((mine, core), (other, 1 - core)):
            k = base + half
            for i in range(2):
                row = i * (3 * SPAN + LAYERS)
                cols = slice(i * SPAN, (i + 1) * SPAN)
                rows = slice(i * SPAN, (i + 3) * SPAN)
                w = msg[at, row:row + 3 * SPAN, :]
                hi = w.astype(BF16)
                w_ref[k, 0, rows, cols] = hi
                w_ref[k, 1, rows, cols] = (w - hi.astype(F32)).astype(BF16)
                empty = slice(3 * SPAN, 4 * SPAN) if i == 0 else slice(0, SPAN)
                w_ref[k, 0, empty, cols] = jnp.zeros((SPAN, SPAN), BF16)
                w_ref[k, 1, empty, cols] = jnp.zeros((SPAN, SPAN), BF16)
                vs[k, :, i * SPAN:(i + 1) * SPAN] = msg[at, row + 3 * SPAN:row + 3 * SPAN + LAYERS, :]
    first = lax.broadcasted_iota(jnp.int32, (2, 2 * SPAN), 0) == 0
    group = 8

    def chunk(c, _):
        e_prev = [jnp.zeros((2, 2 * SPAN), F32)] * group
        for l in range(HALF):
            for q in range(group):
                k = c * group + q
                a_low = vs[k, LAYERS - 1 - l:LAYERS - l, :]
                a_top = vs[k, l - 1:l, :] if l else jnp.zeros((1, 2 * SPAN), F32)
                a = jnp.where(first, a_top, a_low)
                b = jnp.where(first, vs[k, l:l + 1, :], vs[k, LAYERS - 2 - l:LAYERS - 1 - l, :])
                inv = 1.0 / (1.0 + a + b - a * e_prev[q])
                e = b * inv
                c_ref[k, 2 * l:2 * l + 2] = inv
                c_ref[k, 2 * (HALF + l):2 * (HALF + l) + 2] = a * inv
                c_ref[k, 2 * (2 * HALF + l):2 * (2 * HALF + l) + 2] = e
                e_prev[q] = e
        for q in range(group):
            e = e_prev[q]
            both = 1.0 / (1.0 - e[0:1] * e[1:2])
            c_ref[c * group + q, 6 * HALF:6 * HALF + 8] = jnp.broadcast_to(both, (8, 2 * SPAN))
        return 0

    lax.fori_loop(0, PAIRS // group, chunk, 0)


def step_kernel(ids, *refs):
    ins, w, packed, outs = refs[:8], refs[8], refs[9], refs[10:14]
    x0, x1, rain, r_a, r_b, r_c, r_d, final, c, sems = refs[14:]
    z = lax.rem(ids[0], RING)
    upper = lax.broadcasted_iota(jnp.int32, (8, 2 * SPAN), 0) < 4

    def spread(k):
        for l in range(3 * HALF):
            c[k, l] = jnp.where(upper, packed[k, 2 * l:2 * l + 1, :], packed[k, 2 * l + 1:2 * l + 2, :])
        c[k, 3 * HALF] = packed[k, 6 * HALF:6 * HALF + 8, :]

    pad = jnp.zeros((2 * ROWS, SPAN), BF16)
    x0[:, :SPAN] = pad
    x0[:, (2 * PAIRS + 1) * SPAN:] = pad
    at = 0
    for halo in (False, True):
        for s in range(RING):
            base = window_base(z, s, halo)
            for t in range(WIDTH // SPAN):
                lanes = pl.ds(pl.multiple_of((base + 1 + t) * SPAN, SPAN), SPAN)
                v = ins[at][t, :ROWS, :]
                hi = v.astype(BF16)
                x0[:ROWS, lanes] = hi
                x0[ROWS:, lanes] = (v - hi.astype(F32)).astype(BF16)
                rain[:, pl.ds(pl.multiple_of((base + t) * SPAN, SPAN), SPAN)] = ins[at][t, ROWS:, :]
            at += 1

    def product(k, x, r):
        lanes = pl.ds(pl.multiple_of(k * 2 * SPAN, 2 * SPAN), 4 * SPAN)
        both = jnp.dot(x[:, lanes], w[k, 0], preferred_element_type=F32)
        acc = jnp.dot(x[:ROWS, lanes], w[k, 1], preferred_element_type=F32)
        acc = both[:ROWS] + (both[ROWS:] + acc)
        r[...] = acc
        r[:8, :] = acc[:8, :] + rain[:, pl.ds(pl.multiple_of(k * 2 * SPAN, 2 * SPAN), 2 * SPAN)]

    def forward(k, rs):
        ys = [r[:8, :] * c[k + q, 0] for q, r in enumerate(rs)]
        for q, r in enumerate(rs):
            r[:8, :] = ys[q]
        for l in range(1, HALF):
            for q, r in enumerate(rs):
                ys[q] = r[8 * l:8 * l + 8, :] * c[k + q, l] + c[k + q, HALF + l] * ys[q]
                if l < HALF - 1:
                    r[8 * l:8 * l + 8, :] = ys[q]
        return ys

    def backward(k, rs, ys, put):
        xs = [(y + c[k + q, 3 * HALF - 1] * pltpu.roll(y, 4, 0)) * c[k + q, 3 * HALF] for q, y in enumerate(ys)]
        later = list(xs)
        for l in range(HALF - 2, -1, -1):
            for q, r in enumerate(rs):
                xs[q] = r[8 * l:8 * l + 8, :] + c[k + q, 2 * HALF + l] * xs[q]
                if l % 2:
                    later[q] = xs[q]
                else:
                    put(k + q, l // 2, jnp.concatenate([xs[q], later[q]], axis=0))

    for step in range(1, SUBSTEPS + 1):
        src, dst = (x0, x1) if step % 2 else (x1, x0)
        first, last = step // 2, PAIRS - step // 2
        groups = (last - first) // 2

        def put(k, m, v, dst=dst):
            lanes = pl.ds(pl.multiple_of((2 * k + 1) * SPAN, SPAN), 2 * SPAN)
            hi = v.astype(BF16)
            dst[16 * m:16 * m + 16, lanes] = hi
            dst[ROWS + 16 * m:ROWS + 16 * m + 16, lanes] = (v - hi.astype(F32)).astype(BF16)

        def put_final(k, m, v):
            t = (k - 4) // 2
            s = lax.rem(t - z + RING, RING)
            lanes = pl.ds(pl.multiple_of(lax.rem(k, 2) * 2 * SPAN, 2 * SPAN), 2 * SPAN)
            final[s, 16 * m:16 * m + 16, lanes] = v

        write = put_final if step == SUBSTEPS else put

        def one(k, r, src=src):
            product(k, src, r)

        def ready(k, n, step=step):
            if step == 1:
                for q in range(n):
                    spread(k + q)

        near, far = (r_a, r_b), (r_c, r_d)
        one(first, r_a)
        one(first + 1, r_b)

        def body(i, _, first=first, one=one, ready=ready, write=write):
            k = first + 4 * i
            for at, (old, new) in ((k, (near, far)), (k + 2, (far, near))):
                ready(at, 2)
                one(at + 2, new[0])
                ys = forward(at, old)
                one(at + 3, new[1])
                backward(at, old, ys, write)
            return 0

        lax.fori_loop(0, (groups - 1) // 2, body, 0)
        rest = [(last - 2, near)]
        if groups % 2 == 0:
            ready(last - 4, 2)
            one(last - 2, r_c)
            ys = forward(last - 4, near)
            one(last - 1, r_d)
            backward(last - 4, near, ys, write)
            rest = [(last - 2, far)]
        for at, old in rest:
            ready(at, 2)
            backward(at, old, forward(at, old), write)

    copies = [pltpu.make_async_copy(final.at[s], outs[s], sems.at[s]) for s in range(RING)]
    for c_out in copies:
        c_out.start()
    for c_out in copies:
        c_out.wait()


def join_kernel(ids, *refs):
    ins, out, held, ready, sems, out_sems = refs[:RING], *refs[RING:]
    z = lax.rem(ids[0], RING)
    copies = []
    for s in range(RING):
        copies.append(pltpu.make_async_copy(ins[s], held.at[lax.rem(z - s + RING, RING)], sems.at[s]))
        copies[-1].start()
    for c in copies:
        c.wait()
    upper = lax.broadcasted_iota(jnp.int32, (8, WIDTH), 0) < 4
    parts = 4
    depth = HALF // parts
    leave = []
    for part in range(parts):
        for l in range(part * depth, (part + 1) * depth):
            for h in range(2):
                a = held[2 * h, 8 * l:8 * l + 8, :]
                b = held[2 * h + 1, 8 * l:8 * l + 8, :]
                ready[l, 8 * h:8 * h + 8, :] = jnp.where(upper, a, pltpu.roll(b, 4, 0))
                ready[LAYERS - 1 - l, 8 * h:8 * h + 8, :] = jnp.where(upper, pltpu.roll(a, 4, 0), b)
        for i, low in enumerate((part * depth, LAYERS - (part + 1) * depth)):
            span = pl.ds(low, depth)
            leave.append(pltpu.make_async_copy(ready.at[span], out.at[span], out_sems.at[2 * part + i]))
            leave[-1].start()
    for c in leave:
        c.wait()


def shards(moisture, ancestors, adjacency, conductance, vertical, rainfall):
    ids = jnp.stack([lax.axis_index("tile"), lax.axis_index("dom")]).astype(jnp.int32)

    flat = moisture.reshape(LAYERS * GROUP, WIDTH)
    sent = pl.pallas_call(
        send_kernel,
        out_shape=shape((2 * GROUPS, LAYERS, WIDTH)),
        in_specs=[SMEM, SMEM, ANY],
        out_specs=ANY,
        scratch_shapes=[
            pltpu.VMEM((WIDTH // SPAN, LAYERS * GROUP, SPAN), F32),
            pltpu.VMEM((2 * GROUPS, LAYERS, WIDTH), F32),
            pltpu.SemaphoreType.DMA((WIDTH // SPAN,)),
            pltpu.SemaphoreType.DMA((GROUPS,)),
        ],
        compiler_params=params(12),
    )(ids, ancestors, flat)
    coeff = pl.pallas_call(
        coeff_kernel,
        out_shape=shape((MSG, SPAN)),
        in_specs=[SMEM, VMEM, VMEM, VMEM, ANY],
        out_specs=VMEM,
        compiler_params=params(8),
    )(ids, adjacency.T, conductance, vertical, sent)
    c_far = lax.ppermute(coeff, "tile", x_pairs(0))
    c_near = [coeff] + [lax.ppermute(coeff, "tile", z_pairs(s)) for s in range(1, RING)]
    c_far = [c_far] + [lax.ppermute(c_far, "tile", z_pairs(s)) for s in range(1, RING)]
    c_mine = jnp.stack(c_near + c_far)
    got = lax.all_to_all(sent, "dom", split_axis=0, concat_axis=0, tiled=True)

    mine = pl.pallas_call(
        pack_kernel,
        out_shape=[shape((WIDTH // SPAN, ROWS + 8, SPAN))] * RING,
        in_specs=[SMEM, SMEM, VMEM, ANY],
        out_specs=[ANY] * RING,
        scratch_shapes=[
            pltpu.VMEM((2 * GROUPS, LAYERS, WIDTH), F32),
            pltpu.VMEM((RING, WIDTH // SPAN, ROWS + 8, SPAN), F32),
            pltpu.SMEM((GROUPS,), jnp.int32),
            pltpu.SemaphoreType.DMA,
            pltpu.SemaphoreType.DMA((RING,)),
        ],
        compiler_params=params(12),
    )(ids, ancestors, rainfall, got)
    ring = [mine[0]] + [lax.ppermute(mine[s], "tile", z_pairs(s)) for s in range(1, RING)]
    c_mine, *ring = lax.optimization_barrier((c_mine, *ring))
    c_other = lax.ppermute(c_mine, "dom", core_pairs())
    side = [lax.ppermute(ring[s], "tile", x_pairs(s)) for s in range(RING)]

    coefs = pl.pallas_call(
        expand_kernel,
        out_shape=[shape((PAIRS, 2, 4 * SPAN, 2 * SPAN), BF16), shape((PAIRS, 6 * HALF + 8, 2 * SPAN))],
        in_specs=[SMEM, VMEM, VMEM],
        out_specs=[VMEM] * 2,
        scratch_shapes=[pltpu.VMEM((PAIRS, LAYERS, 2 * SPAN), F32)],
        compiler_params=params(26),
    )(ids, c_mine, c_other)

    back = pl.pallas_call(
        step_kernel,
        out_shape=[shape((ROWS, WIDTH))] * RING,
        in_specs=[SMEM] + [VMEM] * 10,
        out_specs=[ANY] * RING,
        scratch_shapes=[pltpu.VMEM((2 * ROWS, (2 * PAIRS + 2) * SPAN), BF16)] * 2
        + [pltpu.VMEM((8, 2 * PAIRS * SPAN), F32)]
        + [pltpu.VMEM((ROWS, 2 * SPAN), F32)] * 4
        + [
            pltpu.VMEM((RING, ROWS, WIDTH), F32),
            pltpu.VMEM((PAIRS, 3 * HALF + 1, 8, 2 * SPAN), F32),
            pltpu.SemaphoreType.DMA((RING,)),
        ],
        compiler_params=params(46),
    )(ids, *ring, *side, *coefs)

    home = [back[0]] + [lax.ppermute(back[s], "tile", z_pairs(s)) for s in range(1, RING)]
    return pl.pallas_call(
        join_kernel,
        out_shape=shape((LAYERS, GROUP, WIDTH)),
        in_specs=[SMEM] + [ANY] * RING,
        out_specs=ANY,
        scratch_shapes=[
            pltpu.VMEM((RING, ROWS, WIDTH), F32),
            pltpu.VMEM((LAYERS, GROUP, WIDTH), F32),
            pltpu.SemaphoreType.DMA((RING,)),
            pltpu.SemaphoreType.DMA((8,)),
        ],
        compiler_params=params(14),
    )(ids, *home)


def solution(mesh):
    in_specs = (
        P(None, "dom", "tile"),
        P(),
        P(),
        P("tile", None, None, None),
        P(None, "tile"),
        P("dom", "tile"),
    )
    out_specs = P(None, "dom", "tile")
    return jax.shard_map(shards, mesh=mesh, in_specs=in_specs, out_specs=out_specs, check_vma=False)
```

time: 191 us -> 172 us (0.901)
  Pallas kernels: 69.8 us -> 45.2 us
  local copies, waits for them, and re-layouts: 4.46 us -> 16.7 us
  starting transfers between devices: 46.4 us -> 34.3 us
  waiting for transfers between devices: 67.6 us -> 74.8 us
    ppermute x19 -> x5, waiting for transfers between devices: 28.6 us -> 15.9 us  [the longest x3 10.1 us: shards(): lax.ppermute(c_far, 'tile', z_pairs(s))]
    ppermute x19 -> x5, starting transfers between devices: 22.1 us -> 10.3 us  [the longest x3 7.44 us: shards(): lax.ppermute(c_far, 'tile', z_pairs(s))]
    ppermute x3, waiting for transfers between devices: 7.13 us -> 18.7 us  [shards(): lax.ppermute(mine[s], 'tile', z_pairs(s))]
    unnamed x63 -> x25, local copies, waits for them, and re-layouts: 4.46 us -> 14.9 us
    pallas_call x1, Pallas kernels: 42.7 us -> 32.4 us  [shards(): pl.pallas_call(step_kernel, out_shape=[shape((ROWS, WIDTH))] * RING, in_s...]
    pallas_call x2, Pallas kernels: 17.1 us -> 8.28 us  [the longest x1 5.09 us: shards(): pl.pallas_call(expand_kernel, out_shape=[shape((PAIRS, 2, 4 * SPAN, 2 * S...]
    ppermute x3, waiting for transfers between devices: 0.01 us -> 6.75 us  [shards(): lax.ppermute(coeff, 'tile', z_pairs(s))]
    all_to_all x0 -> x1, starting transfers between devices: none -> 4.57 us  [shards(): got = lax.all_to_all(sent, 'dom', split_axis=0, concat_axis=0, tiled=True)]
  transfers between devices with their start and end apart: 32 -> 19, of which waited for: 11 -> 11; matrix products, arithmetic and copies ran while one was open for 1% -> 6% of each run, Pallas kernels for 10% -> 4%
where the time goes in v2:
time: 172 us; the launch traced here: 171 us
  waiting for transfers between devices  74.8 us (43%)
  Pallas kernels  45.2 us (26%)
  starting transfers between devices  34.3 us (20%)
  local copies, waits for them, and re-layouts  16.7 us (10%)
    pallas_call x1, Pallas kernels, shards(): pl.pallas_call(step_kernel, out_shape=[shape((ROWS, WIDTH))] * RING, in_s...  32.4 us
    ppermute x3, waiting for transfers between devices, shards(): lax.ppermute(back[s], 'tile', z_pairs(s))  21.2 us
    ppermute x3, waiting for transfers between devices, shards(): lax.ppermute(mine[s], 'tile', z_pairs(s))  18.7 us
    unnamed x25, local copies, waits for them, and re-layouts  14.9 us
    ppermute x4, waiting for transfers between devices, shards(): side = [lax.ppermute(ring[s], 'tile', x_pairs(s)) for s in range(RING)]  12.3 us
    ppermute x3, waiting for transfers between devices, shards(): lax.ppermute(c_far, 'tile', z_pairs(s))  10.1 us
    ppermute x3, starting transfers between devices, shards(): lax.ppermute(c_far, 'tile', z_pairs(s))  7.44 us
    ppermute x3, waiting for transfers between devices, shards(): lax.ppermute(coeff, 'tile', z_pairs(s))  6.75 us
  transfers between devices with their start and end apart: 19, of which 11 were waited for; matrix products, arithmetic and copies ran while one was open for 6% of the time, Pallas kernels for 4%

profile of v2, /device:TPU:0, one launch (start us, length us, event | category | flops | bytes accessed | tf_op | source)
XLA Modules:
  0.0 171.5 jit_solution(1406024084636983015)
XLA Ops:
  2.3 3.2 %shard_map.64.after = f32[16,64,512]{2,1,0:T(8,128)} custom-call(s32[2]{0:T(128)S(1)} %pad_add_fusion.ids, s32[128]{0:T(128)S(1)} %copy-done.7, f32[1024,512]{1,0:T(8,128)S(1)} %bitcast.20), custom_call_target="tpu_custom_call" | custom-call | tf_op jit(solution)/shard_map/pallas_call | solution.py:353
  5.5 4.6 %all-to-all-start = ((f32[16,64,512]{2,1,0:T(8,128)}), f32[16,64,512]{2,1,0:T(8,128)S(1)}, u32[]{:S(2)}, u32[]{:S(2)}) async-start(f32[16,64,512]{2,1,0:T(8,128)} %shard_map.64.after), calls=%async_computation | async-start | bytes 4194304 | tf_op jit(solution)/shard_map/all_to_all | solution.py:377
  11.0 2.8 %collective-permute-start.3 = (f32[896,128]{1,0:T(8,128)S(1)}, f32[896,128]{1,0:T(8,128)S(1)}, u32[]{:S(2)}, u32[]{:S(2)}) collective-permute-start(f32[896,128]{1,0:T(8,128)S(1)} %shard_map.65), channel_id=1, source_target_pairs={{0,96},{8,104},{16,48},{24,56},{32,0},{40,8},{48,80},{56,88},{64,3... | collective-permute-start | bytes 1376264 | tf_op jit(solution)/shard_map/ppermute | solution.py:373
  13.8 1.9 %collective-permute-start = (f32[896,128]{1,0:T(8,128)S(1)}, f32[896,128]{1,0:T(8,128)S(1)}, u32[]{:S(2)}, u32[]{:S(2)}) collective-permute-start(f32[896,128]{1,0:T(8,128)S(1)} %shard_map.65), channel_id=1, source_target_pairs={{0,8},{8,16},{16,24},{24,0},{32,40},{40,48},{48,56},{56,32},{64,72... | collective-permute-start | bytes 1376264 | tf_op jit(solution)/shard_map/ppermute | solution.py:374
  15.7 2.3 %collective-permute-start.1 = (f32[896,128]{1,0:T(8,128)S(1)}, f32[896,128]{1,0:T(8,128)S(1)}, u32[]{:S(2)}, u32[]{:S(2)}) collective-permute-start(f32[896,128]{1,0:T(8,128)S(1)} %shard_map.65), channel_id=1, source_target_pairs={{0,16},{8,24},{16,0},{24,8},{32,48},{40,56},{48,32},{56,40},{64,80... | collective-permute-start | bytes 1376264 | tf_op jit(solution)/shard_map/ppermute | solution.py:374
  19.9 4.4 %collective-permute-done.3 = f32[896,128]{1,0:T(8,128)S(1)} collective-permute-done((f32[896,128]{1,0:T(8,128)S(1)}, f32[896,128]{1,0:T(8,128)S(1)}, u32[]{:S(2)}, u32[]{:S(2)}) %collective-permute-start.3) | collective-permute-done | bytes 458784 | tf_op jit(solution)/shard_map/ppermute | solution.py:373
  24.2 1.9 %collective-permute-start.4 = (f32[896,128]{1,0:T(8,128)S(1)}, f32[896,128]{1,0:T(8,128)}, u32[]{:S(2)}, u32[]{:S(2)}) collective-permute-start(f32[896,128]{1,0:T(8,128)S(1)} %collective-permute-done.3), channel_id=1, source_target_pairs={{0,8},{8,16},{16,24},{24,0},{32,40},{40,48},{48,56},{56,32},{64,72... | collective-permute-start | bytes 1376264 | tf_op jit(solution)/shard_map/ppermute | solution.py:375
  26.2 4.5 %collective-permute-start.5 = (f32[896,128]{1,0:T(8,128)S(1)}, f32[896,128]{1,0:T(8,128)}, u32[]{:S(2)}, u32[]{:S(2)}) collective-permute-start(f32[896,128]{1,0:T(8,128)S(1)} %collective-permute-done.3), channel_id=1, source_target_pairs={{0,16},{8,24},{16,0},{24,8},{32,48},{40,56},{48,32},{56,40},{64,80... | collective-permute-start | bytes 1376264 | tf_op jit(solution)/shard_map/ppermute | solution.py:375
  32.5 6.7 %collective-permute-done.1 = f32[896,128]{1,0:T(8,128)S(1)} collective-permute-done((f32[896,128]{1,0:T(8,128)S(1)}, f32[896,128]{1,0:T(8,128)S(1)}, u32[]{:S(2)}, u32[]{:S(2)}) %collective-permute-start.1) | collective-permute-done | bytes 458784 | tf_op jit(solution)/shard_map/ppermute | solution.py:374
  44.5 2.1 %collective-permute-start.8 = (f32[4,264,128]{2,1,0:T(8,128)S(1)}, f32[4,264,128]{2,1,0:T(8,128)S(1)}, u32[]{:S(2)}, u32[]{:S(2)}) collective-permute-start(f32[4,264,128]{2,1,0:T(8,128)S(1)} %get-tuple-element.22), channel_id=1, source_target_pairs={{0,16},{8,24},{16,0},{24,8},{32,48},{40,56},{48,32},{56,40},{64,80... | collective-permute-start | bytes 1622024 | tf_op jit(solution)/shard_map/ppermute | solution.py:393
  46.6 2.6 %collective-permute-done.4 = f32[896,128]{1,0:T(8,128)} collective-permute-done((f32[896,128]{1,0:T(8,128)S(1)}, f32[896,128]{1,0:T(8,128)}, u32[]{:S(2)}, u32[]{:S(2)}) %collective-permute-start.4) | collective-permute-done | bytes 458784 | tf_op jit(solution)/shard_map/ppermute | solution.py:375
  49.7 1.8 %bitcast_dynamic-update-slice_fusion.2 = f32[8,896,128]{2,1,0:T(8,128)} fusion(f32[8,896,128]{2,1,0:T(8,128)} %bitcast_dynamic-update-slice_fusion.3, f32[896,128]{1,0:T(8,128)} %collective-permute-done.4), kind=kLoop, calls=%fused_computation.2 | loop fusion | bytes 917504
  51.6 7.5 %collective-permute-done.5 = f32[896,128]{1,0:T(8,128)} collective-permute-done((f32[896,128]{1,0:T(8,128)S(1)}, f32[896,128]{1,0:T(8,128)}, u32[]{:S(2)}, u32[]{:S(2)}) %collective-permute-start.5) | collective-permute-done | bytes 458784 | tf_op jit(solution)/shard_map/ppermute | solution.py:375
  60.9 1.8 %bitcast_dynamic-update-slice_fusion.mine = f32[8,896,128]{2,1,0:T(8,128)} fusion(f32[8,896,128]{2,1,0:T(8,128)} %bitcast_dynamic-update-slice_fusion.1, f32[896,128]{1,0:T(8,128)} %collective-permute-done.6), kind=kLoop, calls=%fused_computation | loop fusion | bytes 917504 | tf_op jit(solution)/shard_map/stack | solution.py:376
  62.7 7.7 %collective-permute-done.7.refs_1_ = f32[4,264,128]{2,1,0:T(8,128)S(1)} collective-permute-done((f32[4,264,128]{2,1,0:T(8,128)S(1)}, f32[4,264,128]{2,1,0:T(8,128)S(1)}, u32[]{:S(2)}, u32[]{:S(2)}) %collective-permute-start.7) | collective-permute-done | bytes 540704 | tf_op jit(solution)/shard_map/ppermute | solution.py:393
  70.4 11.0 %collective-permute-done.8.refs_2_ = f32[4,264,128]{2,1,0:T(8,128)S(1)} collective-permute-done((f32[4,264,128]{2,1,0:T(8,128)S(1)}, f32[4,264,128]{2,1,0:T(8,128)S(1)}, u32[]{:S(2)}, u32[]{:S(2)}) %collective-permute-start.8) | collective-permute-done | bytes 540704 | tf_op jit(solution)/shard_map/ppermute | solution.py:393
  88.0 5.1 %shard_map.67 = (bf16[16,2,512,256]{3,2,1,0:T(8,128)(2,1)S(1)}, f32[16,200,256]{2,1,0:T(8,128)S(1)}) custom-call(s32[2]{0:T(128)S(1)} %pad_add_fusion.ids, f32[8,896,128]{2,1,0:T(8,128)} %bitcast_dynamic-update-slice_fusion.mine, f32[8,896,128]{2,1,0:T(8,128)S(1)} %collective-permute-done.14.other), custom_call_target="tpu_custom_call" | custom-call | tf_op jit(solution)/shard_map/pallas_call | solution.py:398
  93.1 3.3 %copy-done = bf16[16,2,512,256]{3,2,1,0:T(8,128)(2,1)} copy-done((bf16[16,2,512,256]{3,2,1,0:T(8,128)(2,1)}, bf16[16,2,512,256]{3,2,1,0:T(8,128)(2,1)S(1)}, u32[]{:S(2)}) %copy-start) | copy-done | bytes 8388632
  99.5 10.9 %collective-permute-done.12.refs_6_ = f32[4,264,128]{2,1,0:T(8,128)S(1)} collective-permute-done((f32[4,264,128]{2,1,0:T(8,128)S(1)}, f32[4,264,128]{2,1,0:T(8,128)S(1)}, u32[]{:S(2)}, u32[]{:S(2)}) %collective-permute-start.12) | collective-permute-done | bytes 540704 | tf_op jit(solution)/shard_map/ppermute | solution.py:396
  110.4 32.4 %shard_map.68 = (f32[256,512]{1,0:T(8,128)S(1)}, f32[256,512]{1,0:T(8,128)S(1)}, f32[256,512]{1,0:T(8,128)S(1)}, f32[256,512]{1,0:T(8,128)S(1)}) custom-call(s32[2]{0:T(128)S(1)} %pad_add_fusion.ids, f32[4,264,128]{2,1,0:T(8,128)S(1)} %get-tuple-element.24.refs_0_, f32[4,264,128]{2,1,0:T(8,128)S(1)} %collective-permute-done.7.refs_1_, ...), custom_call_target="tpu_custom_call" | custom-call | tf_op jit(solution)/shard_map/pallas_call | solution.py:407
  142.7 2.4 %collective-permute-start.15 = (f32[256,512]{1,0:T(8,128)S(1)}, f32[256,512]{1,0:T(8,128)S(1)}, u32[]{:S(2)}, u32[]{:S(2)}) collective-permute-start(f32[256,512]{1,0:T(8,128)S(1)} %get-tuple-element.32), channel_id=1, source_target_pairs={{0,8},{8,16},{16,24},{24,0},{32,40},{40,48},{48,56},{56,32},{64,72... | collective-permute-start | bytes 1572872 | tf_op jit(solution)/shard_map/ppermute | solution.py:423
  145.7 2.2 %collective-permute-start.17 = (f32[256,512]{1,0:T(8,128)S(1)}, f32[256,512]{1,0:T(8,128)S(1)}, u32[]{:S(2)}, u32[]{:S(2)}) collective-permute-start(f32[256,512]{1,0:T(8,128)S(1)} %get-tuple-element.34), channel_id=1, source_target_pairs={{0,24},{8,0},{16,8},{24,16},{32,56},{40,32},{48,40},{56,48},{64,88... | collective-permute-start | bytes 1572872 | tf_op jit(solution)/shard_map/ppermute | solution.py:423
  147.9 20.6 %collective-permute-done.15.refs_1_ = f32[256,512]{1,0:T(8,128)S(1)} collective-permute-done((f32[256,512]{1,0:T(8,128)S(1)}, f32[256,512]{1,0:T(8,128)S(1)}, u32[]{:S(2)}, u32[]{:S(2)}) %collective-permute-start.15) | collective-permute-done | bytes 524320 | tf_op jit(solution)/shard_map/ppermute | solution.py:423
  169.1 2.2 %shard_map.69 = f32[64,16,512]{2,1,0:T(8,128)} custom-call(s32[2]{0:T(128)S(1)} %pad_add_fusion.ids, f32[256,512]{1,0:T(8,128)S(1)} %get-tuple-element.31.refs_0_, f32[256,512]{1,0:T(8,128)S(1)} %collective-permute-done.15.refs_1_, f32[256,512]{1,0:T(8,128)S(1)} %collective-permute-done.16.refs_2_, f32[256,512]{1,0:T(8,128)S(1)} %collective-permute-done.17.refs_3_), custom_call_target="tpu_custom_call" | custom-call | tf_op jit(solution)/shard_map/pallas_call | solution.py:424
  (47 shorter events, 25.2 us)
Async XLA Ops:
  2.3 7.8 %copy-start.3 = (f32[4,3,128,128]{3,2,1,0:T(8,128)S(1)}, f32[4,3,128,128]{3,2,1,0:T(8,128)}, u32[]{:S(2)}) copy-start(f32[4,3,128,128]{3,2,1,0:T(8,128)} %cond.1) | copy-start | bytes 2359300
  2.3 7.8 %copy-start.4 = (f32[63,512]{1,0:T(8,128)S(1)}, f32[63,512]{1,0:T(8,128)}, u32[]{:S(2)}) copy-start(f32[63,512]{1,0:T(8,128)} %vert.1) | copy-start | bytes 387076
  2.3 7.8 %copy-start.6 = (s32[64,3]{0,1:T(4,128)S(1)}, s32[64,3]{0,1:T(4,128)}, u32[]{:S(2)}) copy-start(s32[64,3]{0,1:T(4,128)} %param.8) | copy-start | bytes 2308
  5.5 36.2 %all-to-all-start = ((f32[16,64,512]{2,1,0:T(8,128)}), f32[16,64,512]{2,1,0:T(8,128)S(1)}, u32[]{:S(2)}, u32[]{:S(2)}) async-start(f32[16,64,512]{2,1,0:T(8,128)} %shard_map.64.after), calls=%async_computation | async-start | bytes 4194304 | tf_op jit(solution)/shard_map/all_to_all | solution.py:377
  10.1 31.6 %copy-start.5 = (f32[16,512]{1,0:T(8,128)S(1)}, f32[16,512]{1,0:T(8,128)}, u32[]{:S(2)}) copy-start(f32[16,512]{1,0:T(8,128)} %rain.1) | copy-start | bytes 98308
  10.1 31.6 %copy-start.8 = (s32[128]{0:T(128)S(1)}, s32[128]{0:T(128)}, u32[]{:S(2)}) copy-start(s32[128]{0:T(128)} %anc.3) | copy-start | bytes 1540
  11.0 13.3 %collective-permute-start.3 = (f32[896,128]{1,0:T(8,128)S(1)}, f32[896,128]{1,0:T(8,128)S(1)}, u32[]{:S(2)}, u32[]{:S(2)}) collective-permute-start(f32[896,128]{1,0:T(8,128)S(1)} %shard_map.65), channel_id=1, source_target_pairs={{0,96},{8,104},{16,48},{24,56},{32,0},{40,8},{48,80},{56,88},{64,3... | collective-permute-start | bytes 1376264 | tf_op jit(solution)/shard_map/ppermute | solution.py:373
  13.8 16.9 %collective-permute-start = (f32[896,128]{1,0:T(8,128)S(1)}, f32[896,128]{1,0:T(8,128)S(1)}, u32[]{:S(2)}, u32[]{:S(2)}) collective-permute-start(f32[896,128]{1,0:T(8,128)S(1)} %shard_map.65), channel_id=1, source_target_pairs={{0,8},{8,16},{16,24},{24,0},{32,40},{40,48},{48,56},{56,32},{64,72... | collective-permute-start | bytes 1376264 | tf_op jit(solution)/shard_map/ppermute | solution.py:374
  15.7 23.5 %collective-permute-start.1 = (f32[896,128]{1,0:T(8,128)S(1)}, f32[896,128]{1,0:T(8,128)S(1)}, u32[]{:S(2)}, u32[]{:S(2)}) collective-permute-start(f32[896,128]{1,0:T(8,128)S(1)} %shard_map.65), channel_id=1, source_target_pairs={{0,16},{8,24},{16,0},{24,8},{32,48},{40,56},{48,32},{56,40},{64,80... | collective-permute-start | bytes 1376264 | tf_op jit(solution)/shard_map/ppermute | solution.py:374
  18.0 22.0 %collective-permute-start.2 = (f32[896,128]{1,0:T(8,128)S(1)}, f32[896,128]{1,0:T(8,128)S(1)}, u32[]{:S(2)}, u32[]{:S(2)}) collective-permute-start(f32[896,128]{1,0:T(8,128)S(1)} %shard_map.65), channel_id=1, source_target_pairs={{0,24},{8,0},{16,8},{24,16},{32,56},{40,32},{48,40},{56,48},{64,88... | collective-permute-start | bytes 1376264 | tf_op jit(solution)/shard_map/ppermute | solution.py:374
  24.2 25.0 %collective-permute-start.4 = (f32[896,128]{1,0:T(8,128)S(1)}, f32[896,128]{1,0:T(8,128)}, u32[]{:S(2)}, u32[]{:S(2)}) collective-permute-start(f32[896,128]{1,0:T(8,128)S(1)} %collective-permute-done.3), channel_id=1, source_target_pairs={{0,8},{8,16},{16,24},{24,0},{32,40},{40,48},{48,56},{56,32},{64,72... | collective-permute-start | bytes 1376264 | tf_op jit(solution)/shard_map/ppermute | solution.py:375
  26.2 32.9 %collective-permute-start.5 = (f32[896,128]{1,0:T(8,128)S(1)}, f32[896,128]{1,0:T(8,128)}, u32[]{:S(2)}, u32[]{:S(2)}) collective-permute-start(f32[896,128]{1,0:T(8,128)S(1)} %collective-permute-done.3), channel_id=1, source_target_pairs={{0,16},{8,24},{16,0},{24,8},{32,48},{40,56},{48,32},{56,40},{64,80... | collective-permute-start | bytes 1376264 | tf_op jit(solution)/shard_map/ppermute | solution.py:375
  30.7 30.2 %collective-permute-start.6 = (f32[896,128]{1,0:T(8,128)S(1)}, f32[896,128]{1,0:T(8,128)}, u32[]{:S(2)}, u32[]{:S(2)}) collective-permute-start(f32[896,128]{1,0:T(8,128)S(1)} %collective-permute-done.3), channel_id=1, source_target_pairs={{0,24},{8,0},{16,8},{24,16},{32,56},{40,32},{48,40},{56,48},{64,88... | collective-permute-start | bytes 1376264 | tf_op jit(solution)/shard_map/ppermute | solution.py:375
  43.3 27.1 %collective-permute-start.7 = (f32[4,264,128]{2,1,0:T(8,128)S(1)}, f32[4,264,128]{2,1,0:T(8,128)S(1)}, u32[]{:S(2)}, u32[]{:S(2)}) collective-permute-start(f32[4,264,128]{2,1,0:T(8,128)S(1)} %get-tuple-element.21), channel_id=1, source_target_pairs={{0,8},{8,16},{16,24},{24,0},{32,40},{40,48},{48,56},{56,32},{64,72... | collective-permute-start | bytes 1622024 | tf_op jit(solution)/shard_map/ppermute | solution.py:393
  44.5 36.9 %collective-permute-start.8 = (f32[4,264,128]{2,1,0:T(8,128)S(1)}, f32[4,264,128]{2,1,0:T(8,128)S(1)}, u32[]{:S(2)}, u32[]{:S(2)}) collective-permute-start(f32[4,264,128]{2,1,0:T(8,128)S(1)} %get-tuple-element.22), channel_id=1, source_target_pairs={{0,16},{8,24},{16,0},{24,8},{32,48},{40,56},{48,32},{56,40},{64,80... | collective-permute-start | bytes 1622024 | tf_op jit(solution)/shard_map/ppermute | solution.py:393
  49.2 32.2 %collective-permute-start.9 = (f32[4,264,128]{2,1,0:T(8,128)S(1)}, f32[4,264,128]{2,1,0:T(8,128)S(1)}, u32[]{:S(2)}, u32[]{:S(2)}) collective-permute-start(f32[4,264,128]{2,1,0:T(8,128)S(1)} %get-tuple-element.23), channel_id=1, source_target_pairs={{0,24},{8,0},{16,8},{24,16},{32,56},{40,32},{48,40},{56,48},{64,88... | collective-permute-start | bytes 1622024 | tf_op jit(solution)/shard_map/ppermute | solution.py:393
  81.4 6.6 %collective-permute-start.14 = (f32[8,896,128]{2,1,0:T(8,128)}, f32[8,896,128]{2,1,0:T(8,128)S(1)}, u32[]{:S(2)}, u32[]{:S(2)}) collective-permute-start(f32[8,896,128]{2,1,0:T(8,128)} %bitcast_dynamic-update-slice_fusion.mine), channel_id=1, source_target_pairs={{0,1},{1,0},{2,3},{3,2},{4,5},{5,4},{6,7},{7,6},{8,9},{9,8},{10,11... | collective-permute-start | bytes 11010056 | tf_op jit(solution)/shard_map/ppermute | solution.py:395
  81.4 16.7 %collective-permute-start.10 = (f32[4,264,128]{2,1,0:T(8,128)S(1)}, f32[4,264,128]{2,1,0:T(8,128)S(1)}, u32[]{:S(2)}, u32[]{:S(2)}) collective-permute-start(f32[4,264,128]{2,1,0:T(8,128)S(1)} %get-tuple-element.24.refs_0_), channel_id=1, source_target_pairs={{0,96},{8,104},{16,48},{24,56},{32,0},{40,8},{48,80},{56,88},{64,3... | collective-permute-start | bytes 1622024 | tf_op jit(solution)/shard_map/ppermute | solution.py:396
  83.2 16.3 %collective-permute-start.11 = (f32[4,264,128]{2,1,0:T(8,128)S(1)}, f32[4,264,128]{2,1,0:T(8,128)S(1)}, u32[]{:S(2)}, u32[]{:S(2)}) collective-permute-start(f32[4,264,128]{2,1,0:T(8,128)S(1)} %collective-permute-done.7.refs_1_), channel_id=1, source_target_pairs={{0,32},{8,104},{16,112},{24,56},{32,64},{40,8},{48,16},{56,88},{64... | collective-permute-start | bytes 1622024 | tf_op jit(solution)/shard_map/ppermute | solution.py:396
  83.4 26.9 %collective-permute-start.12 = (f32[4,264,128]{2,1,0:T(8,128)S(1)}, f32[4,264,128]{2,1,0:T(8,128)S(1)}, u32[]{:S(2)}, u32[]{:S(2)}) collective-permute-start(f32[4,264,128]{2,1,0:T(8,128)S(1)} %collective-permute-done.8.refs_2_), channel_id=1, source_target_pairs={{0,32},{8,40},{16,112},{24,120},{32,64},{40,72},{48,16},{56,24},{6... | collective-permute-start | bytes 1622024 | tf_op jit(solution)/shard_map/ppermute | solution.py:396
  84.9 25.4 %collective-permute-start.13 = (f32[4,264,128]{2,1,0:T(8,128)S(1)}, f32[4,264,128]{2,1,0:T(8,128)S(1)}, u32[]{:S(2)}, u32[]{:S(2)}) collective-permute-start(f32[4,264,128]{2,1,0:T(8,128)S(1)} %collective-permute-done.9.refs_3_), channel_id=1, source_target_pairs={{0,96},{8,40},{16,48},{24,120},{32,0},{40,72},{48,80},{56,24},{64,... | collective-permute-start | bytes 1622024 | tf_op jit(solution)/shard_map/ppermute | solution.py:396
  142.7 25.8 %collective-permute-start.15 = (f32[256,512]{1,0:T(8,128)S(1)}, f32[256,512]{1,0:T(8,128)S(1)}, u32[]{:S(2)}, u32[]{:S(2)}) collective-permute-start(f32[256,512]{1,0:T(8,128)S(1)} %get-tuple-element.32), channel_id=1, source_target_pairs={{0,8},{8,16},{16,24},{24,0},{32,40},{40,48},{48,56},{56,32},{64,72... | collective-permute-start | bytes 1572872 | tf_op jit(solution)/shard_map/ppermute | solution.py:423
  145.1 23.4 %collective-permute-start.16 = (f32[256,512]{1,0:T(8,128)S(1)}, f32[256,512]{1,0:T(8,128)S(1)}, u32[]{:S(2)}, u32[]{:S(2)}) collective-permute-start(f32[256,512]{1,0:T(8,128)S(1)} %get-tuple-element.33), channel_id=1, source_target_pairs={{0,16},{8,24},{16,0},{24,8},{32,48},{40,56},{48,32},{56,40},{64,80... | collective-permute-start | bytes 1572872 | tf_op jit(solution)/shard_map/ppermute | solution.py:423
  145.7 23.4 %collective-permute-start.17 = (f32[256,512]{1,0:T(8,128)S(1)}, f32[256,512]{1,0:T(8,128)S(1)}, u32[]{:S(2)}, u32[]{:S(2)}) collective-permute-start(f32[256,512]{1,0:T(8,128)S(1)} %get-tuple-element.34), channel_id=1, source_target_pairs={{0,24},{8,0},{16,8},{24,16},{32,56},{40,32},{48,40},{56,48},{64,88... | collective-permute-start | bytes 1572872 | tf_op jit(solution)/shard_map/ppermute | solution.py:423
  (4 other events, 7.2 us)

commit v3 on v2

--- a/solution.py
+++ b/solution.py
@@ -45,6 +45,10 @@
             step = -1 if (z - s) % 4 < 2 else 1
             out.append((4 * x + z, 4 * ((x + step) % 4) + z))
     return out
+
+
+def row_pairs(step):
+    return [(4 * x + z, 4 * ((x + step) % 4) + z) for x in range(4) for z in range(4)]
 
 
 def core_pairs():
@@ -154,25 +158,44 @@
     return 8 + 4 * t
 
 
-def expand_kernel(ids, mine, other, w_ref, c_ref, vs):
+def order_kernel(ids, *refs):
+    ins, tiles, halves, sems, half_sems = refs[:RING], refs[RING], refs[RING + 1:RING + 3], refs[RING + 3], refs[RING + 4]
     z = lax.rem(ids[0], RING)
+    copies = []
+    for s in range(RING):
+        t = lax.rem(z - s + RING, RING)
+        copies.append(pltpu.make_async_copy(ins[s], tiles.at[t], sems.at[s]))
+        copies[-1].start()
+        for h in range(2):
+            @pl.when(t // 2 == h)
+            def _(s=s, t=t, h=h):
+                pltpu.make_async_copy(ins[s], halves[h].at[t - 2 * h], half_sems.at[s]).start()
+    for s in range(RING):
+        copies[s].wait()
+        pltpu.make_async_copy(ins[s], halves[0].at[0], half_sems.at[s]).wait()
+
+
+def expand_kernel(ids, *refs):
+    msgs = refs[:6]
+    w_ref, c_ref, vs = refs[6:]
     core = lax.rem(ids[1], 2)
-    for at in range(2 * RING):
-        base = window_base(z, at % RING, at >= RING) // 2
-        for msg, half in ((mine, core), (other, 1 - core)):
-            k = base + half
-            for i in range(2):
-                row = i * (3 * SPAN + LAYERS)
-                cols = slice(i * SPAN, (i + 1) * SPAN)
-                rows = slice(i * SPAN, (i + 3) * SPAN)
-                w = msg[at, row:row + 3 * SPAN, :]
-                hi = w.astype(BF16)
-                w_ref[k, 0, rows, cols] = hi
-                w_ref[k, 1, rows, cols] = (w - hi.astype(F32)).astype(BF16)
-                empty = slice(3 * SPAN, 4 * SPAN) if i == 0 else slice(0, SPAN)
-                w_ref[k, 0, empty, cols] = jnp.zeros((SPAN, SPAN), BF16)
-                w_ref[k, 1, empty, cols] = jnp.zeros((SPAN, SPAN), BF16)
-                vs[k, :, i * SPAN:(i + 1) * SPAN] = msg[at, row + 3 * SPAN:row + 3 * SPAN + LAYERS, :]
+    for part, (start, tiles) in enumerate(((4, 4), (12, 2), (0, 2))):
+        for at in range(tiles):
+            for other in range(2):
+                msg = msgs[2 * part + other]
+                k = start + 2 * at + (core if other == 0 else 1 - core)
+                for i in range(2):
+                    row = i * (3 * SPAN + LAYERS)
+                    cols = slice(i * SPAN, (i + 1) * SPAN)
+                    rows = slice(i * SPAN, (i + 3) * SPAN)
+                    w = msg[at, row:row + 3 * SPAN, :]
+                    hi = w.astype(BF16)
+                    w_ref[k, 0, rows, cols] = hi
+                    w_ref[k, 1, rows, cols] = (w - hi.astype(F32)).astype(BF16)
+                    empty = slice(3 * SPAN, 4 * SPAN) if i == 0 else slice(0, SPAN)
+                    w_ref[k, 0, empty, cols] = jnp.zeros((SPAN, SPAN), BF16)
+                    w_ref[k, 1, empty, cols] = jnp.zeros((SPAN, SPAN), BF16)
+                    vs[k, :, i * SPAN:(i + 1) * SPAN] = msg[at, row + 3 * SPAN:row + 3 * SPAN + LAYERS, :]
     first = lax.broadcasted_iota(jnp.int32, (2, 2 * SPAN), 0) == 0
     group = 8
 
@@ -370,10 +393,16 @@
         out_specs=VMEM,
         compiler_params=params(8),
     )(ids, adjacency.T, conductance, vertical, sent)
-    c_far = lax.ppermute(coeff, "tile", x_pairs(0))
-    c_near = [coeff] + [lax.ppermute(coeff, "tile", z_pairs(s)) for s in range(1, RING)]
-    c_far = [c_far] + [lax.ppermute(c_far, "tile", z_pairs(s)) for s in range(1, RING)]
-    c_mine = jnp.stack(c_near + c_far)
+    c_ring = [coeff] + [lax.ppermute(coeff, "tile", z_pairs(s)) for s in range(1, RING)]
+    c_tiles, c_low, c_high = pl.pallas_call(
+        order_kernel,
+        out_shape=[shape((RING, MSG, SPAN)), shape((2, MSG, SPAN)), shape((2, MSG, SPAN))],
+        in_specs=[SMEM] + [ANY] * RING,
+        out_specs=[ANY] * 3,
+        scratch_shapes=[pltpu.SemaphoreType.DMA((RING,)), pltpu.SemaphoreType.DMA((RING,))],
+        compiler_params=params(4),
+    )(ids, *c_ring)
+    c_parts = [c_tiles, lax.ppermute(c_low, "tile", row_pairs(-1)), lax.ppermute(c_high, "tile", row_pairs(1))]
     got = lax.all_to_all(sent, "dom", split_axis=0, concat_axis=0, tiled=True)
 
     mine = pl.pallas_call(
@@ -391,18 +420,20 @@
         compiler_params=params(12),
     )(ids, ancestors, rainfall, got)
     ring = [mine[0]] + [lax.ppermute(mine[s], "tile", z_pairs(s)) for s in range(1, RING)]
-    c_mine, *ring = lax.optimization_barrier((c_mine, *ring))
-    c_other = lax.ppermute(c_mine, "dom", core_pairs())
+    *c_parts, ring[0], ring[1], ring[2], ring[3] = lax.optimization_barrier((*c_parts, *ring))
+    c_all = []
+    for c in c_parts:
+        c_all += [c, lax.ppermute(c, "dom", core_pairs())]
     side = [lax.ppermute(ring[s], "tile", x_pairs(s)) for s in range(RING)]
 
     coefs = pl.pallas_call(
         expand_kernel,
         out_shape=[shape((PAIRS, 2, 4 * SPAN, 2 * SPAN), BF16), shape((PAIRS, 6 * HALF + 8, 2 * SPAN))],
-        in_specs=[SMEM, VMEM, VMEM],
+        in_specs=[SMEM] + [VMEM] * 6,
         out_specs=[VMEM] * 2,
         scratch_shapes=[pltpu.VMEM((PAIRS, LAYERS, 2 * SPAN), F32)],
         compiler_params=params(26),
-    )(ids, c_mine, c_other)
+    )(ids, *c_all)
 
     back = pl.pallas_call(
         step_kernel,

time: 172 us -> 168 us (0.977)
  local copies, waits for them, and re-layouts: 16.7 us -> 8.46 us
    ppermute x3, waiting for transfers between devices: 18.7 us -> 5.53 us  [shards(): lax.ppermute(mine[s], 'tile', z_pairs(s))]
    ppermute x3, waiting for transfers between devices: 6.75 us -> 19.7 us  [shards(): lax.ppermute(coeff, 'tile', z_pairs(s))]
    ppermute x5, starting transfers between devices: 10.3 us -> 3.35 us  [the longest x1 2.76 us: shards(): lax.ppermute(c_low, 'tile', row_pairs(-1))]
    unnamed x25 -> x22, local copies, waits for them, and re-layouts: 14.9 us -> 8.46 us
    ppermute x3, starting transfers between devices: 5.14 us -> 9.63 us  [shards(): lax.ppermute(back[s], 'tile', z_pairs(s))]
    ppermute x5, waiting for transfers between devices: 15.9 us -> 19.3 us  [the longest x1 13.3 us: shards(): lax.ppermute(c_low, 'tile', row_pairs(-1))]
    ppermute x4, waiting for transfers between devices: 12.3 us -> 9.52 us  [shards(): side = [lax.ppermute(ring[s], 'tile', x_pairs(s)) for s in range(RING)]]
    pallas_call x0 -> x1, Pallas kernels: none -> 2.53 us  [shards(): pl.pallas_call(order_kernel, out_shape=[shape((RING, MSG, SPAN)), shape((...]
  transfers between devices with their start and end apart: 19 -> 19, of which waited for: 11 -> 10; matrix products, arithmetic and copies ran while one was open for 6% -> 0% of each run, Pallas kernels for 4% -> 5%
where the time goes in v3:
time: 168 us; the launch traced here: 167 us
  waiting for transfers between devices  76.4 us (45%)
  Pallas kernels  46.8 us (28%)
  starting transfers between devices  35.4 us (21%)
  local copies, waits for them, and re-layouts  8.46 us (5%)
    pallas_call x1, Pallas kernels, shards(): pl.pallas_call(step_kernel, out_shape=[shape((ROWS, WIDTH))] * RING, in_s...  32.4 us
    ppermute x3, waiting for transfers between devices, shards(): lax.ppermute(back[s], 'tile', z_pairs(s))  22.3 us
    ppermute x3, waiting for transfers between devices, shards(): lax.ppermute(coeff, 'tile', z_pairs(s))  19.7 us
    ppermute x1, waiting for transfers between devices, shards(): lax.ppermute(c_low, 'tile', row_pairs(-1))  13.3 us
    ppermute x3, starting transfers between devices, shards(): lax.ppermute(back[s], 'tile', z_pairs(s))  9.63 us
    ppermute x4, waiting for transfers between devices, shards(): side = [lax.ppermute(ring[s], 'tile', x_pairs(s)) for s in range(RING)]  9.52 us
    unnamed x22, local copies, waits for them, and re-layouts  8.46 us
    ppermute x3, starting transfers between devices, shards(): lax.ppermute(coeff, 'tile', z_pairs(s))  6.58 us
  transfers between devices with their start and end apart: 19, of which 10 were waited for; matrix products, arithmetic and copies ran while one was open for 0% of the time, Pallas kernels for 5%

profile of v3, /device:TPU:0, one launch (start us, length us, event | category | flops | bytes accessed | tf_op | source)
XLA Modules:
  0.0 167.4 jit_solution(14266454104569107528)
XLA Ops:
  2.3 3.2 %shard_map.64.after = f32[16,64,512]{2,1,0:T(8,128)} custom-call(s32[2]{0:T(128)S(1)} %pad_add_fusion.ids, s32[128]{0:T(128)S(1)} %copy-done.9, f32[1024,512]{1,0:T(8,128)S(1)} %bitcast.4), custom_call_target="tpu_custom_call" | custom-call | tf_op jit(solution)/shard_map/pallas_call | solution.py:376
  5.5 4.7 %all-to-all-start = ((f32[16,64,512]{2,1,0:T(8,128)}), f32[16,64,512]{2,1,0:T(8,128)S(1)}, u32[]{:S(2)}, u32[]{:S(2)}) async-start(f32[16,64,512]{2,1,0:T(8,128)} %shard_map.64.after), calls=%async_computation | async-start | bytes 4194304 | tf_op jit(solution)/shard_map/all_to_all | solution.py:406
  11.1 2.0 %collective-permute-start = (f32[896,128]{1,0:T(8,128)S(1)}, f32[896,128]{1,0:T(8,128)S(1)}, u32[]{:S(2)}, u32[]{:S(2)}) collective-permute-start(f32[896,128]{1,0:T(8,128)S(1)} %shard_map.65.refs_0_), channel_id=1, source_target_pairs={{0,8},{8,16},{16,24},{24,0},{32,40},{40,48},{48,56},{56,32},{64,72... | collective-permute-start | bytes 1376264 | tf_op jit(solution)/shard_map/ppermute | solution.py:396
  13.1 3.6 %collective-permute-start.1 = (f32[896,128]{1,0:T(8,128)S(1)}, f32[896,128]{1,0:T(8,128)S(1)}, u32[]{:S(2)}, u32[]{:S(2)}) collective-permute-start(f32[896,128]{1,0:T(8,128)S(1)} %shard_map.65.refs_0_), channel_id=1, source_target_pairs={{0,16},{8,24},{16,0},{24,8},{32,48},{40,56},{48,32},{56,40},{64,80... | collective-permute-start | bytes 1376264 | tf_op jit(solution)/shard_map/ppermute | solution.py:396
  17.7 8.7 %collective-permute-done.refs_1_ = f32[896,128]{1,0:T(8,128)S(1)} collective-permute-done((f32[896,128]{1,0:T(8,128)S(1)}, f32[896,128]{1,0:T(8,128)S(1)}, u32[]{:S(2)}, u32[]{:S(2)}) %collective-permute-start) | collective-permute-done | bytes 458784 | tf_op jit(solution)/shard_map/ppermute | solution.py:396
  26.4 11.0 %collective-permute-done.1.refs_2_ = f32[896,128]{1,0:T(8,128)S(1)} collective-permute-done((f32[896,128]{1,0:T(8,128)S(1)}, f32[896,128]{1,0:T(8,128)S(1)}, u32[]{:S(2)}, u32[]{:S(2)}) %collective-permute-start.1) | collective-permute-done | bytes 458784 | tf_op jit(solution)/shard_map/ppermute | solution.py:396
  37.4 2.5 %shard_map.66 = (f32[4,896,128]{2,1,0:T(8,128)S(1)}, f32[2,896,128]{2,1,0:T(8,128)}, f32[2,896,128]{2,1,0:T(8,128)}) custom-call(s32[2]{0:T(128)S(1)} %pad_add_fusion.ids, f32[896,128]{1,0:T(8,128)S(1)} %shard_map.65.refs_0_, f32[896,128]{1,0:T(8,128)S(1)} %collective-permute-done.refs_1_, f32[896,128]{1,0:T(8,128)S(1)} %collective-permute-done.1.refs_2_, ...), custom_call_target="tpu_custom_call" | custom-call | tf_op jit(solution)/shard_map/pallas_call | solution.py:397
  41.2 2.8 %collective-permute-start.3 = (f32[2,896,128]{2,1,0:T(8,128)}, f32[2,896,128]{2,1,0:T(8,128)S(1)}, u32[]{:S(2)}, u32[]{:S(2)}) collective-permute-start(f32[2,896,128]{2,1,0:T(8,128)} %get-tuple-element.26), channel_id=1, source_target_pairs={{0,96},{8,104},{16,112},{24,120},{32,0},{40,8},{48,16},{56,24},{64... | collective-permute-start | bytes 2752520 | tf_op jit(solution)/shard_map/ppermute | solution.py:405
  46.9 2.4 %collective-permute-start.6 = (f32[4,264,128]{2,1,0:T(8,128)S(1)}, f32[4,264,128]{2,1,0:T(8,128)S(1)}, u32[]{:S(2)}, u32[]{:S(2)}) collective-permute-start(f32[4,264,128]{2,1,0:T(8,128)S(1)} %get-tuple-element.30), channel_id=1, source_target_pairs={{0,16},{8,24},{16,0},{24,8},{32,48},{40,56},{48,32},{56,40},{64,80... | collective-permute-start | bytes 1622024 | tf_op jit(solution)/shard_map/ppermute | solution.py:422
  50.5 13.3 %collective-permute-done.3.refs_2_ = f32[2,896,128]{2,1,0:T(8,128)S(1)} collective-permute-done((f32[2,896,128]{2,1,0:T(8,128)}, f32[2,896,128]{2,1,0:T(8,128)S(1)}, u32[]{:S(2)}, u32[]{:S(2)}) %collective-permute-start.3) | collective-permute-done | bytes 917536 | tf_op jit(solution)/shard_map/ppermute | solution.py:405
  63.8 3.4 %collective-permute-done.4.refs_4_ = f32[2,896,128]{2,1,0:T(8,128)} collective-permute-done((f32[2,896,128]{2,1,0:T(8,128)}, f32[2,896,128]{2,1,0:T(8,128)}, u32[]{:S(2)}, u32[]{:S(2)}) %collective-permute-start.4) | collective-permute-done | bytes 917536 | tf_op jit(solution)/shard_map/ppermute | solution.py:405
  67.2 5.5 %collective-permute-done.6.refs_2_ = f32[4,264,128]{2,1,0:T(8,128)S(1)} collective-permute-done((f32[4,264,128]{2,1,0:T(8,128)S(1)}, f32[4,264,128]{2,1,0:T(8,128)S(1)}, u32[]{:S(2)}, u32[]{:S(2)}) %collective-permute-start.6) | collective-permute-done | bytes 540704 | tf_op jit(solution)/shard_map/ppermute | solution.py:422
  73.8 2.8 %collective-permute-start.11 = (f32[4,264,128]{2,1,0:T(8,128)S(1)}, f32[4,264,128]{2,1,0:T(8,128)S(1)}, u32[]{:S(2)}, u32[]{:S(2)}) collective-permute-start(f32[4,264,128]{2,1,0:T(8,128)S(1)} %collective-permute-done.7.refs_3_), channel_id=1, source_target_pairs={{0,96},{8,40},{16,48},{24,120},{32,0},{40,72},{48,80},{56,24},{64,... | collective-permute-start | bytes 1622024 | tf_op jit(solution)/shard_map/ppermute | solution.py:427
  76.6 2.6 %collective-permute-done.13.refs_3_ = f32[2,896,128]{2,1,0:T(8,128)S(1)} collective-permute-done((f32[2,896,128]{2,1,0:T(8,128)S(1)}, f32[2,896,128]{2,1,0:T(8,128)S(1)}, u32[]{:S(2)}, u32[]{:S(2)}) %collective-permute-start.13) | collective-permute-done | bytes 917536 | tf_op jit(solution)/shard_map/ppermute | solution.py:426
  79.2 2.9 %collective-permute-start.8 = (f32[4,264,128]{2,1,0:T(8,128)S(1)}, f32[4,264,128]{2,1,0:T(8,128)S(1)}, u32[]{:S(2)}, u32[]{:S(2)}) collective-permute-start(f32[4,264,128]{2,1,0:T(8,128)S(1)} %get-tuple-element.32.refs_0_), channel_id=1, source_target_pairs={{0,96},{8,104},{16,48},{24,56},{32,0},{40,8},{48,80},{56,88},{64,3... | collective-permute-start | bytes 1622024 | tf_op jit(solution)/shard_map/ppermute | solution.py:427
  82.1 4.2 %shard_map.68 = (bf16[16,2,512,256]{3,2,1,0:T(8,128)(2,1)S(1)}, f32[16,200,256]{2,1,0:T(8,128)S(1)}) custom-call(s32[2]{0:T(128)S(1)} %pad_add_fusion.ids, f32[4,896,128]{2,1,0:T(8,128)S(1)} %copy-done.4, f32[4,896,128]{2,1,0:T(8,128)S(1)} %collective-permute-done.12.refs_1_, f32[2,896,128]{2,1,0:T(8,128)S(1)} %collective-permute-done.3.refs_2_, ...), custom_call_target="tpu_custom_call" | custom-call | tf_op jit(solution)/shard_map/pallas_call | solution.py:429
  86.3 3.3 %copy-done = bf16[16,2,512,256]{3,2,1,0:T(8,128)(2,1)} copy-done((bf16[16,2,512,256]{3,2,1,0:T(8,128)(2,1)}, bf16[16,2,512,256]{3,2,1,0:T(8,128)(2,1)S(1)}, u32[]{:S(2)}) %copy-start) | copy-done | bytes 8388632
  91.2 8.8 %collective-permute-done.8.refs_4_ = f32[4,264,128]{2,1,0:T(8,128)S(1)} collective-permute-done((f32[4,264,128]{2,1,0:T(8,128)S(1)}, f32[4,264,128]{2,1,0:T(8,128)S(1)}, u32[]{:S(2)}, u32[]{:S(2)}) %collective-permute-start.8) | collective-permute-done | bytes 540704 | tf_op jit(solution)/shard_map/ppermute | solution.py:427
  100.8 32.4 %shard_map.69 = (f32[256,512]{1,0:T(8,128)S(1)}, f32[256,512]{1,0:T(8,128)S(1)}, f32[256,512]{1,0:T(8,128)S(1)}, f32[256,512]{1,0:T(8,128)S(1)}) custom-call(s32[2]{0:T(128)S(1)} %pad_add_fusion.ids, f32[4,264,128]{2,1,0:T(8,128)S(1)} %get-tuple-element.32.refs_0_, f32[4,264,128]{2,1,0:T(8,128)S(1)} %collective-permute-done.5.refs_1_, ...), custom_call_target="tpu_custom_call" | custom-call | tf_op jit(solution)/shard_map/pallas_call | solution.py:438
  133.1 6.0 %collective-permute-start.15 = (f32[256,512]{1,0:T(8,128)S(1)}, f32[256,512]{1,0:T(8,128)S(1)}, u32[]{:S(2)}, u32[]{:S(2)}) collective-permute-start(f32[256,512]{1,0:T(8,128)S(1)} %get-tuple-element.42), channel_id=1, source_target_pairs={{0,8},{8,16},{16,24},{24,0},{32,40},{40,48},{48,56},{56,32},{64,72... | collective-permute-start | bytes 1572872 | tf_op jit(solution)/shard_map/ppermute | solution.py:454
  139.2 3.6 %collective-permute-start.16 = (f32[256,512]{1,0:T(8,128)S(1)}, f32[256,512]{1,0:T(8,128)S(1)}, u32[]{:S(2)}, u32[]{:S(2)}) collective-permute-start(f32[256,512]{1,0:T(8,128)S(1)} %get-tuple-element.43), channel_id=1, source_target_pairs={{0,16},{8,24},{16,0},{24,8},{32,48},{40,56},{48,32},{56,40},{64,80... | collective-permute-start | bytes 1572872 | tf_op jit(solution)/shard_map/ppermute | solution.py:454
  142.8 10.5 %collective-permute-done.15.refs_1_ = f32[256,512]{1,0:T(8,128)S(1)} collective-permute-done((f32[256,512]{1,0:T(8,128)S(1)}, f32[256,512]{1,0:T(8,128)S(1)}, u32[]{:S(2)}, u32[]{:S(2)}) %collective-permute-start.15) | collective-permute-done | bytes 524320 | tf_op jit(solution)/shard_map/ppermute | solution.py:454
  153.2 11.9 %collective-permute-done.16.refs_2_ = f32[256,512]{1,0:T(8,128)S(1)} collective-permute-done((f32[256,512]{1,0:T(8,128)S(1)}, f32[256,512]{1,0:T(8,128)S(1)}, u32[]{:S(2)}, u32[]{:S(2)}) %collective-permute-start.16) | collective-permute-done | bytes 524320 | tf_op jit(solution)/shard_map/ppermute | solution.py:454
  165.1 2.2 %shard_map.70 = f32[64,16,512]{2,1,0:T(8,128)} custom-call(s32[2]{0:T(128)S(1)} %pad_add_fusion.ids, f32[256,512]{1,0:T(8,128)S(1)} %get-tuple-element.41.refs_0_, f32[256,512]{1,0:T(8,128)S(1)} %collective-permute-done.15.refs_1_, f32[256,512]{1,0:T(8,128)S(1)} %collective-permute-done.16.refs_2_, f32[256,512]{1,0:T(8,128)S(1)} %collective-permute-done.17.refs_3_), custom_call_target="tpu_custom_call" | custom-call | tf_op jit(solution)/shard_map/pallas_call | solution.py:455
  (44 shorter events, 13.0 us)
Async XLA Ops:
  5.5 4.7 %copy-start.5 = (f32[4,3,128,128]{3,2,1,0:T(8,128)S(1)}, f32[4,3,128,128]{3,2,1,0:T(8,128)}, u32[]{:S(2)}) copy-start(f32[4,3,128,128]{3,2,1,0:T(8,128)} %cond.1) | copy-start | bytes 2359300
  5.5 4.7 %copy-start.6 = (f32[63,512]{1,0:T(8,128)S(1)}, f32[63,512]{1,0:T(8,128)}, u32[]{:S(2)}) copy-start(f32[63,512]{1,0:T(8,128)} %vert.1) | copy-start | bytes 387076
  5.5 38.4 %all-to-all-start = ((f32[16,64,512]{2,1,0:T(8,128)}), f32[16,64,512]{2,1,0:T(8,128)S(1)}, u32[]{:S(2)}, u32[]{:S(2)}) async-start(f32[16,64,512]{2,1,0:T(8,128)} %shard_map.64.after), calls=%async_computation | async-start | bytes 4194304 | tf_op jit(solution)/shard_map/all_to_all | solution.py:406
  10.3 33.7 %copy-start.7 = (f32[16,512]{1,0:T(8,128)S(1)}, f32[16,512]{1,0:T(8,128)}, u32[]{:S(2)}) copy-start(f32[16,512]{1,0:T(8,128)} %rain.1) | copy-start | bytes 98308
  10.3 33.7 %copy-start.10 = (s32[128]{0:T(128)S(1)}, s32[128]{0:T(128)}, u32[]{:S(2)}) copy-start(s32[128]{0:T(128)} %anc.3) | copy-start | bytes 1540
  11.1 15.3 %collective-permute-start = (f32[896,128]{1,0:T(8,128)S(1)}, f32[896,128]{1,0:T(8,128)S(1)}, u32[]{:S(2)}, u32[]{:S(2)}) collective-permute-start(f32[896,128]{1,0:T(8,128)S(1)} %shard_map.65.refs_0_), channel_id=1, source_target_pairs={{0,8},{8,16},{16,24},{24,0},{32,40},{40,48},{48,56},{56,32},{64,72... | collective-permute-start | bytes 1376264 | tf_op jit(solution)/shard_map/ppermute | solution.py:396
  13.1 24.3 %collective-permute-start.1 = (f32[896,128]{1,0:T(8,128)S(1)}, f32[896,128]{1,0:T(8,128)S(1)}, u32[]{:S(2)}, u32[]{:S(2)}) collective-permute-start(f32[896,128]{1,0:T(8,128)S(1)} %shard_map.65.refs_0_), channel_id=1, source_target_pairs={{0,16},{8,24},{16,0},{24,8},{32,48},{40,56},{48,32},{56,40},{64,80... | collective-permute-start | bytes 1376264 | tf_op jit(solution)/shard_map/ppermute | solution.py:396
  16.7 20.7 %collective-permute-start.2 = (f32[896,128]{1,0:T(8,128)S(1)}, f32[896,128]{1,0:T(8,128)S(1)}, u32[]{:S(2)}, u32[]{:S(2)}) collective-permute-start(f32[896,128]{1,0:T(8,128)S(1)} %shard_map.65.refs_0_), channel_id=1, source_target_pairs={{0,24},{8,0},{16,8},{24,16},{32,56},{40,32},{48,40},{56,48},{64,88... | collective-permute-start | bytes 1376264 | tf_op jit(solution)/shard_map/ppermute | solution.py:396
  41.2 22.6 %collective-permute-start.3 = (f32[2,896,128]{2,1,0:T(8,128)}, f32[2,896,128]{2,1,0:T(8,128)S(1)}, u32[]{:S(2)}, u32[]{:S(2)}) collective-permute-start(f32[2,896,128]{2,1,0:T(8,128)} %get-tuple-element.26), channel_id=1, source_target_pairs={{0,96},{8,104},{16,112},{24,120},{32,0},{40,8},{48,16},{56,24},{64... | collective-permute-start | bytes 2752520 | tf_op jit(solution)/shard_map/ppermute | solution.py:405
  44.0 23.2 %collective-permute-start.4 = (f32[2,896,128]{2,1,0:T(8,128)}, f32[2,896,128]{2,1,0:T(8,128)}, u32[]{:S(2)}, u32[]{:S(2)}) collective-permute-start(f32[2,896,128]{2,1,0:T(8,128)} %get-tuple-element.27), channel_id=1, source_target_pairs={{0,32},{8,40},{16,48},{24,56},{32,64},{40,72},{48,80},{56,88},{64,... | collective-permute-start | bytes 2752520 | tf_op jit(solution)/shard_map/ppermute | solution.py:405
  44.0 28.7 %copy-start.4 = (f32[4,896,128]{2,1,0:T(8,128)S(1)}, f32[4,896,128]{2,1,0:T(8,128)}, u32[]{:S(2)}) copy-start(f32[4,896,128]{2,1,0:T(8,128)} %copy-done.3) | copy-start | bytes 5505028
  45.6 21.6 %collective-permute-start.5 = (f32[4,264,128]{2,1,0:T(8,128)S(1)}, f32[4,264,128]{2,1,0:T(8,128)S(1)}, u32[]{:S(2)}, u32[]{:S(2)}) collective-permute-start(f32[4,264,128]{2,1,0:T(8,128)S(1)} %get-tuple-element.29), channel_id=1, source_target_pairs={{0,8},{8,16},{16,24},{24,0},{32,40},{40,48},{48,56},{56,32},{64,72... | collective-permute-start | bytes 1622024 | tf_op jit(solution)/shard_map/ppermute | solution.py:422
  46.9 25.9 %collective-permute-start.6 = (f32[4,264,128]{2,1,0:T(8,128)S(1)}, f32[4,264,128]{2,1,0:T(8,128)S(1)}, u32[]{:S(2)}, u32[]{:S(2)}) collective-permute-start(f32[4,264,128]{2,1,0:T(8,128)S(1)} %get-tuple-element.30), channel_id=1, source_target_pairs={{0,16},{8,24},{16,0},{24,8},{32,48},{40,56},{48,32},{56,40},{64,80... | collective-permute-start | bytes 1622024 | tf_op jit(solution)/shard_map/ppermute | solution.py:422
  49.3 23.5 %collective-permute-start.7 = (f32[4,264,128]{2,1,0:T(8,128)S(1)}, f32[4,264,128]{2,1,0:T(8,128)S(1)}, u32[]{:S(2)}, u32[]{:S(2)}) collective-permute-start(f32[4,264,128]{2,1,0:T(8,128)S(1)} %get-tuple-element.31), channel_id=1, source_target_pairs={{0,24},{8,0},{16,8},{24,16},{32,56},{40,32},{48,40},{56,48},{64,88... | collective-permute-start | bytes 1622024 | tf_op jit(solution)/shard_map/ppermute | solution.py:422
  72.7 9.4 %collective-permute-start.12 = (f32[4,896,128]{2,1,0:T(8,128)S(1)}, f32[4,896,128]{2,1,0:T(8,128)S(1)}, u32[]{:S(2)}, u32[]{:S(2)}) collective-permute-start(f32[4,896,128]{2,1,0:T(8,128)S(1)} %copy-done.4), channel_id=1, source_target_pairs={{0,1},{1,0},{2,3},{3,2},{4,5},{5,4},{6,7},{7,6},{8,9},{9,8},{10,11... | collective-permute-start | bytes 5505032 | tf_op jit(solution)/shard_map/ppermute | solution.py:426
  72.7 6.4 %collective-permute-start.13 = (f32[2,896,128]{2,1,0:T(8,128)S(1)}, f32[2,896,128]{2,1,0:T(8,128)S(1)}, u32[]{:S(2)}, u32[]{:S(2)}) collective-permute-start(f32[2,896,128]{2,1,0:T(8,128)S(1)} %collective-permute-done.3.refs_2_), channel_id=1, source_target_pairs={{0,1},{1,0},{2,3},{3,2},{4,5},{5,4},{6,7},{7,6},{8,9},{9,8},{10,11... | collective-permute-start | bytes 2752520 | tf_op jit(solution)/shard_map/ppermute | solution.py:426
  73.3 8.8 %collective-permute-start.14 = (f32[2,896,128]{2,1,0:T(8,128)}, f32[2,896,128]{2,1,0:T(8,128)S(1)}, u32[]{:S(2)}, u32[]{:S(2)}) collective-permute-start(f32[2,896,128]{2,1,0:T(8,128)} %collective-permute-done.4.refs_4_), channel_id=1, source_target_pairs={{0,1},{1,0},{2,3},{3,2},{4,5},{5,4},{6,7},{7,6},{8,9},{9,8},{10,11... | collective-permute-start | bytes 2752520 | tf_op jit(solution)/shard_map/ppermute | solution.py:426
  73.3 17.9 %collective-permute-start.10 = (f32[4,264,128]{2,1,0:T(8,128)S(1)}, f32[4,264,128]{2,1,0:T(8,128)S(1)}, u32[]{:S(2)}, u32[]{:S(2)}) collective-permute-start(f32[4,264,128]{2,1,0:T(8,128)S(1)} %collective-permute-done.6.refs_2_), channel_id=1, source_target_pairs={{0,32},{8,40},{16,112},{24,120},{32,64},{40,72},{48,16},{56,24},{6... | collective-permute-start | bytes 1622024 | tf_op jit(solution)/shard_map/ppermute | solution.py:427
  73.8 17.4 %collective-permute-start.11 = (f32[4,264,128]{2,1,0:T(8,128)S(1)}, f32[4,264,128]{2,1,0:T(8,128)S(1)}, u32[]{:S(2)}, u32[]{:S(2)}) collective-permute-start(f32[4,264,128]{2,1,0:T(8,128)S(1)} %collective-permute-done.7.refs_3_), channel_id=1, source_target_pairs={{0,96},{8,40},{16,48},{24,120},{32,0},{40,72},{48,80},{56,24},{64,... | collective-permute-start | bytes 1622024 | tf_op jit(solution)/shard_map/ppermute | solution.py:427
  79.2 20.9 %collective-permute-start.8 = (f32[4,264,128]{2,1,0:T(8,128)S(1)}, f32[4,264,128]{2,1,0:T(8,128)S(1)}, u32[]{:S(2)}, u32[]{:S(2)}) collective-permute-start(f32[4,264,128]{2,1,0:T(8,128)S(1)} %get-tuple-element.32.refs_0_), channel_id=1, source_target_pairs={{0,96},{8,104},{16,48},{24,56},{32,0},{40,8},{48,80},{56,88},{64,3... | collective-permute-start | bytes 1622024 | tf_op jit(solution)/shard_map/ppermute | solution.py:427
  82.1 18.7 %collective-permute-start.9 = (f32[4,264,128]{2,1,0:T(8,128)S(1)}, f32[4,264,128]{2,1,0:T(8,128)S(1)}, u32[]{:S(2)}, u32[]{:S(2)}) collective-permute-start(f32[4,264,128]{2,1,0:T(8,128)S(1)} %collective-permute-done.5.refs_1_), channel_id=1, source_target_pairs={{0,32},{8,104},{16,112},{24,56},{32,64},{40,8},{48,16},{56,88},{64... | collective-permute-start | bytes 1622024 | tf_op jit(solution)/shard_map/ppermute | solution.py:427
  133.1 20.1 %collective-permute-start.15 = (f32[256,512]{1,0:T(8,128)S(1)}, f32[256,512]{1,0:T(8,128)S(1)}, u32[]{:S(2)}, u32[]{:S(2)}) collective-permute-start(f32[256,512]{1,0:T(8,128)S(1)} %get-tuple-element.42), channel_id=1, source_target_pairs={{0,8},{8,16},{16,24},{24,0},{32,40},{40,48},{48,56},{56,32},{64,72... | collective-permute-start | bytes 1572872 | tf_op jit(solution)/shard_map/ppermute | solution.py:454
  139.2 25.9 %collective-permute-start.16 = (f32[256,512]{1,0:T(8,128)S(1)}, f32[256,512]{1,0:T(8,128)S(1)}, u32[]{:S(2)}, u32[]{:S(2)}) collective-permute-start(f32[256,512]{1,0:T(8,128)S(1)} %get-tuple-element.43), channel_id=1, source_target_pairs={{0,16},{8,24},{16,0},{24,8},{32,48},{40,56},{48,32},{56,40},{64,80... | collective-permute-start | bytes 1572872 | tf_op jit(solution)/shard_map/ppermute | solution.py:454
  142.8 22.3 %collective-permute-start.17 = (f32[256,512]{1,0:T(8,128)S(1)}, f32[256,512]{1,0:T(8,128)S(1)}, u32[]{:S(2)}, u32[]{:S(2)}) collective-permute-start(f32[256,512]{1,0:T(8,128)S(1)} %get-tuple-element.44), channel_id=1, source_target_pairs={{0,24},{8,0},{16,8},{24,16},{32,56},{40,32},{48,40},{56,48},{64,88... | collective-permute-start | bytes 1572872 | tf_op jit(solution)/shard_map/ppermute | solution.py:454
  (6 other events, 13.2 us)

commit v4 on v3

--- a/solution.py
+++ b/solution.py
@@ -175,6 +175,19 @@
         pltpu.make_async_copy(ins[s], halves[0].at[0], half_sems.at[s]).wait()
 
 
+def edge_kernel(ids, *refs):
+    ins, halves, sems = refs[:RING], refs[RING:RING + 2], refs[RING + 2]
+    z = lax.rem(ids[0], RING)
+    for s in range(RING):
+        t = lax.rem(z - s + RING, RING)
+        for h in range(2):
+            @pl.when(t // 2 == h)
+            def _(s=s, t=t, h=h):
+                pltpu.make_async_copy(ins[s], halves[h].at[t - 2 * h], sems.at[s]).start()
+    for s in range(RING):
+        pltpu.make_async_copy(ins[s], halves[0].at[0], sems.at[s]).wait()
+
+
 def expand_kernel(ids, *refs):
     msgs = refs[:6]
     w_ref, c_ref, vs = refs[6:]
@@ -224,8 +237,8 @@
 
 
 def step_kernel(ids, *refs):
-    ins, w, packed, outs = refs[:8], refs[8], refs[9], refs[10:14]
-    x0, x1, rain, r_a, r_b, r_c, r_d, final, c, sems = refs[14:]
+    ins, side, w, packed, outs = refs[:4], refs[4:6], refs[6], refs[7], refs[8:12]
+    x0, x1, rain, r_a, r_b, r_c, r_d, final, c, sems = refs[12:]
     z = lax.rem(ids[0], RING)
     upper = lax.broadcasted_iota(jnp.int32, (8, 2 * SPAN), 0) < 4
 
@@ -237,18 +250,16 @@
     pad = jnp.zeros((2 * ROWS, SPAN), BF16)
     x0[:, :SPAN] = pad
     x0[:, (2 * PAIRS + 1) * SPAN:] = pad
-    at = 0
-    for halo in (False, True):
-        for s in range(RING):
-            base = window_base(z, s, halo)
-            for t in range(WIDTH // SPAN):
-                lanes = pl.ds(pl.multiple_of((base + 1 + t) * SPAN, SPAN), SPAN)
-                v = ins[at][t, :ROWS, :]
-                hi = v.astype(BF16)
-                x0[:ROWS, lanes] = hi
-                x0[ROWS:, lanes] = (v - hi.astype(F32)).astype(BF16)
-                rain[:, pl.ds(pl.multiple_of((base + t) * SPAN, SPAN), SPAN)] = ins[at][t, ROWS:, :]
-            at += 1
+    tiles = [(ins[s], window_base(z, s, False)) for s in range(RING)]
+    tiles += [(side[0].at[t], 24 + 4 * t) for t in range(2)] + [(side[1].at[t], 4 * t) for t in range(2)]
+    for src, base in tiles:
+        for t in range(WIDTH // SPAN):
+            lanes = pl.ds(pl.multiple_of((base + 1 + t) * SPAN, SPAN), SPAN)
+            v = src[t, :ROWS, :]
+            hi = v.astype(BF16)
+            x0[:ROWS, lanes] = hi
+            x0[ROWS:, lanes] = (v - hi.astype(F32)).astype(BF16)
+            rain[:, pl.ds(pl.multiple_of((base + t) * SPAN, SPAN), SPAN)] = src[t, ROWS:, :]
 
     def product(k, x, r):
         lanes = pl.ds(pl.multiple_of(k * 2 * SPAN, 2 * SPAN), 4 * SPAN)
@@ -424,7 +435,16 @@
     c_all = []
     for c in c_parts:
         c_all += [c, lax.ppermute(c, "dom", core_pairs())]
-    side = [lax.ppermute(ring[s], "tile", x_pairs(s)) for s in range(RING)]
+    state = (WIDTH // SPAN, ROWS + 8, SPAN)
+    low, high = pl.pallas_call(
+        edge_kernel,
+        out_shape=[shape((2, *state)), shape((2, *state))],
+        in_specs=[SMEM] + [ANY] * RING,
+        out_specs=[ANY] * 2,
+        scratch_shapes=[pltpu.SemaphoreType.DMA((RING,))],
+        compiler_params=params(4),
+    )(ids, *ring)
+    side = [lax.ppermute(low, "tile", row_pairs(-1)), lax.ppermute(high, "tile", row_pairs(1))]
 
     coefs = pl.pallas_call(
         expand_kernel,
@@ -438,7 +458,7 @@
     back = pl.pallas_call(
         step_kernel,
         out_shape=[shape((ROWS, WIDTH))] * RING,
-        in_specs=[SMEM] + [VMEM] * 10,
+        in_specs=[SMEM] + [VMEM] * 8,
         out_specs=[ANY] * RING,
         scratch_shapes=[pltpu.VMEM((2 * ROWS, (2 * PAIRS + 2) * SPAN), BF16)] * 2
         + [pltpu.VMEM((8, 2 * PAIRS * SPAN), F32)]

time: 168 us -> 165 us (0.982)
  starting transfers between devices: 35.4 us -> 27.1 us
  waiting for transfers between devices: 76.4 us -> 81.5 us
    ppermute x3, starting transfers between devices: 9.63 us -> 4.56 us  [shards(): lax.ppermute(back[s], 'tile', z_pairs(s))]
    ppermute x4 -> x2, waiting for transfers between devices: 9.52 us -> 14.1 us  [the longest x1 10.7 us: shards(): lax.ppermute(low, 'tile', row_pairs(-1))]
    ppermute x4 -> x2, starting transfers between devices: 6.19 us -> 3.02 us  [the longest x1 3.02 us: shards(): lax.ppermute(low, 'tile', row_pairs(-1))]
  transfers between devices with their start and end apart: 19 -> 17, of which waited for: 10 -> 11; matrix products, arithmetic and copies ran while one was open for 0% -> 0% of each run, Pallas kernels for 5% -> 6%
where the time goes in v4:
time: 165 us
  waiting for transfers between devices  81.5 us (49%)
  Pallas kernels  47.5 us (29%)
  starting transfers between devices  27.1 us (16%)
  local copies, waits for them, and re-layouts  8.47 us (5%)
    pallas_call x1, Pallas kernels, shards(): pl.pallas_call(step_kernel, out_shape=[shape((ROWS, WIDTH))] * RING, in_s...  32.2 us
    ppermute x3, waiting for transfers between devices, shards(): lax.ppermute(back[s], 'tile', z_pairs(s))  22 us
    ppermute x3, waiting for transfers between devices, shards(): lax.ppermute(coeff, 'tile', z_pairs(s))  19.7 us
    ppermute x1, waiting for transfers between devices, shards(): lax.ppermute(c_low, 'tile', row_pairs(-1))  13.3 us
    ppermute x1, waiting for transfers between devices, shards(): lax.ppermute(low, 'tile', row_pairs(-1))  10.7 us
    unnamed x22, local copies, waits for them, and re-layouts  8.47 us
    ppermute x3, starting transfers between devices, shards(): lax.ppermute(coeff, 'tile', z_pairs(s))  6.58 us
    ppermute x3, waiting for transfers between devices, shards(): lax.ppermute(mine[s], 'tile', z_pairs(s))  5.54 us
  transfers between devices with their start and end apart: 17, of which 11 were waited for; matrix products, arithmetic and copies ran while one was open for 0% of the time, Pallas kernels for 6%

profile of v4, /device:TPU:0, one launch (start us, length us, event | category | flops | bytes accessed | tf_op | source)
XLA Modules:
  0.0 165.0 jit_solution(14913939265454493196)
XLA Ops:
  2.3 3.2 %shard_map.64.after = f32[16,64,512]{2,1,0:T(8,128)} custom-call(s32[2]{0:T(128)S(1)} %pad_add_fusion.ids, s32[128]{0:T(128)S(1)} %copy-done.9, f32[1024,512]{1,0:T(8,128)S(1)} %bitcast.4), custom_call_target="tpu_custom_call" | custom-call | tf_op jit(solution)/shard_map/pallas_call | solution.py:387
  5.6 4.7 %all-to-all-start = ((f32[16,64,512]{2,1,0:T(8,128)}), f32[16,64,512]{2,1,0:T(8,128)S(1)}, u32[]{:S(2)}, u32[]{:S(2)}) async-start(f32[16,64,512]{2,1,0:T(8,128)} %shard_map.64.after), calls=%async_computation | async-start | bytes 4194304 | tf_op jit(solution)/shard_map/all_to_all | solution.py:417
  11.1 2.0 %collective-permute-start = (f32[896,128]{1,0:T(8,128)S(1)}, f32[896,128]{1,0:T(8,128)S(1)}, u32[]{:S(2)}, u32[]{:S(2)}) collective-permute-start(f32[896,128]{1,0:T(8,128)S(1)} %shard_map.65.refs_0_), channel_id=1, source_target_pairs={{0,8},{8,16},{16,24},{24,0},{32,40},{40,48},{48,56},{56,32},{64,72... | collective-permute-start | bytes 1376264 | tf_op jit(solution)/shard_map/ppermute | solution.py:407
  13.1 3.6 %collective-permute-start.1 = (f32[896,128]{1,0:T(8,128)S(1)}, f32[896,128]{1,0:T(8,128)S(1)}, u32[]{:S(2)}, u32[]{:S(2)}) collective-permute-start(f32[896,128]{1,0:T(8,128)S(1)} %shard_map.65.refs_0_), channel_id=1, source_target_pairs={{0,16},{8,24},{16,0},{24,8},{32,48},{40,56},{48,32},{56,40},{64,80... | collective-permute-start | bytes 1376264 | tf_op jit(solution)/shard_map/ppermute | solution.py:407
  17.7 8.7 %collective-permute-done.refs_1_ = f32[896,128]{1,0:T(8,128)S(1)} collective-permute-done((f32[896,128]{1,0:T(8,128)S(1)}, f32[896,128]{1,0:T(8,128)S(1)}, u32[]{:S(2)}, u32[]{:S(2)}) %collective-permute-start) | collective-permute-done | bytes 458784 | tf_op jit(solution)/shard_map/ppermute | solution.py:407
  26.4 11.0 %collective-permute-done.1.refs_2_ = f32[896,128]{1,0:T(8,128)S(1)} collective-permute-done((f32[896,128]{1,0:T(8,128)S(1)}, f32[896,128]{1,0:T(8,128)S(1)}, u32[]{:S(2)}, u32[]{:S(2)}) %collective-permute-start.1) | collective-permute-done | bytes 458784 | tf_op jit(solution)/shard_map/ppermute | solution.py:407
  37.4 2.5 %shard_map.66 = (f32[4,896,128]{2,1,0:T(8,128)S(1)}, f32[2,896,128]{2,1,0:T(8,128)}, f32[2,896,128]{2,1,0:T(8,128)}) custom-call(s32[2]{0:T(128)S(1)} %pad_add_fusion.ids, f32[896,128]{1,0:T(8,128)S(1)} %shard_map.65.refs_0_, f32[896,128]{1,0:T(8,128)S(1)} %collective-permute-done.refs_1_, f32[896,128]{1,0:T(8,128)S(1)} %collective-permute-done.1.refs_2_, ...), custom_call_target="tpu_custom_call" | custom-call | tf_op jit(solution)/shard_map/pallas_call | solution.py:408
  41.2 2.8 %collective-permute-start.3 = (f32[2,896,128]{2,1,0:T(8,128)}, f32[2,896,128]{2,1,0:T(8,128)S(1)}, u32[]{:S(2)}, u32[]{:S(2)}) collective-permute-start(f32[2,896,128]{2,1,0:T(8,128)} %get-tuple-element.28), channel_id=1, source_target_pairs={{0,96},{8,104},{16,112},{24,120},{32,0},{40,8},{48,16},{56,24},{64... | collective-permute-start | bytes 2752520 | tf_op jit(solution)/shard_map/ppermute | solution.py:416
  46.9 2.4 %collective-permute-start.6 = (f32[4,264,128]{2,1,0:T(8,128)S(1)}, f32[4,264,128]{2,1,0:T(8,128)S(1)}, u32[]{:S(2)}, u32[]{:S(2)}) collective-permute-start(f32[4,264,128]{2,1,0:T(8,128)S(1)} %get-tuple-element.32), channel_id=1, source_target_pairs={{0,16},{8,24},{16,0},{24,8},{32,48},{40,56},{48,32},{56,40},{64,80... | collective-permute-start | bytes 1622024 | tf_op jit(solution)/shard_map/ppermute | solution.py:433
  50.5 13.3 %collective-permute-done.3.refs_2_ = f32[2,896,128]{2,1,0:T(8,128)S(1)} collective-permute-done((f32[2,896,128]{2,1,0:T(8,128)}, f32[2,896,128]{2,1,0:T(8,128)S(1)}, u32[]{:S(2)}, u32[]{:S(2)}) %collective-permute-start.3) | collective-permute-done | bytes 917536 | tf_op jit(solution)/shard_map/ppermute | solution.py:416
  63.8 3.4 %collective-permute-done.4.refs_4_ = f32[2,896,128]{2,1,0:T(8,128)} collective-permute-done((f32[2,896,128]{2,1,0:T(8,128)}, f32[2,896,128]{2,1,0:T(8,128)}, u32[]{:S(2)}, u32[]{:S(2)}) %collective-permute-start.4) | collective-permute-done | bytes 917536 | tf_op jit(solution)/shard_map/ppermute | solution.py:416
  67.2 5.5 %collective-permute-done.6.refs_2_ = f32[4,264,128]{2,1,0:T(8,128)S(1)} collective-permute-done((f32[4,264,128]{2,1,0:T(8,128)S(1)}, f32[4,264,128]{2,1,0:T(8,128)S(1)}, u32[]{:S(2)}, u32[]{:S(2)}) %collective-permute-start.6) | collective-permute-done | bytes 540704 | tf_op jit(solution)/shard_map/ppermute | solution.py:433
  73.7 3.0 %collective-permute-start.8 = (f32[2,4,264,128]{3,2,1,0:T(8,128)S(1)}, f32[2,4,264,128]{3,2,1,0:T(8,128)S(1)}, u32[]{:S(2)}, u32[]{:S(2)}) collective-permute-start(f32[2,4,264,128]{3,2,1,0:T(8,128)S(1)} %get-tuple-element.38), channel_id=1, source_target_pairs={{0,96},{8,104},{16,112},{24,120},{32,0},{40,8},{48,16},{56,24},{64... | collective-permute-start | bytes 3244040 | tf_op jit(solution)/shard_map/ppermute | solution.py:447
  77.2 2.0 %collective-permute-done.11.refs_3_ = f32[2,896,128]{2,1,0:T(8,128)S(1)} collective-permute-done((f32[2,896,128]{2,1,0:T(8,128)S(1)}, f32[2,896,128]{2,1,0:T(8,128)S(1)}, u32[]{:S(2)}, u32[]{:S(2)}) %collective-permute-start.11) | collective-permute-done | bytes 917536 | tf_op jit(solution)/shard_map/ppermute | solution.py:437
  80.7 4.2 %shard_map.69 = (bf16[16,2,512,256]{3,2,1,0:T(8,128)(2,1)S(1)}, f32[16,200,256]{2,1,0:T(8,128)S(1)}) custom-call(s32[2]{0:T(128)S(1)} %pad_add_fusion.ids, f32[4,896,128]{2,1,0:T(8,128)S(1)} %copy-done.4, f32[4,896,128]{2,1,0:T(8,128)S(1)} %collective-permute-done.10.refs_1_, f32[2,896,128]{2,1,0:T(8,128)S(1)} %collective-permute-done.3.refs_2_, ...), custom_call_target="tpu_custom_call" | custom-call | tf_op jit(solution)/shard_map/pallas_call | solution.py:449
  84.9 3.3 %copy-done = bf16[16,2,512,256]{3,2,1,0:T(8,128)(2,1)} copy-done((bf16[16,2,512,256]{3,2,1,0:T(8,128)(2,1)}, bf16[16,2,512,256]{3,2,1,0:T(8,128)(2,1)S(1)}, u32[]{:S(2)}) %copy-start) | copy-done | bytes 8388632
  88.1 1.7 %copy-done.1 = f32[16,200,256]{2,1,0:T(8,128)} copy-done((f32[16,200,256]{2,1,0:T(8,128)}, f32[16,200,256]{2,1,0:T(8,128)S(1)}, u32[]{:S(2)}) %copy-start.1) | copy-done | bytes 3276824
  89.8 10.7 %collective-permute-done.8.refs_4_ = f32[2,4,264,128]{3,2,1,0:T(8,128)S(1)} collective-permute-done((f32[2,4,264,128]{3,2,1,0:T(8,128)S(1)}, f32[2,4,264,128]{3,2,1,0:T(8,128)S(1)}, u32[]{:S(2)}, u32[]{:S(2)}) %collective-permute-start.8) | collective-permute-done | bytes 1081376 | tf_op jit(solution)/shard_map/ppermute | solution.py:447
  100.5 3.4 %collective-permute-done.9.refs_5_ = f32[2,4,264,128]{3,2,1,0:T(8,128)S(1)} collective-permute-done((f32[2,4,264,128]{3,2,1,0:T(8,128)S(1)}, f32[2,4,264,128]{3,2,1,0:T(8,128)S(1)}, u32[]{:S(2)}, u32[]{:S(2)}) %collective-permute-start.9) | collective-permute-done | bytes 1081376 | tf_op jit(solution)/shard_map/ppermute | solution.py:447
  103.9 32.2 %shard_map.70 = (f32[256,512]{1,0:T(8,128)S(1)}, f32[256,512]{1,0:T(8,128)S(1)}, f32[256,512]{1,0:T(8,128)S(1)}, f32[256,512]{1,0:T(8,128)S(1)}) custom-call(s32[2]{0:T(128)S(1)} %pad_add_fusion.ids, f32[4,264,128]{2,1,0:T(8,128)S(1)} %get-tuple-element.34.refs_0_, f32[4,264,128]{2,1,0:T(8,128)S(1)} %collective-permute-done.5.refs_1_, ...), custom_call_target="tpu_custom_call" | custom-call | tf_op jit(solution)/shard_map/pallas_call | solution.py:458
  137.4 2.8 %collective-permute-start.14 = (f32[256,512]{1,0:T(8,128)S(1)}, f32[256,512]{1,0:T(8,128)S(1)}, u32[]{:S(2)}, u32[]{:S(2)}) collective-permute-start(f32[256,512]{1,0:T(8,128)S(1)} %get-tuple-element.47), channel_id=1, source_target_pairs={{0,16},{8,24},{16,0},{24,8},{32,48},{40,56},{48,32},{56,40},{64,80... | collective-permute-start | bytes 1572872 | tf_op jit(solution)/shard_map/ppermute | solution.py:474
  140.7 10.8 %collective-permute-done.13.refs_1_ = f32[256,512]{1,0:T(8,128)S(1)} collective-permute-done((f32[256,512]{1,0:T(8,128)S(1)}, f32[256,512]{1,0:T(8,128)S(1)}, u32[]{:S(2)}, u32[]{:S(2)}) %collective-permute-start.13) | collective-permute-done | bytes 524320 | tf_op jit(solution)/shard_map/ppermute | solution.py:474
  151.5 11.2 %collective-permute-done.14.refs_2_ = f32[256,512]{1,0:T(8,128)S(1)} collective-permute-done((f32[256,512]{1,0:T(8,128)S(1)}, f32[256,512]{1,0:T(8,128)S(1)}, u32[]{:S(2)}, u32[]{:S(2)}) %collective-permute-start.14) | collective-permute-done | bytes 524320 | tf_op jit(solution)/shard_map/ppermute | solution.py:474
  162.7 2.2 %shard_map.71 = f32[64,16,512]{2,1,0:T(8,128)} custom-call(s32[2]{0:T(128)S(1)} %pad_add_fusion.ids, f32[256,512]{1,0:T(8,128)S(1)} %get-tuple-element.45.refs_0_, f32[256,512]{1,0:T(8,128)S(1)} %collective-permute-done.13.refs_1_, f32[256,512]{1,0:T(8,128)S(1)} %collective-permute-done.14.refs_2_, f32[256,512]{1,0:T(8,128)S(1)} %collective-permute-done.15.refs_3_), custom_call_target="tpu_custom_call" | custom-call | tf_op jit(solution)/shard_map/pallas_call | solution.py:475
  (41 shorter events, 14.2 us)
Async XLA Ops:
  5.5 4.7 %copy-start.5 = (f32[4,3,128,128]{3,2,1,0:T(8,128)S(1)}, f32[4,3,128,128]{3,2,1,0:T(8,128)}, u32[]{:S(2)}) copy-start(f32[4,3,128,128]{3,2,1,0:T(8,128)} %cond.1) | copy-start | bytes 2359300
  5.5 4.7 %copy-start.6 = (f32[63,512]{1,0:T(8,128)S(1)}, f32[63,512]{1,0:T(8,128)}, u32[]{:S(2)}) copy-start(f32[63,512]{1,0:T(8,128)} %vert.1) | copy-start | bytes 387076
  5.5 4.7 %copy-start.8 = (s32[64,3]{0,1:T(4,128)S(1)}, s32[64,3]{0,1:T(4,128)}, u32[]{:S(2)}) copy-start(s32[64,3]{0,1:T(4,128)} %param.8) | copy-start | bytes 2308
  5.6 38.4 %all-to-all-start = ((f32[16,64,512]{2,1,0:T(8,128)}), f32[16,64,512]{2,1,0:T(8,128)S(1)}, u32[]{:S(2)}, u32[]{:S(2)}) async-start(f32[16,64,512]{2,1,0:T(8,128)} %shard_map.64.after), calls=%async_computation | async-start | bytes 4194304 | tf_op jit(solution)/shard_map/all_to_all | solution.py:417
  10.3 33.7 %copy-start.7 = (f32[16,512]{1,0:T(8,128)S(1)}, f32[16,512]{1,0:T(8,128)}, u32[]{:S(2)}) copy-start(f32[16,512]{1,0:T(8,128)} %rain.1) | copy-start | bytes 98308
  10.3 33.7 %copy-start.10 = (s32[128]{0:T(128)S(1)}, s32[128]{0:T(128)}, u32[]{:S(2)}) copy-start(s32[128]{0:T(128)} %anc.3) | copy-start | bytes 1540
  11.1 15.3 %collective-permute-start = (f32[896,128]{1,0:T(8,128)S(1)}, f32[896,128]{1,0:T(8,128)S(1)}, u32[]{:S(2)}, u32[]{:S(2)}) collective-permute-start(f32[896,128]{1,0:T(8,128)S(1)} %shard_map.65.refs_0_), channel_id=1, source_target_pairs={{0,8},{8,16},{16,24},{24,0},{32,40},{40,48},{48,56},{56,32},{64,72... | collective-permute-start | bytes 1376264 | tf_op jit(solution)/shard_map/ppermute | solution.py:407
  13.1 24.3 %collective-permute-start.1 = (f32[896,128]{1,0:T(8,128)S(1)}, f32[896,128]{1,0:T(8,128)S(1)}, u32[]{:S(2)}, u32[]{:S(2)}) collective-permute-start(f32[896,128]{1,0:T(8,128)S(1)} %shard_map.65.refs_0_), channel_id=1, source_target_pairs={{0,16},{8,24},{16,0},{24,8},{32,48},{40,56},{48,32},{56,40},{64,80... | collective-permute-start | bytes 1376264 | tf_op jit(solution)/shard_map/ppermute | solution.py:407
  16.7 20.7 %collective-permute-start.2 = (f32[896,128]{1,0:T(8,128)S(1)}, f32[896,128]{1,0:T(8,128)S(1)}, u32[]{:S(2)}, u32[]{:S(2)}) collective-permute-start(f32[896,128]{1,0:T(8,128)S(1)} %shard_map.65.refs_0_), channel_id=1, source_target_pairs={{0,24},{8,0},{16,8},{24,16},{32,56},{40,32},{48,40},{56,48},{64,88... | collective-permute-start | bytes 1376264 | tf_op jit(solution)/shard_map/ppermute | solution.py:407
  41.2 22.6 %collective-permute-start.3 = (f32[2,896,128]{2,1,0:T(8,128)}, f32[2,896,128]{2,1,0:T(8,128)S(1)}, u32[]{:S(2)}, u32[]{:S(2)}) collective-permute-start(f32[2,896,128]{2,1,0:T(8,128)} %get-tuple-element.28), channel_id=1, source_target_pairs={{0,96},{8,104},{16,112},{24,120},{32,0},{40,8},{48,16},{56,24},{64... | collective-permute-start | bytes 2752520 | tf_op jit(solution)/shard_map/ppermute | solution.py:416
  44.0 23.2 %collective-permute-start.4 = (f32[2,896,128]{2,1,0:T(8,128)}, f32[2,896,128]{2,1,0:T(8,128)}, u32[]{:S(2)}, u32[]{:S(2)}) collective-permute-start(f32[2,896,128]{2,1,0:T(8,128)} %get-tuple-element.29), channel_id=1, source_target_pairs={{0,32},{8,40},{16,48},{24,56},{32,64},{40,72},{48,80},{56,88},{64,... | collective-permute-start | bytes 2752520 | tf_op jit(solution)/shard_map/ppermute | solution.py:416
  44.0 28.7 %copy-start.4 = (f32[4,896,128]{2,1,0:T(8,128)S(1)}, f32[4,896,128]{2,1,0:T(8,128)}, u32[]{:S(2)}) copy-start(f32[4,896,128]{2,1,0:T(8,128)} %copy-done.3) | copy-start | bytes 5505028
  45.6 21.6 %collective-permute-start.5 = (f32[4,264,128]{2,1,0:T(8,128)S(1)}, f32[4,264,128]{2,1,0:T(8,128)S(1)}, u32[]{:S(2)}, u32[]{:S(2)}) collective-permute-start(f32[4,264,128]{2,1,0:T(8,128)S(1)} %get-tuple-element.31), channel_id=1, source_target_pairs={{0,8},{8,16},{16,24},{24,0},{32,40},{40,48},{48,56},{56,32},{64,72... | collective-permute-start | bytes 1622024 | tf_op jit(solution)/shard_map/ppermute | solution.py:433
  46.9 25.9 %collective-permute-start.6 = (f32[4,264,128]{2,1,0:T(8,128)S(1)}, f32[4,264,128]{2,1,0:T(8,128)S(1)}, u32[]{:S(2)}, u32[]{:S(2)}) collective-permute-start(f32[4,264,128]{2,1,0:T(8,128)S(1)} %get-tuple-element.32), channel_id=1, source_target_pairs={{0,16},{8,24},{16,0},{24,8},{32,48},{40,56},{48,32},{56,40},{64,80... | collective-permute-start | bytes 1622024 | tf_op jit(solution)/shard_map/ppermute | solution.py:433
  49.3 23.5 %collective-permute-start.7 = (f32[4,264,128]{2,1,0:T(8,128)S(1)}, f32[4,264,128]{2,1,0:T(8,128)S(1)}, u32[]{:S(2)}, u32[]{:S(2)}) collective-permute-start(f32[4,264,128]{2,1,0:T(8,128)S(1)} %get-tuple-element.33), channel_id=1, source_target_pairs={{0,24},{8,0},{16,8},{24,16},{32,56},{40,32},{48,40},{56,48},{64,88... | collective-permute-start | bytes 1622024 | tf_op jit(solution)/shard_map/ppermute | solution.py:433
  72.8 7.9 %collective-permute-start.10 = (f32[4,896,128]{2,1,0:T(8,128)S(1)}, f32[4,896,128]{2,1,0:T(8,128)S(1)}, u32[]{:S(2)}, u32[]{:S(2)}) collective-permute-start(f32[4,896,128]{2,1,0:T(8,128)S(1)} %copy-done.4), channel_id=1, source_target_pairs={{0,1},{1,0},{2,3},{3,2},{4,5},{5,4},{6,7},{7,6},{8,9},{9,8},{10,11... | collective-permute-start | bytes 5505032 | tf_op jit(solution)/shard_map/ppermute | solution.py:437
  73.7 26.8 %collective-permute-start.8 = (f32[2,4,264,128]{3,2,1,0:T(8,128)S(1)}, f32[2,4,264,128]{3,2,1,0:T(8,128)S(1)}, u32[]{:S(2)}, u32[]{:S(2)}) collective-permute-start(f32[2,4,264,128]{3,2,1,0:T(8,128)S(1)} %get-tuple-element.38), channel_id=1, source_target_pairs={{0,96},{8,104},{16,112},{24,120},{32,0},{40,8},{48,16},{56,24},{64... | collective-permute-start | bytes 3244040 | tf_op jit(solution)/shard_map/ppermute | solution.py:447
  76.7 27.2 %collective-permute-start.9 = (f32[2,4,264,128]{3,2,1,0:T(8,128)S(1)}, f32[2,4,264,128]{3,2,1,0:T(8,128)S(1)}, u32[]{:S(2)}, u32[]{:S(2)}) collective-permute-start(f32[2,4,264,128]{3,2,1,0:T(8,128)S(1)} %get-tuple-element.39), channel_id=1, source_target_pairs={{0,32},{8,40},{16,48},{24,56},{32,64},{40,72},{48,80},{56,88},{64,... | collective-permute-start | bytes 3244040 | tf_op jit(solution)/shard_map/ppermute | solution.py:447
  76.7 2.5 %collective-permute-start.11 = (f32[2,896,128]{2,1,0:T(8,128)S(1)}, f32[2,896,128]{2,1,0:T(8,128)S(1)}, u32[]{:S(2)}, u32[]{:S(2)}) collective-permute-start(f32[2,896,128]{2,1,0:T(8,128)S(1)} %collective-permute-done.3.refs_2_), channel_id=1, source_target_pairs={{0,1},{1,0},{2,3},{3,2},{4,5},{5,4},{6,7},{7,6},{8,9},{9,8},{10,11... | collective-permute-start | bytes 2752520 | tf_op jit(solution)/shard_map/ppermute | solution.py:437
  76.9 3.8 %collective-permute-start.12 = (f32[2,896,128]{2,1,0:T(8,128)}, f32[2,896,128]{2,1,0:T(8,128)S(1)}, u32[]{:S(2)}, u32[]{:S(2)}) collective-permute-start(f32[2,896,128]{2,1,0:T(8,128)} %collective-permute-done.4.refs_4_), channel_id=1, source_target_pairs={{0,1},{1,0},{2,3},{3,2},{4,5},{5,4},{6,7},{7,6},{8,9},{9,8},{10,11... | collective-permute-start | bytes 2752520 | tf_op jit(solution)/shard_map/ppermute | solution.py:437
  84.9 3.3 %copy-start = (bf16[16,2,512,256]{3,2,1,0:T(8,128)(2,1)}, bf16[16,2,512,256]{3,2,1,0:T(8,128)(2,1)S(1)}, u32[]{:S(2)}) copy-start(bf16[16,2,512,256]{3,2,1,0:T(8,128)(2,1)S(1)} %get-tuple-element.43.refs_6_) | copy-start | bytes 25165828
  136.1 15.4 %collective-permute-start.13 = (f32[256,512]{1,0:T(8,128)S(1)}, f32[256,512]{1,0:T(8,128)S(1)}, u32[]{:S(2)}, u32[]{:S(2)}) collective-permute-start(f32[256,512]{1,0:T(8,128)S(1)} %get-tuple-element.46), channel_id=1, source_target_pairs={{0,8},{8,16},{16,24},{24,0},{32,40},{40,48},{48,56},{56,32},{64,72... | collective-permute-start | bytes 1572872 | tf_op jit(solution)/shard_map/ppermute | solution.py:474
  137.4 25.3 %collective-permute-start.14 = (f32[256,512]{1,0:T(8,128)S(1)}, f32[256,512]{1,0:T(8,128)S(1)}, u32[]{:S(2)}, u32[]{:S(2)}) collective-permute-start(f32[256,512]{1,0:T(8,128)S(1)} %get-tuple-element.47), channel_id=1, source_target_pairs={{0,16},{8,24},{16,0},{24,8},{32,48},{40,56},{48,32},{56,40},{64,80... | collective-permute-start | bytes 1572872 | tf_op jit(solution)/shard_map/ppermute | solution.py:474
  140.2 22.4 %collective-permute-start.15 = (f32[256,512]{1,0:T(8,128)S(1)}, f32[256,512]{1,0:T(8,128)S(1)}, u32[]{:S(2)}, u32[]{:S(2)}) collective-permute-start(f32[256,512]{1,0:T(8,128)S(1)} %get-tuple-element.48), channel_id=1, source_target_pairs={{0,24},{8,0},{16,8},{24,16},{32,56},{40,32},{48,40},{56,48},{64,88... | collective-permute-start | bytes 1572872 | tf_op jit(solution)/shard_map/ppermute | solution.py:474
  (4 other events, 5.2 us)

commit v5 on v4

--- a/solution.py
+++ b/solution.py
@@ -158,23 +158,6 @@
     return 8 + 4 * t
 
 
-def order_kernel(ids, *refs):
-    ins, tiles, halves, sems, half_sems = refs[:RING], refs[RING], refs[RING + 1:RING + 3], refs[RING + 3], refs[RING + 4]
-    z = lax.rem(ids[0], RING)
-    copies = []
-    for s in range(RING):
-        t = lax.rem(z - s + RING, RING)
-        copies.append(pltpu.make_async_copy(ins[s], tiles.at[t], sems.at[s]))
-        copies[-1].start()
-        for h in range(2):
-            @pl.when(t // 2 == h)
-            def _(s=s, t=t, h=h):
-                pltpu.make_async_copy(ins[s], halves[h].at[t - 2 * h], half_sems.at[s]).start()
-    for s in range(RING):
-        copies[s].wait()
-        pltpu.make_async_copy(ins[s], halves[0].at[0], half_sems.at[s]).wait()
-
-
 def edge_kernel(ids, *refs):
     ins, halves, sems = refs[:RING], refs[RING:RING + 2], refs[RING + 2]
     z = lax.rem(ids[0], RING)
@@ -189,11 +172,11 @@
 
 
 def expand_kernel(ids, *refs):
-    msgs = refs[:6]
-    w_ref, c_ref, vs = refs[6:]
+    msgs = refs[:8]
+    w_ref, c_ref, vs = refs[8:]
     core = lax.rem(ids[1], 2)
-    for part, (start, tiles) in enumerate(((4, 4), (12, 2), (0, 2))):
-        for at in range(tiles):
+    for part, start in enumerate((4, 8, 12, 0)):
+        for at in range(2):
             for other in range(2):
                 msg = msgs[2 * part + other]
                 k = start + 2 * at + (core if other == 0 else 1 - core)
@@ -405,15 +388,15 @@
         compiler_params=params(8),
     )(ids, adjacency.T, conductance, vertical, sent)
     c_ring = [coeff] + [lax.ppermute(coeff, "tile", z_pairs(s)) for s in range(1, RING)]
-    c_tiles, c_low, c_high = pl.pallas_call(
-        order_kernel,
-        out_shape=[shape((RING, MSG, SPAN)), shape((2, MSG, SPAN)), shape((2, MSG, SPAN))],
+    c_low, c_high = pl.pallas_call(
+        edge_kernel,
+        out_shape=[shape((2, MSG, SPAN))] * 2,
         in_specs=[SMEM] + [ANY] * RING,
-        out_specs=[ANY] * 3,
-        scratch_shapes=[pltpu.SemaphoreType.DMA((RING,)), pltpu.SemaphoreType.DMA((RING,))],
+        out_specs=[ANY] * 2,
+        scratch_shapes=[pltpu.SemaphoreType.DMA((RING,))],
         compiler_params=params(4),
     )(ids, *c_ring)
-    c_parts = [c_tiles, lax.ppermute(c_low, "tile", row_pairs(-1)), lax.ppermute(c_high, "tile", row_pairs(1))]
+    c_parts = [c_low, c_high, lax.ppermute(c_low, "tile", row_pairs(-1)), lax.ppermute(c_high, "tile", row_pairs(1))]
     got = lax.all_to_all(sent, "dom", split_axis=0, concat_axis=0, tiled=True)
 
     mine = pl.pallas_call(
@@ -449,7 +432,7 @@
     coefs = pl.pallas_call(
         expand_kernel,
         out_shape=[shape((PAIRS, 2, 4 * SPAN, 2 * SPAN), BF16), shape((PAIRS, 6 * HALF + 8, 2 * SPAN))],
-        in_specs=[SMEM] + [VMEM] * 6,
+        in_specs=[SMEM] + [VMEM] * 8,
         out_specs=[VMEM] * 2,
         scratch_shapes=[pltpu.VMEM((PAIRS, LAYERS, 2 * SPAN), F32)],
         compiler_params=params(26),

time: 165 us -> 163 us (0.988)
    ppermute x1, waiting for transfers between devices: 10.7 us -> 8.8 us  [shards(): lax.ppermute(low, 'tile', row_pairs(-1))]
    unnamed x22 -> x18, local copies, waits for them, and re-layouts: 8.47 us -> 7.21 us
    ppermute x3 -> x4, waiting for transfers between devices: 3.49 us -> 4.57 us  [shards(): c_all += [c, lax.ppermute(c, 'dom', core_pairs())]]
  transfers between devices with their start and end apart: 17 -> 18, of which waited for: 11 -> 13; matrix products, arithmetic and copies ran while one was open for 0% -> 0% of each run, Pallas kernels for 6% -> 6%
where the time goes in v5:
time: 163 us
  waiting for transfers between devices  80.4 us (49%)
  Pallas kernels  47.4 us (29%)
  starting transfers between devices  27.7 us (17%)
  local copies, waits for them, and re-layouts  7.21 us (4%)
    pallas_call x1, Pallas kernels, shards(): pl.pallas_call(step_kernel, out_shape=[shape((ROWS, WIDTH))] * RING, in_s...  32.2 us
    ppermute x3, waiting for transfers between devices, shards(): lax.ppermute(back[s], 'tile', z_pairs(s))  21.8 us
    ppermute x3, waiting for transfers between devices, shards(): lax.ppermute(coeff, 'tile', z_pairs(s))  19.7 us
    ppermute x1, waiting for transfers between devices, shards(): lax.ppermute(c_low, 'tile', row_pairs(-1))  12.8 us
    ppermute x1, waiting for transfers between devices, shards(): lax.ppermute(low, 'tile', row_pairs(-1))  8.8 us
    unnamed x18, local copies, waits for them, and re-layouts  7.21 us
    ppermute x3, starting transfers between devices, shards(): lax.ppermute(coeff, 'tile', z_pairs(s))  6.58 us
    ppermute x3, waiting for transfers between devices, shards(): lax.ppermute(mine[s], 'tile', z_pairs(s))  5.47 us
  transfers between devices with their start and end apart: 18, of which 13 were waited for; matrix products, arithmetic and copies ran while one was open for 0% of the time, Pallas kernels for 6%

profile of v5, /device:TPU:0, one launch (start us, length us, event | category | flops | bytes accessed | tf_op | source)
XLA Modules:
  0.0 163.1 jit_solution(3471650915491522554)
XLA Ops:
  2.3 3.2 %shard_map.64.after = f32[16,64,512]{2,1,0:T(8,128)} custom-call(s32[2]{0:T(128)S(1)} %pad_add_fusion.ids, s32[128]{0:T(128)S(1)} %copy-done.7, f32[1024,512]{1,0:T(8,128)S(1)} %bitcast.4), custom_call_target="tpu_custom_call" | custom-call | tf_op jit(solution)/shard_map/pallas_call | solution.py:370
  5.5 4.7 %all-to-all-start = ((f32[16,64,512]{2,1,0:T(8,128)}), f32[16,64,512]{2,1,0:T(8,128)S(1)}, u32[]{:S(2)}, u32[]{:S(2)}) async-start(f32[16,64,512]{2,1,0:T(8,128)} %shard_map.64.after), calls=%async_computation | async-start | bytes 4194304 | tf_op jit(solution)/shard_map/all_to_all | solution.py:400
  11.1 2.0 %collective-permute-start = (f32[896,128]{1,0:T(8,128)S(1)}, f32[896,128]{1,0:T(8,128)S(1)}, u32[]{:S(2)}, u32[]{:S(2)}) collective-permute-start(f32[896,128]{1,0:T(8,128)S(1)} %shard_map.65.refs_0_), channel_id=1, source_target_pairs={{0,8},{8,16},{16,24},{24,0},{32,40},{40,48},{48,56},{56,32},{64,72... | collective-permute-start | bytes 1376264 | tf_op jit(solution)/shard_map/ppermute | solution.py:390
  13.1 3.6 %collective-permute-start.1 = (f32[896,128]{1,0:T(8,128)S(1)}, f32[896,128]{1,0:T(8,128)S(1)}, u32[]{:S(2)}, u32[]{:S(2)}) collective-permute-start(f32[896,128]{1,0:T(8,128)S(1)} %shard_map.65.refs_0_), channel_id=1, source_target_pairs={{0,16},{8,24},{16,0},{24,8},{32,48},{40,56},{48,32},{56,40},{64,80... | collective-permute-start | bytes 1376264 | tf_op jit(solution)/shard_map/ppermute | solution.py:390
  17.7 8.7 %collective-permute-done.refs_1_ = f32[896,128]{1,0:T(8,128)S(1)} collective-permute-done((f32[896,128]{1,0:T(8,128)S(1)}, f32[896,128]{1,0:T(8,128)S(1)}, u32[]{:S(2)}, u32[]{:S(2)}) %collective-permute-start) | collective-permute-done | bytes 458784 | tf_op jit(solution)/shard_map/ppermute | solution.py:390
  26.4 11.0 %collective-permute-done.1.refs_2_ = f32[896,128]{1,0:T(8,128)S(1)} collective-permute-done((f32[896,128]{1,0:T(8,128)S(1)}, f32[896,128]{1,0:T(8,128)S(1)}, u32[]{:S(2)}, u32[]{:S(2)}) %collective-permute-start.1) | collective-permute-done | bytes 458784 | tf_op jit(solution)/shard_map/ppermute | solution.py:390
  37.4 1.8 %shard_map.66 = (f32[2,896,128]{2,1,0:T(8,128)S(1)}, f32[2,896,128]{2,1,0:T(8,128)}) custom-call(s32[2]{0:T(128)S(1)} %pad_add_fusion.ids, f32[896,128]{1,0:T(8,128)S(1)} %shard_map.65.refs_0_, f32[896,128]{1,0:T(8,128)S(1)} %collective-permute-done.refs_1_, f32[896,128]{1,0:T(8,128)S(1)} %collective-permute-done.1.refs_2_, ...), custom_call_target="tpu_custom_call" | custom-call | tf_op jit(solution)/shard_map/pallas_call | solution.py:391
  39.3 2.8 %collective-permute-start.3 = (f32[2,896,128]{2,1,0:T(8,128)S(1)}, f32[2,896,128]{2,1,0:T(8,128)}, u32[]{:S(2)}, u32[]{:S(2)}) collective-permute-start(f32[2,896,128]{2,1,0:T(8,128)S(1)} %get-tuple-element.39.refs_0_), channel_id=1, source_target_pairs={{0,96},{8,104},{16,112},{24,120},{32,0},{40,8},{48,16},{56,24},{64... | collective-permute-start | bytes 2752520 | tf_op jit(solution)/shard_map/ppermute | solution.py:399
  45.3 1.8 %collective-permute-start.6 = (f32[4,264,128]{2,1,0:T(8,128)S(1)}, f32[4,264,128]{2,1,0:T(8,128)S(1)}, u32[]{:S(2)}, u32[]{:S(2)}) collective-permute-start(f32[4,264,128]{2,1,0:T(8,128)S(1)} %get-tuple-element.31), channel_id=1, source_target_pairs={{0,16},{8,24},{16,0},{24,8},{32,48},{40,56},{48,32},{56,40},{64,80... | collective-permute-start | bytes 1622024 | tf_op jit(solution)/shard_map/ppermute | solution.py:416
  48.8 12.8 %collective-permute-done.3.refs_4_ = f32[2,896,128]{2,1,0:T(8,128)} collective-permute-done((f32[2,896,128]{2,1,0:T(8,128)S(1)}, f32[2,896,128]{2,1,0:T(8,128)}, u32[]{:S(2)}, u32[]{:S(2)}) %collective-permute-start.3) | collective-permute-done | bytes 917536 | tf_op jit(solution)/shard_map/ppermute | solution.py:399
  61.6 3.7 %collective-permute-done.4.refs_6_ = f32[2,896,128]{2,1,0:T(8,128)} collective-permute-done((f32[2,896,128]{2,1,0:T(8,128)}, f32[2,896,128]{2,1,0:T(8,128)}, u32[]{:S(2)}, u32[]{:S(2)}) %collective-permute-start.4) | collective-permute-done | bytes 917536 | tf_op jit(solution)/shard_map/ppermute | solution.py:399
  65.3 5.2 %collective-permute-done.6.refs_2_ = f32[4,264,128]{2,1,0:T(8,128)S(1)} collective-permute-done((f32[4,264,128]{2,1,0:T(8,128)S(1)}, f32[4,264,128]{2,1,0:T(8,128)S(1)}, u32[]{:S(2)}, u32[]{:S(2)}) %collective-permute-start.6) | collective-permute-done | bytes 540704 | tf_op jit(solution)/shard_map/ppermute | solution.py:416
  71.7 3.0 %collective-permute-start.8 = (f32[2,4,264,128]{3,2,1,0:T(8,128)S(1)}, f32[2,4,264,128]{3,2,1,0:T(8,128)S(1)}, u32[]{:S(2)}, u32[]{:S(2)}) collective-permute-start(f32[2,4,264,128]{3,2,1,0:T(8,128)S(1)} %get-tuple-element.37), channel_id=1, source_target_pairs={{0,96},{8,104},{16,112},{24,120},{32,0},{40,8},{48,16},{56,24},{64... | collective-permute-start | bytes 3244040 | tf_op jit(solution)/shard_map/ppermute | solution.py:430
  75.4 1.9 %collective-permute-done.11.refs_3_ = f32[2,896,128]{2,1,0:T(8,128)S(1)} collective-permute-done((f32[2,896,128]{2,1,0:T(8,128)}, f32[2,896,128]{2,1,0:T(8,128)S(1)}, u32[]{:S(2)}, u32[]{:S(2)}) %collective-permute-start.11) | collective-permute-done | bytes 917536 | tf_op jit(solution)/shard_map/ppermute | solution.py:420
  80.0 4.7 %shard_map.69 = (bf16[16,2,512,256]{3,2,1,0:T(8,128)(2,1)S(1)}, f32[16,200,256]{2,1,0:T(8,128)S(1)}) custom-call(s32[2]{0:T(128)S(1)} %pad_add_fusion.ids, f32[2,896,128]{2,1,0:T(8,128)S(1)} %get-tuple-element.39.refs_0_, f32[2,896,128]{2,1,0:T(8,128)S(1)} %collective-permute-done.10.refs_1_, f32[2,896,128]{2,1,0:T(8,128)} %get-tuple-element.40.refs_2_, ...), custom_call_target="tpu_custom_call" | custom-call | tf_op jit(solution)/shard_map/pallas_call | solution.py:432
  84.8 3.3 %copy-done = bf16[16,2,512,256]{3,2,1,0:T(8,128)(2,1)} copy-done((bf16[16,2,512,256]{3,2,1,0:T(8,128)(2,1)}, bf16[16,2,512,256]{3,2,1,0:T(8,128)(2,1)S(1)}, u32[]{:S(2)}) %copy-start) | copy-done | bytes 8388632
  88.0 1.7 %copy-done.1 = f32[16,200,256]{2,1,0:T(8,128)} copy-done((f32[16,200,256]{2,1,0:T(8,128)}, f32[16,200,256]{2,1,0:T(8,128)S(1)}, u32[]{:S(2)}) %copy-start.1) | copy-done | bytes 3276824
  89.7 8.8 %collective-permute-done.8.refs_4_ = f32[2,4,264,128]{3,2,1,0:T(8,128)S(1)} collective-permute-done((f32[2,4,264,128]{3,2,1,0:T(8,128)S(1)}, f32[2,4,264,128]{3,2,1,0:T(8,128)S(1)}, u32[]{:S(2)}, u32[]{:S(2)}) %collective-permute-start.8) | collective-permute-done | bytes 1081376 | tf_op jit(solution)/shard_map/ppermute | solution.py:430
  98.5 3.4 %collective-permute-done.9.refs_5_ = f32[2,4,264,128]{3,2,1,0:T(8,128)S(1)} collective-permute-done((f32[2,4,264,128]{3,2,1,0:T(8,128)S(1)}, f32[2,4,264,128]{3,2,1,0:T(8,128)S(1)}, u32[]{:S(2)}, u32[]{:S(2)}) %collective-permute-start.9) | collective-permute-done | bytes 1081376 | tf_op jit(solution)/shard_map/ppermute | solution.py:430
  101.9 32.2 %shard_map.70 = (f32[256,512]{1,0:T(8,128)S(1)}, f32[256,512]{1,0:T(8,128)S(1)}, f32[256,512]{1,0:T(8,128)S(1)}, f32[256,512]{1,0:T(8,128)S(1)}) custom-call(s32[2]{0:T(128)S(1)} %pad_add_fusion.ids, f32[4,264,128]{2,1,0:T(8,128)S(1)} %get-tuple-element.33.refs_0_, f32[4,264,128]{2,1,0:T(8,128)S(1)} %collective-permute-done.5.refs_1_, ...), custom_call_target="tpu_custom_call" | custom-call | tf_op jit(solution)/shard_map/pallas_call | solution.py:441
  135.6 2.7 %collective-permute-start.15 = (f32[256,512]{1,0:T(8,128)S(1)}, f32[256,512]{1,0:T(8,128)S(1)}, u32[]{:S(2)}, u32[]{:S(2)}) collective-permute-start(f32[256,512]{1,0:T(8,128)S(1)} %get-tuple-element.47), channel_id=1, source_target_pairs={{0,16},{8,24},{16,0},{24,8},{32,48},{40,56},{48,32},{56,40},{64,80... | collective-permute-start | bytes 1572872 | tf_op jit(solution)/shard_map/ppermute | solution.py:457
  138.9 10.5 %collective-permute-done.14.refs_1_ = f32[256,512]{1,0:T(8,128)S(1)} collective-permute-done((f32[256,512]{1,0:T(8,128)S(1)}, f32[256,512]{1,0:T(8,128)S(1)}, u32[]{:S(2)}, u32[]{:S(2)}) %collective-permute-start.14) | collective-permute-done | bytes 524320 | tf_op jit(solution)/shard_map/ppermute | solution.py:457
  149.4 11.3 %collective-permute-done.15.refs_2_ = f32[256,512]{1,0:T(8,128)S(1)} collective-permute-done((f32[256,512]{1,0:T(8,128)S(1)}, f32[256,512]{1,0:T(8,128)S(1)}, u32[]{:S(2)}, u32[]{:S(2)}) %collective-permute-start.15) | collective-permute-done | bytes 524320 | tf_op jit(solution)/shard_map/ppermute | solution.py:457
  160.8 2.2 %shard_map.71 = f32[64,16,512]{2,1,0:T(8,128)} custom-call(s32[2]{0:T(128)S(1)} %pad_add_fusion.ids, f32[256,512]{1,0:T(8,128)S(1)} %get-tuple-element.45.refs_0_, f32[256,512]{1,0:T(8,128)S(1)} %collective-permute-done.14.refs_1_, f32[256,512]{1,0:T(8,128)S(1)} %collective-permute-done.15.refs_2_, f32[256,512]{1,0:T(8,128)S(1)} %collective-permute-done.16.refs_3_), custom_call_target="tpu_custom_call" | custom-call | tf_op jit(solution)/shard_map/pallas_call | solution.py:458
  (39 shorter events, 15.5 us)
Async XLA Ops:
  5.5 4.7 %copy-start.3 = (f32[4,3,128,128]{3,2,1,0:T(8,128)S(1)}, f32[4,3,128,128]{3,2,1,0:T(8,128)}, u32[]{:S(2)}) copy-start(f32[4,3,128,128]{3,2,1,0:T(8,128)} %cond.1) | copy-start | bytes 2359300
  5.5 4.7 %copy-start.4 = (f32[63,512]{1,0:T(8,128)S(1)}, f32[63,512]{1,0:T(8,128)}, u32[]{:S(2)}) copy-start(f32[63,512]{1,0:T(8,128)} %vert.1) | copy-start | bytes 387076
  5.5 4.7 %copy-start.6 = (s32[64,3]{0,1:T(4,128)S(1)}, s32[64,3]{0,1:T(4,128)}, u32[]{:S(2)}) copy-start(s32[64,3]{0,1:T(4,128)} %param.8) | copy-start | bytes 2308
  5.5 36.6 %all-to-all-start = ((f32[16,64,512]{2,1,0:T(8,128)}), f32[16,64,512]{2,1,0:T(8,128)S(1)}, u32[]{:S(2)}, u32[]{:S(2)}) async-start(f32[16,64,512]{2,1,0:T(8,128)} %shard_map.64.after), calls=%async_computation | async-start | bytes 4194304 | tf_op jit(solution)/shard_map/all_to_all | solution.py:400
  10.3 31.8 %copy-start.5 = (f32[16,512]{1,0:T(8,128)S(1)}, f32[16,512]{1,0:T(8,128)}, u32[]{:S(2)}) copy-start(f32[16,512]{1,0:T(8,128)} %rain.1) | copy-start | bytes 98308
  10.3 31.8 %copy-start.8 = (s32[128]{0:T(128)S(1)}, s32[128]{0:T(128)}, u32[]{:S(2)}) copy-start(s32[128]{0:T(128)} %anc.3) | copy-start | bytes 1540
  11.1 15.3 %collective-permute-start = (f32[896,128]{1,0:T(8,128)S(1)}, f32[896,128]{1,0:T(8,128)S(1)}, u32[]{:S(2)}, u32[]{:S(2)}) collective-permute-start(f32[896,128]{1,0:T(8,128)S(1)} %shard_map.65.refs_0_), channel_id=1, source_target_pairs={{0,8},{8,16},{16,24},{24,0},{32,40},{40,48},{48,56},{56,32},{64,72... | collective-permute-start | bytes 1376264 | tf_op jit(solution)/shard_map/ppermute | solution.py:390
  13.1 24.3 %collective-permute-start.1 = (f32[896,128]{1,0:T(8,128)S(1)}, f32[896,128]{1,0:T(8,128)S(1)}, u32[]{:S(2)}, u32[]{:S(2)}) collective-permute-start(f32[896,128]{1,0:T(8,128)S(1)} %shard_map.65.refs_0_), channel_id=1, source_target_pairs={{0,16},{8,24},{16,0},{24,8},{32,48},{40,56},{48,32},{56,40},{64,80... | collective-permute-start | bytes 1376264 | tf_op jit(solution)/shard_map/ppermute | solution.py:390
  16.7 20.7 %collective-permute-start.2 = (f32[896,128]{1,0:T(8,128)S(1)}, f32[896,128]{1,0:T(8,128)S(1)}, u32[]{:S(2)}, u32[]{:S(2)}) collective-permute-start(f32[896,128]{1,0:T(8,128)S(1)} %shard_map.65.refs_0_), channel_id=1, source_target_pairs={{0,24},{8,0},{16,8},{24,16},{32,56},{40,32},{48,40},{56,48},{64,88... | collective-permute-start | bytes 1376264 | tf_op jit(solution)/shard_map/ppermute | solution.py:390
  39.3 22.3 %collective-permute-start.3 = (f32[2,896,128]{2,1,0:T(8,128)S(1)}, f32[2,896,128]{2,1,0:T(8,128)}, u32[]{:S(2)}, u32[]{:S(2)}) collective-permute-start(f32[2,896,128]{2,1,0:T(8,128)S(1)} %get-tuple-element.39.refs_0_), channel_id=1, source_target_pairs={{0,96},{8,104},{16,112},{24,120},{32,0},{40,8},{48,16},{56,24},{64... | collective-permute-start | bytes 2752520 | tf_op jit(solution)/shard_map/ppermute | solution.py:399
  42.1 23.2 %collective-permute-start.4 = (f32[2,896,128]{2,1,0:T(8,128)}, f32[2,896,128]{2,1,0:T(8,128)}, u32[]{:S(2)}, u32[]{:S(2)}) collective-permute-start(f32[2,896,128]{2,1,0:T(8,128)} %get-tuple-element.40.refs_2_), channel_id=1, source_target_pairs={{0,32},{8,40},{16,48},{24,56},{32,64},{40,72},{48,80},{56,88},{64,... | collective-permute-start | bytes 2752520 | tf_op jit(solution)/shard_map/ppermute | solution.py:399
  43.7 21.6 %collective-permute-start.5 = (f32[4,264,128]{2,1,0:T(8,128)S(1)}, f32[4,264,128]{2,1,0:T(8,128)S(1)}, u32[]{:S(2)}, u32[]{:S(2)}) collective-permute-start(f32[4,264,128]{2,1,0:T(8,128)S(1)} %get-tuple-element.30), channel_id=1, source_target_pairs={{0,8},{8,16},{16,24},{24,0},{32,40},{40,48},{48,56},{56,32},{64,72... | collective-permute-start | bytes 1622024 | tf_op jit(solution)/shard_map/ppermute | solution.py:416
  45.3 25.3 %collective-permute-start.6 = (f32[4,264,128]{2,1,0:T(8,128)S(1)}, f32[4,264,128]{2,1,0:T(8,128)S(1)}, u32[]{:S(2)}, u32[]{:S(2)}) collective-permute-start(f32[4,264,128]{2,1,0:T(8,128)S(1)} %get-tuple-element.31), channel_id=1, source_target_pairs={{0,16},{8,24},{16,0},{24,8},{32,48},{40,56},{48,32},{56,40},{64,80... | collective-permute-start | bytes 1622024 | tf_op jit(solution)/shard_map/ppermute | solution.py:416
  47.1 23.7 %collective-permute-start.7 = (f32[4,264,128]{2,1,0:T(8,128)S(1)}, f32[4,264,128]{2,1,0:T(8,128)S(1)}, u32[]{:S(2)}, u32[]{:S(2)}) collective-permute-start(f32[4,264,128]{2,1,0:T(8,128)S(1)} %get-tuple-element.32), channel_id=1, source_target_pairs={{0,24},{8,0},{16,8},{24,16},{32,56},{40,32},{48,40},{56,48},{64,88... | collective-permute-start | bytes 1622024 | tf_op jit(solution)/shard_map/ppermute | solution.py:416
  70.8 4.4 %collective-permute-start.10 = (f32[2,896,128]{2,1,0:T(8,128)S(1)}, f32[2,896,128]{2,1,0:T(8,128)S(1)}, u32[]{:S(2)}, u32[]{:S(2)}) collective-permute-start(f32[2,896,128]{2,1,0:T(8,128)S(1)} %get-tuple-element.39.refs_0_), channel_id=1, source_target_pairs={{0,1},{1,0},{2,3},{3,2},{4,5},{5,4},{6,7},{7,6},{8,9},{9,8},{10,11... | collective-permute-start | bytes 2752520 | tf_op jit(solution)/shard_map/ppermute | solution.py:420
  71.7 26.8 %collective-permute-start.8 = (f32[2,4,264,128]{3,2,1,0:T(8,128)S(1)}, f32[2,4,264,128]{3,2,1,0:T(8,128)S(1)}, u32[]{:S(2)}, u32[]{:S(2)}) collective-permute-start(f32[2,4,264,128]{3,2,1,0:T(8,128)S(1)} %get-tuple-element.37), channel_id=1, source_target_pairs={{0,96},{8,104},{16,112},{24,120},{32,0},{40,8},{48,16},{56,24},{64... | collective-permute-start | bytes 3244040 | tf_op jit(solution)/shard_map/ppermute | solution.py:430
  74.7 27.2 %collective-permute-start.9 = (f32[2,4,264,128]{3,2,1,0:T(8,128)S(1)}, f32[2,4,264,128]{3,2,1,0:T(8,128)S(1)}, u32[]{:S(2)}, u32[]{:S(2)}) collective-permute-start(f32[2,4,264,128]{3,2,1,0:T(8,128)S(1)} %get-tuple-element.38), channel_id=1, source_target_pairs={{0,32},{8,40},{16,48},{24,56},{32,64},{40,72},{48,80},{56,88},{64,... | collective-permute-start | bytes 3244040 | tf_op jit(solution)/shard_map/ppermute | solution.py:430
  74.7 2.7 %collective-permute-start.11 = (f32[2,896,128]{2,1,0:T(8,128)}, f32[2,896,128]{2,1,0:T(8,128)S(1)}, u32[]{:S(2)}, u32[]{:S(2)}) collective-permute-start(f32[2,896,128]{2,1,0:T(8,128)} %get-tuple-element.40.refs_2_), channel_id=1, source_target_pairs={{0,1},{1,0},{2,3},{3,2},{4,5},{5,4},{6,7},{7,6},{8,9},{9,8},{10,11... | collective-permute-start | bytes 2752520 | tf_op jit(solution)/shard_map/ppermute | solution.py:420
  74.9 3.8 %collective-permute-start.12 = (f32[2,896,128]{2,1,0:T(8,128)}, f32[2,896,128]{2,1,0:T(8,128)S(1)}, u32[]{:S(2)}, u32[]{:S(2)}) collective-permute-start(f32[2,896,128]{2,1,0:T(8,128)} %collective-permute-done.3.refs_4_), channel_id=1, source_target_pairs={{0,1},{1,0},{2,3},{3,2},{4,5},{5,4},{6,7},{7,6},{8,9},{9,8},{10,11... | collective-permute-start | bytes 2752520 | tf_op jit(solution)/shard_map/ppermute | solution.py:420
  75.2 4.8 %collective-permute-start.13 = (f32[2,896,128]{2,1,0:T(8,128)}, f32[2,896,128]{2,1,0:T(8,128)S(1)}, u32[]{:S(2)}, u32[]{:S(2)}) collective-permute-start(f32[2,896,128]{2,1,0:T(8,128)} %collective-permute-done.4.refs_6_), channel_id=1, source_target_pairs={{0,1},{1,0},{2,3},{3,2},{4,5},{5,4},{6,7},{7,6},{8,9},{9,8},{10,11... | collective-permute-start | bytes 2752520 | tf_op jit(solution)/shard_map/ppermute | solution.py:420
  84.7 3.3 %copy-start = (bf16[16,2,512,256]{3,2,1,0:T(8,128)(2,1)}, bf16[16,2,512,256]{3,2,1,0:T(8,128)(2,1)S(1)}, u32[]{:S(2)}) copy-start(bf16[16,2,512,256]{3,2,1,0:T(8,128)(2,1)S(1)} %get-tuple-element.43.refs_6_) | copy-start | bytes 25165828
  134.1 15.3 %collective-permute-start.14 = (f32[256,512]{1,0:T(8,128)S(1)}, f32[256,512]{1,0:T(8,128)S(1)}, u32[]{:S(2)}, u32[]{:S(2)}) collective-permute-start(f32[256,512]{1,0:T(8,128)S(1)} %get-tuple-element.46), channel_id=1, source_target_pairs={{0,8},{8,16},{16,24},{24,0},{32,40},{40,48},{48,56},{56,32},{64,72... | collective-permute-start | bytes 1572872 | tf_op jit(solution)/shard_map/ppermute | solution.py:457
  135.6 25.1 %collective-permute-start.15 = (f32[256,512]{1,0:T(8,128)S(1)}, f32[256,512]{1,0:T(8,128)S(1)}, u32[]{:S(2)}, u32[]{:S(2)}) collective-permute-start(f32[256,512]{1,0:T(8,128)S(1)} %get-tuple-element.47), channel_id=1, source_target_pairs={{0,16},{8,24},{16,0},{24,8},{32,48},{40,56},{48,32},{56,40},{64,80... | collective-permute-start | bytes 1572872 | tf_op jit(solution)/shard_map/ppermute | solution.py:457
  138.3 22.4 %collective-permute-start.16 = (f32[256,512]{1,0:T(8,128)S(1)}, f32[256,512]{1,0:T(8,128)S(1)}, u32[]{:S(2)}, u32[]{:S(2)}) collective-permute-start(f32[256,512]{1,0:T(8,128)S(1)} %get-tuple-element.48), channel_id=1, source_target_pairs={{0,24},{8,0},{16,8},{24,16},{32,56},{40,32},{48,40},{56,48},{64,88... | collective-permute-start | bytes 1572872 | tf_op jit(solution)/shard_map/ppermute | solution.py:457
  (3 other events, 3.9 us)
